TPU v7x, 256 devices: a whole 4x4x8 slice. The times are simulated.
256 devices in a mesh: inner: 8 (over z_lo, y), outer: 32 (over z_hi, x, core).
Axes of the slice: x: 4, y: 4, z: 8 (z_hi: 4, z_lo: 2; z = z_hi * 2 + z_lo), core: 2. Of those that a mesh axis runs over, the one named last changes fastest.
Arguments:
- queries: bfloat16 [32768, 2048], P(('outer', 'inner')), may hold values from -5 to 5, as said below
- keys: bfloat16 [32768, 2048], P(('outer', 'inner')), may hold values from -5 to 5, as said below
- values: bfloat16 [32768, 2048], P(('outer', 'inner')), may hold values from -6 to 6
- out_grad: bfloat16 [32768, 2048], P(('outer', 'inner')), may hold values from -6 to 6
- stretch_pos: int32 [512], replicated, may hold values from 0 to 511, as said below
- block_mask: int32 [512, 32], replicated, may hold values from 0 to 1, as said below
Outputs:
- attn_out: bfloat16 [32768, 2048], P(('outer', 'inner'))
- d_query: bfloat16 [32768, 2048], P(('outer', 'inner'))
- d_key: bfloat16 [32768, 2048], P(('outer', 'inner'))
- d_value: bfloat16 [32768, 2048], P(('outer', 'inner'))
Inputs may be any that keep to these rules, and one draw needn't show every extreme that they name: `queries`: a query row's features lie in the printed range. `keys`: a key row's features lie in the printed range. `stretch_pos`: paired order: stored stretches 2 g and 2 g + 1 hold sequence stretches p and 511 - p for some p below 256; every stretch position appears once. `block_mask`: each stretch's entry for itself (window index c mod (16)) is 1.
All inputs are finite; a program needn't handle non-finite values.
Results may differ from a plain program's by a relative error of at most 0.027.
Values may be sent and summed in bfloat16 or wider, within the bound.
No kernel may reach another device: no remote copies, remote signals or barrier semaphores. Data moves between devices by JAX's collectives and lax.ppermute only.
A program may use at most 128 MiB of HBM per device.

v0:
```python
import jax
import jax.numpy as jnp
from jax import lax
from jax.sharding import PartitionSpec as P

H = 16
HEAD = 128
HD = 2048


def shifted(value, axis, steps):
    count = lax.axis_size(axis)
    pairs = [(source, (source + steps) % count) for source in range(count)]
    return lax.ppermute(value, axis, pairs)


def window_mask(query_pos, key_pos, flags):
    seen = flags[:, None, :, None] == 1
    causal = key_pos[None, None, :, :] <= query_pos[:, :, None, None]
    both = jnp.logical_and(seen, causal)
    return both.reshape(
        query_pos.shape[0] * query_pos.shape[1], key_pos.shape[0] * key_pos.shape[1]
    )


def local_attention(query, window_k, window_v, out_grad, allowed):
    rows = query.shape[0]
    width = window_k.shape[0]
    scale = 1.0 / HEAD**0.5
    query3 = query.reshape(rows, H, HEAD)
    key3 = window_k.reshape(width, H, HEAD)
    value3 = window_v.reshape(width, H, HEAD)
    grad3 = out_grad.reshape(rows, H, HEAD)
    scores = jnp.einsum("qhd,khd->hqk", query3, key3, preferred_element_type=jnp.float32) * scale
    masked = jnp.where(allowed[None], scores, -1e30)
    top = jnp.max(masked, axis=-1, keepdims=True)
    expo = jnp.where(allowed[None], jnp.exp(masked - top), 0.0)
    total = jnp.sum(expo, axis=-1, keepdims=True)
    probs = expo / total
    probs_b = probs.astype(jnp.bfloat16)
    output = jnp.einsum("hqk,khd->qhd", probs_b, value3, preferred_element_type=jnp.float32).astype(
        jnp.bfloat16
    )
    delta = jnp.transpose(jnp.sum(grad3.astype(jnp.float32) * output.astype(jnp.float32), axis=-1))
    dprob = jnp.einsum("qhd,khd->hqk", grad3, value3, preferred_element_type=jnp.float32)
    dscore = (probs * (dprob - delta[:, :, None])).astype(jnp.bfloat16)
    dquery = (
        jnp.einsum("hqk,khd->qhd", dscore, key3, preferred_element_type=jnp.float32) * scale
    ).astype(jnp.bfloat16)
    return (
        output.reshape(rows, HD),
        dquery.reshape(rows, HD),
        dscore,
        probs_b,
        top[:, :, 0],
        total[:, :, 0],
        delta,
    )


def rounded_again(term):
    return lax.optimization_barrier(term.astype(jnp.bfloat16)).astype(jnp.float32)


def body(queries, keys, values, out_grad, stretch_pos, block_mask):
    inner_count = lax.axis_size("inner")
    outer_count = lax.axis_size("outer")
    outer_place = lax.axis_index("outer")
    inner_place = lax.axis_index("inner")
    rows = queries.shape[0]
    half_rows = rows // 2
    group_span = 2 * inner_count
    device_place = outer_place * inner_count + inner_place
    offsets = jnp.arange(half_rows, dtype=jnp.int32)
    pos_rows = stretch_pos[:, None] * half_rows + offsets[None, :]
    own_pos = lax.dynamic_slice_in_dim(pos_rows, outer_place * group_span, group_span, 0)
    prev_group = (outer_place + outer_count - 1) % outer_count
    prev_pos = lax.dynamic_slice_in_dim(pos_rows, prev_group * group_span, group_span, 0)
    key_pos = jnp.concatenate([own_pos, prev_pos], axis=0)
    query_pos = lax.dynamic_slice_in_dim(pos_rows, device_place * 2, 2, 0)
    own_flags = lax.dynamic_slice_in_dim(block_mask, device_place * 2, 2, 0)
    allowed = window_mask(query_pos, key_pos, own_flags)
    own_k, own_v = (
        lax.all_gather(keys, "inner", axis=0, tiled=True),
        lax.all_gather(values, "inner", axis=0, tiled=True),
    )
    prev_k, prev_v = shifted((own_k, own_v), "outer", 1)
    window_k = jnp.concatenate([own_k, prev_k], axis=0)
    window_v = jnp.concatenate([own_v, prev_v], axis=0)
    output, dquery, dscore, probs_b, top, total, delta = local_attention(
        queries, window_k, window_v, out_grad, allowed
    )
    scale = 1.0 / HEAD**0.5
    query3 = queries.reshape(rows, H, HEAD)
    grad3 = out_grad.reshape(rows, H, HEAD)
    width = window_k.shape[0]
    dkey_terms = (
        jnp.einsum("hqk,qhd->khd", dscore, query3, preferred_element_type=jnp.float32) * scale
    ).reshape(width, HD)
    dvalue_terms = jnp.einsum(
        "hqk,qhd->khd", probs_b, grad3, preferred_element_type=jnp.float32
    ).reshape(width, HD)
    span = own_k.shape[0]
    own_dk, own_dv, prev_dk, prev_dv = (
        lax.psum_scatter(
            dkey_terms[:span].astype(jnp.bfloat16), "inner", scatter_dimension=0, tiled=True
        ).astype(jnp.float32),
        lax.psum_scatter(
            dvalue_terms[:span].astype(jnp.bfloat16), "inner", scatter_dimension=0, tiled=True
        ).astype(jnp.float32),
        lax.psum_scatter(
            dkey_terms[span:].astype(jnp.bfloat16), "inner", scatter_dimension=0, tiled=True
        ).astype(jnp.float32),
        lax.psum_scatter(
            dvalue_terms[span:].astype(jnp.bfloat16), "inner", scatter_dimension=0, tiled=True
        ).astype(jnp.float32),
    )
    back_dk, back_dv = shifted(
        (prev_dk.astype(jnp.bfloat16), prev_dv.astype(jnp.bfloat16)), "outer", -1
    )
    d_key = (rounded_again(own_dk) + back_dk.astype(jnp.float32)).astype(jnp.bfloat16)
    d_value = (rounded_again(own_dv) + back_dv.astype(jnp.float32)).astype(jnp.bfloat16)
    return (output, dquery, d_key, d_value)


def solution(mesh):
    in_specs = (
        P(("outer", "inner"), None),
        P(("outer", "inner"), None),
        P(("outer", "inner"), None),
        P(("outer", "inner"), None),
        P(),
        P(),
    )
    out_specs = (
        P(("outer", "inner"), None),
        P(("outer", "inner"), None),
        P(("outer", "inner"), None),
        P(("outer", "inner"), None),
    )
    return jax.shard_map(body, mesh=mesh, in_specs=in_specs, out_specs=out_specs, check_vma=False)
```

profile of v0, /device:TPU:7, one launch (start us, length us, event | category | flops | bytes accessed | tf_op | source)
XLA Modules:
  0.0 596.3 jit_solution(17823765019160828648)
XLA Ops:
  8.0 2.0 copy.73
  10.1 57.9 %all-gather.3.cloned.1.call-done = bf16[1024,2048]{1,0:T(8,128)(2,1)} async-done(((bf16[128,2048]{1,0:T(8,128)(2,1)}), bf16[1024,2048]{1,0:T(8,128)(2,1)}) %all-gather.3.cloned.1.call-update) | async-done | bytes 4194320 | tf_op jit(solution)/shard_map/all_gather | solution.py:85
  68.0 2.8 collective-permute-start
  70.8 111.0 %all-gather.5.cloned.1.call-done = bf16[1024,2048]{0,1:T(8,128)(2,1)} async-done(((bf16[128,2048]{0,1:T(8,128)(2,1)}), bf16[1024,2048]{0,1:T(8,128)(2,1)}) %all-gather.5.cloned.1.call-update) | async-done | bytes 4194320 | tf_op jit(solution)/shard_map/all_gather | solution.py:84
  184.8 1.3 copy.105
  186.1 1.3 copy.77
  187.4 13.8 %collective-permute-done = bf16[1024,2048]{1,0:T(8,128)(2,1)} collective-permute-done((bf16[1024,2048]{1,0:T(8,128)(2,1)}, bf16[1024,2048]{1,0:T(8,128)(2,1)}, u32[]{:S(2)}, u32[]{:S(2)}) %collective-permute-start) | collective-permute-done | bytes 4194336 | tf_op jit(solution)/shard_map/ppermute | solution.py:14
  201.2 8.4 %pad_maximum_fusion = bf16[2048,2048]{1,0:T(8,128)(2,1)} fusion(bf16[1024,2048]{1,0:T(8,128)(2,1)} %collective-permute-done, bf16[1024,2048]{1,0:T(8,128)(2,1)} %all-gather.3.cloned.1.call-done), kind=kLoop, calls=%fused_computation.8 | loop fusion | flops 16777216 | bytes 16777216 | tf_op jit(solution)/shard_map/concatenate | solution.py:89
  209.6 12.3 %copy.70 = bf16[2048,2048]{0,1:T(8,128)(2,1)} copy(bf16[2048,2048]{1,0:T(8,128)(2,1)} %pad_maximum_fusion) | data formatting | bytes 16777216 | tf_op jit(solution)/shard_map/concatenate | solution.py:89
  221.9 25.1 %collective-permute-done.1 = bf16[1024,2048]{0,1:T(8,128)(2,1)} collective-permute-done((bf16[1024,2048]{0,1:T(8,128)(2,1)}, bf16[1024,2048]{0,1:T(8,128)(2,1)}, u32[]{:S(2)}, u32[]{:S(2)}) %collective-permute-start.1) | collective-permute-done | bytes 4194336 | tf_op jit(solution)/shard_map/ppermute | solution.py:14
  247.0 8.1 %pad_maximum_fusion.1 = bf16[2048,2048]{0,1:T(8,128)(2,1)} fusion(bf16[1024,2048]{0,1:T(8,128)(2,1)} %collective-permute-done.1, bf16[1024,2048]{0,1:T(8,128)(2,1)} %all-gather.5.cloned.1.call-done), kind=kLoop, calls=%fused_computation.9 | loop fusion | flops 16777216 | bytes 16777216 | tf_op jit(solution)/shard_map/concatenate | solution.py:88
  255.2 13.3 %fusion.15 = (f32[16,128]{1,0:T(8,128)S(1)}, f32[16,128,2048]{1,2,0:T(8,128)}) fusion(pred[128,2048]{0,1:T(8,128)(4,1)S(1)} %copy.72, bf16[2048,16,128]{0,2,1:T(8,128)(2,1)} %bitcast.58, bf16[128,16,128]{0,2,1:T(8,128)(2,1)S(1)} %bitcast.64), kind=kOutput, calls=%fused_computation.36 | convolution fusion | flops 1094715392 | bytes 25960448 | tf_op jit(solution)/shard_map/sub | solution.py:37
  268.4 6.7 %fusion.7 = bf16[16,128,2048]{1,2,0:T(8,128)(2,1)S(1)} fusion(f32[16,128,2048]{1,2,0:T(8,128)} %get-tuple-element.27, f32[16,128]{1,0:T(8,128)S(1)} %get-tuple-element.26), kind=kLoop, calls=%fused_computation.15 | loop fusion | flops 8388608 | bytes 25174016 | tf_op jit(solution)/shard_map/convert_element_type | solution.py:40
  275.2 2.7 copy-done.3
  277.8 2.4 multiply_reduce_fusion
  280.2 13.5 %fusion.1 = bf16[16,128,2048]{1,2,0:T(8,128)(2,1)} fusion(f32[16,128]{1,0:T(8,128)S(1)} %bitcast.68, f32[16,128,2048]{1,2,0:T(8,128)} %get-tuple-element.27, f32[16,128]{1,0:T(8,128)S(1)} %get-tuple-element.26, bf16[2048,16,128]{0,2,1:T(8,128)(2,1)} %bitcast.60, bf16[128,16,128]{0,2,1:T(8,128)(2,1)S(1)} %bitcast.62), kind=kOutput, calls=%fused_computation.2 | convolution fusion | flops 1090519040 | bytes 34095104 | tf_op jit(solution)/shard_map/qhd,khd->hqk/dot_general | solution.py:45
  293.7 5.7 fusion.3
  299.4 3.6 fusion.14
  303.0 6.4 %copy.85 = bf16[1024,16,128]{0,2,1:T(8,128)(2,1)} copy(bf16[1024,16,128]{2,0,1:T(8,128)(2,1)} %get-tuple-element.23) | data formatting | bytes 8388608 | tf_op jit(solution)/shard_map/slice | solution.py:112
  309.4 6.5 %copy.102 = bf16[1024,2048]{1,0:T(8,128)(2,1)} copy(bf16[1024,2048]{0,1:T(8,128)(2,1)} %bitcast.54) | data formatting | bytes 8388608
  316.0 9.0 %convert_bitcast_fusion = bf16[2048,16,128]{0,2,1:T(8,128)(2,1)} fusion(bf16[16,128,2048]{1,2,0:T(8,128)(2,1)} %copy-done.2, bf16[128,16,128]{0,2,1:T(8,128)(2,1)S(1)} %bitcast.63), kind=kOutput, calls=%fused_computation.10 | convolution fusion | flops 1077936128 | bytes 17301504 | tf_op jit(solution)/shard_map/hqk,qhd->khd/dot_general | solution.py:100
  324.9 6.0 %fusion.13 = (bf16[1024,16,128]{0,2,1:T(8,128)(2,1)}, bf16[1024,16,128]{0,2,1:T(8,128)(2,1)}) fusion(bf16[2048,16,128]{0,2,1:T(8,128)(2,1)} %convert_bitcast_fusion), kind=kLoop, calls=%fused_computation.34 | loop fusion | bytes 16777216 | tf_op jit(solution)/shard_map/slice | solution.py:109
  331.0 6.5 %copy.88 = bf16[1024,2048]{1,0:T(8,128)(2,1)} copy(bf16[1024,2048]{0,1:T(8,128)(2,1)} %bitcast.57) | data formatting | bytes 8388608 | tf_op jit(solution)/shard_map/convert_element_type | solution.py:115
  337.6 6.4 %copy.84 = bf16[1024,16,128]{0,2,1:T(8,128)(2,1)} copy(bf16[1024,16,128]{2,0,1:T(8,128)(2,1)} %get-tuple-element.22) | data formatting | bytes 8388608 | tf_op jit(solution)/shard_map/slice | solution.py:106
  344.0 6.5 %copy.100 = bf16[1024,2048]{1,0:T(8,128)(2,1)} copy(bf16[1024,2048]{0,1:T(8,128)(2,1)} %bitcast.55) | data formatting | bytes 8388608
  350.6 6.5 %copy.87 = bf16[1024,2048]{1,0:T(8,128)(2,1)} copy(bf16[1024,2048]{0,1:T(8,128)(2,1)} %bitcast.56) | data formatting | bytes 8388608 | tf_op jit(solution)/shard_map/convert_element_type | solution.py:109
  357.1 58.4 %reduce-scatter.15.cloned.1.call-done = bf16[128,2048]{1,0:T(8,128)(2,1)} async-done(((bf16[1024,2048]{1,0:T(8,128)(2,1)}), bf16[128,2048]{1,0:T(8,128)(2,1)}) %reduce-scatter.15.cloned.1.call-update) | async-done | bytes 524304
  417.5 54.9 %reduce-scatter.11.cloned.1.call-done = bf16[128,2048]{1,0:T(8,128)(2,1)} async-done(((bf16[1024,2048]{1,0:T(8,128)(2,1)}), bf16[128,2048]{1,0:T(8,128)(2,1)}) %reduce-scatter.11.cloned.1.call-update) | async-done | bytes 524304 | tf_op jit(solution)/shard_map/reduce_scatter | solution.py:114
  473.0 8.1 %fusion.10 = bf16[16,128,128]{2,1,0:T(8,128)(2,1)S(1)} fusion(bf16[2048,16,128]{0,2,1:T(8,128)(2,1)} %bitcast.59, bf16[16,128,2048]{1,2,0:T(8,128)(2,1)} %fusion.1), kind=kOutput, calls=%fused_computation.18 | convolution fusion | flops 1074266112 | bytes 17301504 | tf_op jit(solution)/shard_map/hqk,khd->qhd/dot_general | solution.py:48
  483.2 46.3 %reduce-scatter.13.cloned.1.call-done = bf16[128,2048]{1,0:T(8,128)(2,1)} async-done(((bf16[1024,2048]{1,0:T(8,128)(2,1)}), bf16[128,2048]{1,0:T(8,128)(2,1)}) %reduce-scatter.13.cloned.1.call-update) | async-done | bytes 524304
  530.8 55.6 %reduce-scatter.9.cloned.1.call-done = bf16[128,2048]{1,0:T(8,128)(2,1)} async-done(((bf16[1024,2048]{1,0:T(8,128)(2,1)}), bf16[128,2048]{1,0:T(8,128)(2,1)}) %reduce-scatter.9.cloned.1.call-update) | async-done | bytes 524304 | tf_op jit(solution)/shard_map/reduce_scatter | solution.py:108
  587.5 2.0 add_convert_fusion
  (44 shorter events, 11.1 us)
Async XLA Ops:
  7.2 175.6 %copy-start = (s32[512,32]{0,1:T(8,128)S(1)}, s32[512,32]{0,1:T(8,128)}, u32[]{:S(2)}) copy-start(s32[512,32]{0,1:T(8,128)} %param.11) | copy-start | bytes 196612
  7.2 60.8 %all-gather.3.cloned.1.call-start = ((), (), s32[]{:S(2)}) async-start(), calls=%async_computation.4 | async-start | bytes 4718592 | tf_op jit(solution)/shard_map/all_gather | solution.py:85
  7.9 173.8 %all-gather.5.cloned.1.call-start = ((), (), s32[]{:S(2)}) async-start(), calls=%async_computation.5 | async-start | bytes 4718592 | tf_op jit(solution)/shard_map/all_gather | solution.py:84
  10.0 405.5 %reduce-scatter.15.cloned.1.call-start = ((), (), s32[]{:S(2)}) async-start(), calls=%async_computation.9 | async-start | bytes 4718592
  68.0 133.2 %collective-permute-start = (bf16[1024,2048]{1,0:T(8,128)(2,1)}, bf16[1024,2048]{1,0:T(8,128)(2,1)}, u32[]{:S(2)}, u32[]{:S(2)}) collective-permute-start(bf16[1024,2048]{1,0:T(8,128)(2,1)} %all-gather.3.cloned.1.call-done), channel_id=1, source_target_pairs={{0,1},{1,2},{2,3},{3,4},{4,5},{5,6},{6,7},{7,8},{8,9},{9,10},{10,1... | collective-permute-start | bytes 12582920 | tf_op jit(solution)/shard_map/ppermute | solution.py:14
  181.8 65.2 %collective-permute-start.1 = (bf16[1024,2048]{0,1:T(8,128)(2,1)}, bf16[1024,2048]{0,1:T(8,128)(2,1)}, u32[]{:S(2)}, u32[]{:S(2)}) collective-permute-start(bf16[1024,2048]{0,1:T(8,128)(2,1)} %all-gather.5.cloned.1.call-done), channel_id=1, source_target_pairs={{0,1},{1,2},{2,3},{3,4},{4,5},{5,6},{6,7},{7,8},{8,9},{9,10},{10,1... | collective-permute-start | bytes 12582920 | tf_op jit(solution)/shard_map/ppermute | solution.py:14
  268.4 9.4 %copy-start.3 = (bf16[2048,2048]{0,1:T(8,128)(2,1)S(1)}, bf16[2048,2048]{0,1:T(8,128)(2,1)}, u32[]{:S(2)}) copy-start(bf16[2048,2048]{0,1:T(8,128)(2,1)} %copy.70) | copy-start | bytes 25165828
  275.2 5.0 copy-start.2
  315.9 156.5 %reduce-scatter.11.cloned.1.call-start = ((), (), s32[]{:S(2)}) async-start(), calls=%async_computation.7 | async-start | bytes 4718592 | tf_op jit(solution)/shard_map/reduce_scatter | solution.py:114
  337.6 191.9 %reduce-scatter.13.cloned.1.call-start = ((), (), s32[]{:S(2)}) async-start(), calls=%async_computation.8 | async-start | bytes 4718592
  350.5 235.8 %reduce-scatter.9.cloned.1.call-start = ((), (), s32[]{:S(2)}) async-start(), calls=%async_computation.6 | async-start | bytes 4718592 | tf_op jit(solution)/shard_map/reduce_scatter | solution.py:108
  416.8 169.6 %collective-permute-start.2 = (bf16[128,2048]{0,1:T(8,128)(2,1)S(1)}, bf16[128,2048]{0,1:T(8,128)(2,1)S(1)}, u32[]{:S(2)}, u32[]{:S(2)}) collective-permute-start(bf16[128,2048]{0,1:T(8,128)(2,1)S(1)} %copy.103), channel_id=1, source_target_pairs={{0,31},{1,0},{2,1},{3,2},{4,3},{5,4},{6,5},{7,6},{8,7},{9,8},{10,9... | collective-permute-start | bytes 1572872 | tf_op jit(solution)/shard_map/ppermute | solution.py:14
  472.4 115.1 %collective-permute-start.3 = (bf16[128,2048]{1,0:T(8,128)(2,1)}, bf16[128,2048]{1,0:T(8,128)(2,1)S(1)}, u32[]{:S(2)}, u32[]{:S(2)}) collective-permute-start(bf16[128,2048]{1,0:T(8,128)(2,1)} %reduce-scatter.11.cloned.1.call-done), channel_id=1, source_target_pairs={{0,31},{1,0},{2,1},{3,2},{4,3},{5,4},{6,5},{7,6},{8,7},{9,8},{10,9... | collective-permute-start | bytes 1572872 | tf_op jit(solution)/shard_map/ppermute | solution.py:14
  473.0 116.5 %copy-start.1 = (s32[512,32]{0,1:T(8,128)S(1)}, s32[512,32]{0,1:T(8,128)}, u32[]{:S(2)}) copy-start(s32[512,32]{0,1:T(8,128)} %param.11) | copy-start | bytes 196612
Sparse Core Ops, SparseCore 0:
  9.8 58.1 all-gather.2
  70.3 111.4 all-gather.4
  316.1 99.3 reduce-scatter.14
  417.9 54.4 reduce-scatter.10
  474.8 54.6 reduce-scatter.12
  531.9 54.4 reduce-scatter.8
where the time goes:
time: 599 us; the launch traced here: 596 us
  waiting for transfers between devices  424 us (71%)
  local copies, waits for them, and re-layouts  75.7 us (13%)
  matrix products  51.9 us (9%)
  other arithmetic  26.4 us (4%)
  between operations  14.3 us (2%)
    all_gather x1, waiting for transfers between devices, body(): lax.all_gather(keys, 'inner', axis=0, tiled=True)  111 us
    unnamed x8, waiting for transfers between devices  105 us
    all_gather x1, waiting for transfers between devices, body(): lax.all_gather(values, 'inner', axis=0, tiled=True)  57.9 us
    reduce_scatter x1, waiting for transfers between devices, body(): lax.psum_scatter(dvalue_terms[:span].astype(jnp.bfloat16), 'inner', scatt...  55.6 us
    reduce_scatter x1, waiting for transfers between devices, body(): lax.psum_scatter(dvalue_terms[span:].astype(jnp.bfloat16), 'inner', scatt...  54.9 us
    ppermute x4, waiting for transfers between devices, shifted(): return lax.ppermute(value, axis, pairs)  38.9 us
    unnamed x18, local copies, waits for them, and re-layouts  24.8 us
    dot_general x1, matrix products, local_attention(): jnp.einsum('qhd,khd->hqk', grad3, value3, preferred_element_type=jnp.floa...  13.5 us
  transfers between devices with their start and end apart: 10, of which 8 were waited for; matrix products, arithmetic and copies ran while one was open for 14% of the time, Pallas kernels for 0%

commit v1 on v0

v1 whole, which is shorter than its diff:
```python
import functools

import jax
import jax.numpy as jnp
from jax import lax
from jax.experimental import pallas as pl
from jax.experimental.pallas import tpu as pltpu
from jax.sharding import PartitionSpec as P

H = 16
HEAD = 128
CH = 64
NEG = -1e30
TILE = 256
SCALE = 1.0 / HEAD**0.5
LOG2E = 1.4426950408889634


def shifted(value, axis, steps):
    count = lax.axis_size(axis)
    pairs = [(source, (source + steps) % count) for source in range(count)]
    return lax.ppermute(value, axis, pairs)


def exchanged(value):
    return lax.all_to_all(value, "inner", split_axis=0, concat_axis=0, tiled=True)


def dot(a, b):
    return lax.dot_general(a, b, (((1,), (0,)), ((), ())), preferred_element_type=jnp.float32)


def dot_t(a, b):
    return lax.dot_general(a, b, (((1,), (1,)), ((), ())), preferred_element_type=jnp.float32)


def pack_kernel(a_ref, b_ref, o_ref):
    peers, heads = o_ref.shape[0], o_ref.shape[1]
    for peer in range(peers):
        for head in range(heads):
            at = (peer * heads + head) * HEAD
            o_ref[peer, head, 0] = a_ref[:, at : at + HEAD]
            o_ref[peer, head, 1] = b_ref[:, at : at + HEAD]


def pack(a, b, peers):
    rows, width = a.shape
    heads = width // HEAD // peers
    return pl.pallas_call(
        pack_kernel,
        out_shape=jax.ShapeDtypeStruct((peers, heads, 2, rows, HEAD), a.dtype),
    )(a, b)


def unpack_kernel(i_ref, a_ref, b_ref):
    peers, heads = i_ref.shape[0], i_ref.shape[1]
    for peer in range(peers):
        for head in range(heads):
            at = (peer * heads + head) * HEAD
            a_ref[:, at : at + HEAD] = i_ref[peer, head, 0]
            b_ref[:, at : at + HEAD] = i_ref[peer, head, 1]


def unpack(packed):
    peers, heads, _, rows, _ = packed.shape
    shape = jax.ShapeDtypeStruct((rows, peers * heads * HEAD), packed.dtype)
    return pl.pallas_call(unpack_kernel, out_shape=(shape, shape))(packed)


def attention_kernel(bias_ref, qg_ref, kv0_ref, kv1_ref, oq_ref, own_ref, prev_ref, acc_k, acc_v, s_ref):
    step = pl.program_id(1)
    span = kv0_ref.shape[0] * kv0_ref.shape[3]
    keys = (kv0_ref[:, 0, 0].reshape(span, HEAD), kv1_ref[:, 0, 0].reshape(span, HEAD))
    vals = (kv0_ref[:, 0, 1].reshape(span, HEAD), kv1_ref[:, 0, 1].reshape(span, HEAD))
    q = qg_ref[:, 0, 0].reshape(TILE, HEAD)
    g = qg_ref[:, 0, 1].reshape(TILE, HEAD)

    @pl.when(step == 0)
    def _():
        acc_k[...] = jnp.zeros_like(acc_k)
        acc_v[...] = jnp.zeros_like(acc_v)

    for half in range(2):
        s = dot_t(q, keys[half]) * (SCALE * LOG2E)
        for j in range(TILE // CH):
            rows = slice(j * CH, (j + 1) * CH)
            cols = slice(half * span, (half + 1) * span)
            s_ref[rows, cols] = s[rows] + bias_ref[0, j : j + 1, cols]
    row = lax.broadcasted_iota(jnp.int32, (TILE, TILE), 0)
    col = lax.broadcasted_iota(jnp.int32, (TILE, TILE), 1)
    later = jnp.logical_and(row // CH == col // CH, col > row)
    own = pl.ds(pl.multiple_of(step * TILE, TILE), TILE)
    s_ref[:, own] = s_ref[:, own] + jnp.where(later, NEG, 0.0)

    s = s_ref[...]
    top = jnp.max(s, axis=1, keepdims=True)
    e = jnp.exp2(s - top)
    total = jnp.sum(e, axis=1, keepdims=True)
    p = e * (1.0 / total)
    pb = p.astype(jnp.bfloat16)
    out = (dot(pb[:, :span], vals[0]) + dot(pb[:, span:], vals[1])).astype(jnp.bfloat16)
    delta = jnp.sum(g.astype(jnp.float32) * out.astype(jnp.float32), axis=1, keepdims=True)
    dq = jnp.zeros((TILE, HEAD), jnp.float32)
    qt = q.T
    gt = g.T
    for half in range(2):
        cols = slice(half * span, (half + 1) * span)
        dp = dot_t(g, vals[half])
        ds = (p[:, cols] * (dp - delta)).astype(jnp.bfloat16)
        dq = dq + dot(ds, keys[half])
        acc_k[:, cols] += dot(qt, ds)
        acc_v[:, cols] += dot(gt, pb[:, cols])
    oq_ref[:, 0, 0] = out.reshape(oq_ref.shape[0], -1, HEAD)
    oq_ref[:, 0, 1] = (dq * SCALE).astype(jnp.bfloat16).reshape(oq_ref.shape[0], -1, HEAD)

    @pl.when(step == pl.num_programs(1) - 1)
    def _():
        blocks = own_ref.shape[0]
        rows = own_ref.shape[3]
        for which, acc, factor in ((0, acc_k, SCALE), (1, acc_v, 1.0)):
            for block in range(blocks):
                at = block * rows
                own_ref[block, 0, which] = (acc[:, at : at + rows].T * factor).astype(own_ref.dtype)
                at += span
                prev_ref[block, 0, which] = (acc[:, at : at + rows].T * factor).astype(prev_ref.dtype)


def attention(bias, qg, kv0, kv1):
    peers, heads, _, rows, _ = qg.shape
    tiles = peers * rows // TILE
    per = TILE // rows
    whole = pl.BlockSpec((peers, 1, 2, rows, HEAD), lambda h, i: (0, h, 0, 0, 0))
    tile = pl.BlockSpec((per, 1, 2, rows, HEAD), lambda h, i: (i, h, 0, 0, 0))
    shape = jax.ShapeDtypeStruct(qg.shape, jnp.bfloat16)
    width = 2 * peers * rows
    return pl.pallas_call(
        attention_kernel,
        grid=(heads, tiles),
        in_specs=[
            pl.BlockSpec((1, TILE // CH, width), lambda h, i: (i, 0, 0)),
            tile,
            whole,
            whole,
        ],
        out_specs=(tile, whole, whole),
        out_shape=(shape, jax.ShapeDtypeStruct(qg.shape, jnp.float32), shape),
        scratch_shapes=[
            pltpu.VMEM((HEAD, width), jnp.float32),
            pltpu.VMEM((HEAD, width), jnp.float32),
            pltpu.VMEM((TILE, width), jnp.float32),
        ],
        compiler_params=pltpu.CompilerParams(vmem_limit_bytes=48 * 2**20),
    )(bias, qg, kv0, kv1)


def window_bias(stretch_pos, block_mask, group, groups, span):
    prev = (group + groups - 1) % groups
    own_pos = lax.dynamic_slice_in_dim(stretch_pos, group * span, span, 0)
    prev_pos = lax.dynamic_slice_in_dim(stretch_pos, prev * span, span, 0)
    key_pos = jnp.concatenate([own_pos, prev_pos], axis=0)
    flags = lax.dynamic_slice_in_dim(block_mask, group * span, span, 0)
    seen = jnp.logical_and(flags == 1, key_pos[None, :] <= own_pos[:, None])
    bias = jnp.where(seen, 0.0, NEG).astype(jnp.float32)
    wide = jnp.broadcast_to(bias[:, :, None], bias.shape + (CH,))
    return wide.reshape(span * CH // TILE, TILE // CH, -1)


def body(queries, keys, values, out_grad, stretch_pos, block_mask):
    peers = lax.axis_size("inner")
    groups = lax.axis_size("outer")
    group = lax.axis_index("outer")
    bias = window_bias(stretch_pos, block_mask, group, groups, 2 * peers)
    kv = exchanged(pack(keys, values, peers))
    prev_kv = shifted(kv, "outer", 1)
    qg = exchanged(pack(queries, out_grad, peers))
    oq, own, prev = attention(bias, qg, kv, prev_kv)
    back = shifted(prev, "outer", -1)
    output, dquery = unpack(exchanged(oq))
    dkv = (own + back.astype(jnp.float32)).astype(jnp.bfloat16)
    d_key, d_value = unpack(exchanged(dkv))
    return (output, dquery, d_key, d_value)


def solution(mesh):
    rows = P(("outer", "inner"), None)
    return jax.shard_map(
        body,
        mesh=mesh,
        in_specs=(rows, rows, rows, rows, P(), P()),
        out_specs=(rows, rows, rows, rows),
        check_vma=False,
    )
```

time: 599 us -> 154 us (0.26)
  waiting for transfers between devices: 424 us -> 67.4 us
  local copies, waits for them, and re-layouts: 75.7 us -> 3.36 us
  matrix products: 51.9 us -> 0 us
  starting transfers between devices: 4.38 us -> 45.3 us
  Pallas kernels: 0 us -> 32.1 us
  other arithmetic: 26.4 us -> 3.79 us
  between operations: 14.3 us -> 0.68 us
    all_gather x2 -> x0, waiting for transfers between devices: 169 us -> none  [the longest x1 111 us: body(): lax.all_gather(keys, 'inner', axis=0, tiled=True)]
    reduce_scatter x2 -> x0, waiting for transfers between devices: 110 us -> none  [the longest x1 55.6 us: body(): lax.psum_scatter(dvalue_terms[:span].astype(jnp.bfloat16), 'inner', scatt...]
    unnamed x8 -> x0, waiting for transfers between devices: 105 us -> none
    all_to_all x0 -> x4, starting transfers between devices: none -> 41.6 us  [exchanged(): lax.all_to_all(value, 'inner', split_axis=0, concat_axis=0, tiled=True)]
    dot_general x5 -> x0, matrix products: 38.7 us -> none  [the longest x1 13.5 us: local_attention(): jnp.einsum('qhd,khd->hqk', grad3, value3, preferred_element_type=jnp.floa...]
    all_to_all x0 -> x4, waiting for transfers between devices: none -> 37 us  [exchanged(): lax.all_to_all(value, 'inner', split_axis=0, concat_axis=0, tiled=True)]
    pallas_call x0 -> x5, Pallas kernels: none -> 32.1 us  [the longest x1 22.4 us: attention(): pl.pallas_call(attention_kernel, grid=(heads, tiles), in_specs=[pl.BlockS...]
    slice x4 -> x0, local copies, waits for them, and re-layouts: 22.4 us -> none  [the longest x2 9.98 us: body(): dkey_terms[:span].astype(jnp.bfloat16)]
  transfers between devices with their start and end apart: 10 -> 6, of which waited for: 8 -> 5; matrix products, arithmetic and copies ran while one was open for 14% -> 3% of each run, Pallas kernels for 0% -> 3%
where the time goes in v1:
time: 154 us; the launch traced here: 153 us
  waiting for transfers between devices  67.4 us (44%)
  starting transfers between devices  45.3 us (29%)
  Pallas kernels  32.1 us (21%)
  other arithmetic  3.79 us (2%)
  local copies, waits for them, and re-layouts  3.36 us (2%)
    all_to_all x4, starting transfers between devices, exchanged(): lax.all_to_all(value, 'inner', split_axis=0, concat_axis=0, tiled=True)  41.6 us
    all_to_all x4, waiting for transfers between devices, exchanged(): lax.all_to_all(value, 'inner', split_axis=0, concat_axis=0, tiled=True)  37 us
    ppermute x2, waiting for transfers between devices, shifted(): return lax.ppermute(value, axis, pairs)  30.4 us
    pallas_call x1, Pallas kernels, attention(): pl.pallas_call(attention_kernel, grid=(heads, tiles), in_specs=[pl.BlockS...  22.4 us
    pallas_call x2, Pallas kernels, unpack(): return pl.pallas_call(unpack_kernel, out_shape=(shape, shape))(packed)  4.97 us
    pallas_call x2, Pallas kernels, pack(): pl.pallas_call(pack_kernel, out_shape=jax.ShapeDtypeStruct((peers, heads,...  4.74 us
    ppermute x2, starting transfers between devices, shifted(): return lax.ppermute(value, axis, pairs)  3.69 us
  transfers between devices with their start and end apart: 6, of which 5 were waited for; matrix products, arithmetic and copies ran while one was open for 3% of the time, Pallas kernels for 3%

profile of v1, /device:TPU:7, one launch (start us, length us, event | category | flops | bytes accessed | tf_op | source)
XLA Modules:
  0.0 152.6 jit_solution(4825264407610056531)
XLA Ops:
  0.6 2.4 %shard_map.94 = bf16[8,2,2,128,128]{4,3,2,1,0:T(8,128)(2,1)} custom-call(bf16[128,2048]{1,0:T(8,128)(2,1)} %a_ref.3, bf16[128,2048]{1,0:T(8,128)(2,1)} %b_ref.3), custom_call_target="tpu_custom_call" | custom-call | tf_op jit(solution)/shard_map/pallas_call | solution.py:49
  3.0 5.5 %all-to-all-start.1 = ((bf16[8,2,2,128,128]{4,3,2,1,0:T(8,128)(2,1)}), bf16[8,2,2,128,128]{4,3,2,1,0:T(8,128)(2,1)S(1)}, u32[]{:S(2)}, u32[]{:S(2)}) async-start(bf16[8,2,2,128,128]{4,3,2,1,0:T(8,128)(2,1)} %shard_map.94), calls=%async_computation.1 | async-start | bytes 2097152 | tf_op jit(solution)/shard_map/all_to_all | solution.py:26
  8.5 0.0 copy-start.5
  8.5 2.4 %shard_map.93 = bf16[8,2,2,128,128]{4,3,2,1,0:T(8,128)(2,1)} custom-call(bf16[128,2048]{1,0:T(8,128)(2,1)} %a_ref.2, bf16[128,2048]{1,0:T(8,128)(2,1)} %b_ref.2), custom_call_target="tpu_custom_call" | custom-call | tf_op jit(solution)/shard_map/pallas_call | solution.py:49
  10.9 12.5 %all-to-all-done.1.kv0_ref = bf16[8,2,2,128,128]{4,3,2,1,0:T(8,128)(2,1)S(1)} async-done(((bf16[8,2,2,128,128]{4,3,2,1,0:T(8,128)(2,1)}), bf16[8,2,2,128,128]{4,3,2,1,0:T(8,128)(2,1)S(1)}, u32[]{:S(2)}, u32[]{:S(2)}) %all-to-all-start.1) | async-done | bytes 1048608 | tf_op jit(solution)/shard_map/all_to_all | solution.py:26
  23.5 3.7 %all-to-all-start = ((bf16[8,2,2,128,128]{4,3,2,1,0:T(8,128)(2,1)}), bf16[8,2,2,128,128]{4,3,2,1,0:T(8,128)(2,1)S(1)}, u32[]{:S(2)}, u32[]{:S(2)}) async-start(bf16[8,2,2,128,128]{4,3,2,1,0:T(8,128)(2,1)} %shard_map.93), calls=%async_computation | async-start | bytes 2097152 | tf_op jit(solution)/shard_map/all_to_all | solution.py:26
  27.2 3.6 %collective-permute-start = (bf16[8,2,2,128,128]{4,3,2,1,0:T(8,128)(2,1)S(1)}, bf16[8,2,2,128,128]{4,3,2,1,0:T(8,128)(2,1)S(1)}, u32[]{:S(2)}, u32[]{:S(2)}) collective-permute-start(bf16[8,2,2,128,128]{4,3,2,1,0:T(8,128)(2,1)S(1)} %all-to-all-done.1.kv0_ref), channel_id=1, source_target_pairs={{0,1},{1,2},{2,3},{3,4},{4,5},{5,6},{6,7},{7,8},{8,9},{9,10},{10,1... | collective-permute-start | bytes 3145736 | tf_op jit(solution)/shard_map/ppermute | solution.py:22
  30.8 0.0 copy-done.5
  30.8 0.1 fusion.2
  30.8 0.1 pad_add_fusion
  30.9 0.8 fusion.1
  31.7 0.1 copy.10
  31.8 0.1 broadcast_in_dim.18
  31.9 0.1 reshape.14.bias_ref
  32.1 17.5 %all-to-all-done.qg_ref = bf16[8,2,2,128,128]{4,3,2,1,0:T(8,128)(2,1)S(1)} async-done(((bf16[8,2,2,128,128]{4,3,2,1,0:T(8,128)(2,1)}), bf16[8,2,2,128,128]{4,3,2,1,0:T(8,128)(2,1)S(1)}, u32[]{:S(2)}, u32[]{:S(2)}) %all-to-all-start) | async-done | bytes 1048608 | tf_op jit(solution)/shard_map/all_to_all | solution.py:26
  49.6 12.1 %collective-permute-done.kv1_ref = bf16[8,2,2,128,128]{4,3,2,1,0:T(8,128)(2,1)S(1)} collective-permute-done((bf16[8,2,2,128,128]{4,3,2,1,0:T(8,128)(2,1)S(1)}, bf16[8,2,2,128,128]{4,3,2,1,0:T(8,128)(2,1)S(1)}, u32[]{:S(2)}, u32[]{:S(2)}) %collective-permute-start) | collective-permute-done | bytes 1048608 | tf_op jit(solution)/shard_map/ppermute | solution.py:22
  61.6 22.4 %shard_map.95 = (bf16[8,2,2,128,128]{4,3,2,1,0:T(8,128)(2,1)S(1)}, f32[8,2,2,128,128]{4,3,2,1,0:T(8,128)}, bf16[8,2,2,128,128]{4,3,2,1,0:T(8,128)(2,1)S(1)}) custom-call(f32[4,4,2048]{2,1,0:T(4,128)S(1)} %reshape.14.bias_ref, bf16[8,2,2,128,128]{4,3,2,1,0:T(8,128)(2,1)S(1)} %all-to-all-done.qg_ref, bf16[8,2,2,128,128]{4,3,2,1,0:T(8,128)(2,1)S(1)} %all-to-all-done.1.kv0_ref, ...), custom_call_target="tpu_custom_call" | custom-call | tf_op jit(solution)/shard_map/pallas_call | solution.py:136
  84.1 0.0 copy-start
  84.1 1.0 copy-done
  85.0 1.0 copy-done.1
  86.0 4.3 %all-to-all-start.2 = ((bf16[8,2,2,128,128]{4,3,2,1,0:T(8,128)(2,1)}), bf16[8,2,2,128,128]{4,3,2,1,0:T(8,128)(2,1)S(1)}, u32[]{:S(2)}, u32[]{:S(2)}) async-start(bf16[8,2,2,128,128]{4,3,2,1,0:T(8,128)(2,1)} %copy-done), calls=%async_computation.2 | async-start | bytes 2097152 | tf_op jit(solution)/shard_map/all_to_all | solution.py:26
  90.3 0.0 copy-done.2
  90.4 0.1 collective-permute-start.1
  90.4 18.3 %collective-permute-done.1 = bf16[8,2,2,128,128]{4,3,2,1,0:T(8,128)(2,1)S(1)} collective-permute-done((bf16[8,2,2,128,128]{4,3,2,1,0:T(8,128)(2,1)S(1)}, bf16[8,2,2,128,128]{4,3,2,1,0:T(8,128)(2,1)S(1)}, u32[]{:S(2)}, u32[]{:S(2)}) %collective-permute-start.1) | collective-permute-done | bytes 1048608 | tf_op jit(solution)/shard_map/ppermute | solution.py:22
  108.8 2.9 %add_convert_fusion = bf16[8,2,2,128,128]{4,3,2,1,0:T(8,128)(2,1)} fusion(f32[8,2,2,128,128]{4,3,2,1,0:T(8,128)} %get-tuple-element.14, bf16[8,2,2,128,128]{4,3,2,1,0:T(8,128)(2,1)S(1)} %collective-permute-done.1), kind=kLoop, calls=%fused_computation | loop fusion | flops 1572864 | bytes 4194304 | tf_op jit(solution)/shard_map/convert_element_type | solution.py:179
  111.7 0.0 all-to-all-done.2.i_ref
  111.7 28.0 %all-to-all-start.3 = ((bf16[8,2,2,128,128]{4,3,2,1,0:T(8,128)(2,1)}), bf16[8,2,2,128,128]{4,3,2,1,0:T(8,128)(2,1)S(1)}, u32[]{:S(2)}, u32[]{:S(2)}) async-start(bf16[8,2,2,128,128]{4,3,2,1,0:T(8,128)(2,1)} %add_convert_fusion), calls=%async_computation.3 | async-start | bytes 2097152 | tf_op jit(solution)/shard_map/all_to_all | solution.py:26
  139.7 0.0 copy-done.3
  139.7 2.5 %shard_map.96 = (bf16[128,2048]{1,0:T(8,128)(2,1)}, bf16[128,2048]{1,0:T(8,128)(2,1)}) custom-call(bf16[8,2,2,128,128]{4,3,2,1,0:T(8,128)(2,1)} %copy-done.3), custom_call_target="tpu_custom_call" | custom-call | tf_op jit(solution)/shard_map/pallas_call | solution.py:67
  142.2 7.0 %all-to-all-done.3.i_ref = bf16[8,2,2,128,128]{4,3,2,1,0:T(8,128)(2,1)S(1)} async-done(((bf16[8,2,2,128,128]{4,3,2,1,0:T(8,128)(2,1)}), bf16[8,2,2,128,128]{4,3,2,1,0:T(8,128)(2,1)S(1)}, u32[]{:S(2)}, u32[]{:S(2)}) %all-to-all-start.3) | async-done | bytes 1048608 | tf_op jit(solution)/shard_map/all_to_all | solution.py:26
  149.2 1.0 copy-done.4
  150.1 2.5 %shard_map.97 = (bf16[128,2048]{1,0:T(8,128)(2,1)}, bf16[128,2048]{1,0:T(8,128)(2,1)}) custom-call(bf16[8,2,2,128,128]{4,3,2,1,0:T(8,128)(2,1)} %copy-done.4), custom_call_target="tpu_custom_call" | custom-call | tf_op jit(solution)/shard_map/pallas_call | solution.py:67
  (4 shorter events, 0.0 us)
Async XLA Ops:
  3.0 20.5 %all-to-all-start.1 = ((bf16[8,2,2,128,128]{4,3,2,1,0:T(8,128)(2,1)}), bf16[8,2,2,128,128]{4,3,2,1,0:T(8,128)(2,1)S(1)}, u32[]{:S(2)}, u32[]{:S(2)}) async-start(bf16[8,2,2,128,128]{4,3,2,1,0:T(8,128)(2,1)} %shard_map.94), calls=%async_computation.1 | async-start | bytes 2097152 | tf_op jit(solution)/shard_map/all_to_all | solution.py:26
  8.5 22.2 %copy-start.5 = (s32[512]{0:T(512)S(1)}, s32[512]{0:T(512)}, u32[]{:S(2)}) copy-start(s32[512]{0:T(512)} %param.10) | copy-start | bytes 6148
  23.5 26.1 %all-to-all-start = ((bf16[8,2,2,128,128]{4,3,2,1,0:T(8,128)(2,1)}), bf16[8,2,2,128,128]{4,3,2,1,0:T(8,128)(2,1)S(1)}, u32[]{:S(2)}, u32[]{:S(2)}) async-start(bf16[8,2,2,128,128]{4,3,2,1,0:T(8,128)(2,1)} %shard_map.93), calls=%async_computation | async-start | bytes 2097152 | tf_op jit(solution)/shard_map/all_to_all | solution.py:26
  27.2 34.5 %collective-permute-start = (bf16[8,2,2,128,128]{4,3,2,1,0:T(8,128)(2,1)S(1)}, bf16[8,2,2,128,128]{4,3,2,1,0:T(8,128)(2,1)S(1)}, u32[]{:S(2)}, u32[]{:S(2)}) collective-permute-start(bf16[8,2,2,128,128]{4,3,2,1,0:T(8,128)(2,1)S(1)} %all-to-all-done.1.kv0_ref), channel_id=1, source_target_pairs={{0,1},{1,2},{2,3},{3,4},{4,5},{5,6},{6,7},{7,8},{8,9},{9,10},{10,1... | collective-permute-start | bytes 3145736 | tf_op jit(solution)/shard_map/ppermute | solution.py:22
  84.1 1.0 copy-start
  85.0 1.0 copy-start.1
  86.0 4.3 %copy-start.2 = (bf16[8,2,2,128,128]{4,3,2,1,0:T(8,128)(2,1)S(1)}, bf16[8,2,2,128,128]{4,3,2,1,0:T(8,128)(2,1)}, u32[]{:S(2)}) copy-start(bf16[8,2,2,128,128]{4,3,2,1,0:T(8,128)(2,1)} %copy-done.1) | copy-start | bytes 3145732
  86.0 25.7 %all-to-all-start.2 = ((bf16[8,2,2,128,128]{4,3,2,1,0:T(8,128)(2,1)}), bf16[8,2,2,128,128]{4,3,2,1,0:T(8,128)(2,1)S(1)}, u32[]{:S(2)}, u32[]{:S(2)}) async-start(bf16[8,2,2,128,128]{4,3,2,1,0:T(8,128)(2,1)} %copy-done), calls=%async_computation.2 | async-start | bytes 2097152 | tf_op jit(solution)/shard_map/all_to_all | solution.py:26
  90.4 18.4 %collective-permute-start.1 = (bf16[8,2,2,128,128]{4,3,2,1,0:T(8,128)(2,1)S(1)}, bf16[8,2,2,128,128]{4,3,2,1,0:T(8,128)(2,1)S(1)}, u32[]{:S(2)}, u32[]{:S(2)}) collective-permute-start(bf16[8,2,2,128,128]{4,3,2,1,0:T(8,128)(2,1)S(1)} %copy-done.2), channel_id=1, source_target_pairs={{0,31},{1,0},{2,1},{3,2},{4,3},{5,4},{6,5},{7,6},{8,7},{9,8},{10,9... | collective-permute-start | bytes 3145736 | tf_op jit(solution)/shard_map/ppermute | solution.py:22
  111.7 28.0 %copy-start.3 = (bf16[8,2,2,128,128]{4,3,2,1,0:T(8,128)(2,1)}, bf16[8,2,2,128,128]{4,3,2,1,0:T(8,128)(2,1)S(1)}, u32[]{:S(2)}) copy-start(bf16[8,2,2,128,128]{4,3,2,1,0:T(8,128)(2,1)S(1)} %all-to-all-done.2.i_ref) | copy-start | bytes 3145732
  111.7 37.5 %all-to-all-start.3 = ((bf16[8,2,2,128,128]{4,3,2,1,0:T(8,128)(2,1)}), bf16[8,2,2,128,128]{4,3,2,1,0:T(8,128)(2,1)S(1)}, u32[]{:S(2)}, u32[]{:S(2)}) async-start(bf16[8,2,2,128,128]{4,3,2,1,0:T(8,128)(2,1)} %add_convert_fusion), calls=%async_computation.3 | async-start | bytes 2097152 | tf_op jit(solution)/shard_map/all_to_all | solution.py:26
  149.2 1.0 copy-start.4

commit v2 on v1

--- a/solution.py
+++ b/solution.py
@@ -1,5 +1,3 @@
-import functools
-
 import jax
 import jax.numpy as jnp
 from jax import lax
@@ -14,16 +12,15 @@
 TILE = 256
 SCALE = 1.0 / HEAD**0.5
 LOG2E = 1.4426950408889634
-
-
-def shifted(value, axis, steps):
-    count = lax.axis_size(axis)
-    pairs = [(source, (source + steps) % count) for source in range(count)]
-    return lax.ppermute(value, axis, pairs)
+RUN = 8
 
 
 def exchanged(value):
     return lax.all_to_all(value, "inner", split_axis=0, concat_axis=0, tiled=True)
+
+
+def added(a, b):
+    return (a.astype(jnp.float32) + b.astype(jnp.float32)).astype(jnp.bfloat16)
 
 
 def dot(a, b):
@@ -52,7 +49,23 @@
     )(a, b)
 
 
-def unpack_kernel(i_ref, a_ref, b_ref):
+def unpack_kernel(*refs):
+    parts, (a_ref, b_ref) = refs[:-2], refs[-2:]
+    heads = len(parts)
+    for head, part in enumerate(parts):
+        for peer in range(part.shape[0]):
+            at = (peer * heads + head) * HEAD
+            a_ref[:, at : at + HEAD] = part[peer, 0]
+            b_ref[:, at : at + HEAD] = part[peer, 1]
+
+
+def unpack(parts):
+    peers, _, rows, _ = parts[0].shape
+    shape = jax.ShapeDtypeStruct((rows, peers * len(parts) * HEAD), parts[0].dtype)
+    return pl.pallas_call(unpack_kernel, out_shape=(shape, shape))(*parts)
+
+
+def split_kernel(i_ref, a_ref, b_ref):
     peers, heads = i_ref.shape[0], i_ref.shape[1]
     for peer in range(peers):
         for head in range(heads):
@@ -61,17 +74,17 @@
             b_ref[:, at : at + HEAD] = i_ref[peer, head, 1]
 
 
-def unpack(packed):
+def split(packed):
     peers, heads, _, rows, _ = packed.shape
     shape = jax.ShapeDtypeStruct((rows, peers * heads * HEAD), packed.dtype)
-    return pl.pallas_call(unpack_kernel, out_shape=(shape, shape))(packed)
+    return pl.pallas_call(split_kernel, out_shape=(shape, shape))(packed)
 
 
 def attention_kernel(bias_ref, qg_ref, kv0_ref, kv1_ref, oq_ref, own_ref, prev_ref, acc_k, acc_v, s_ref):
-    step = pl.program_id(1)
-    span = kv0_ref.shape[0] * kv0_ref.shape[3]
-    keys = (kv0_ref[:, 0, 0].reshape(span, HEAD), kv1_ref[:, 0, 0].reshape(span, HEAD))
-    vals = (kv0_ref[:, 0, 1].reshape(span, HEAD), kv1_ref[:, 0, 1].reshape(span, HEAD))
+    step = pl.program_id(0)
+    span = kv1_ref.shape[0] * kv1_ref.shape[2]
+    keys = (kv0_ref[:, 0, 0].reshape(span, HEAD), kv1_ref[:, 0].reshape(span, HEAD))
+    vals = (kv0_ref[:, 0, 1].reshape(span, HEAD), kv1_ref[:, 1].reshape(span, HEAD))
     q = qg_ref[:, 0, 0].reshape(TILE, HEAD)
     g = qg_ref[:, 0, 1].reshape(TILE, HEAD)
 
@@ -110,46 +123,46 @@
         dq = dq + dot(ds, keys[half])
         acc_k[:, cols] += dot(qt, ds)
         acc_v[:, cols] += dot(gt, pb[:, cols])
-    oq_ref[:, 0, 0] = out.reshape(oq_ref.shape[0], -1, HEAD)
-    oq_ref[:, 0, 1] = (dq * SCALE).astype(jnp.bfloat16).reshape(oq_ref.shape[0], -1, HEAD)
-
-    @pl.when(step == pl.num_programs(1) - 1)
+    oq_ref[:, 0] = out.reshape(oq_ref.shape[0], -1, HEAD)
+    oq_ref[:, 1] = (dq * SCALE).astype(jnp.bfloat16).reshape(oq_ref.shape[0], -1, HEAD)
+
+    @pl.when(step == pl.num_programs(0) - 1)
     def _():
         blocks = own_ref.shape[0]
-        rows = own_ref.shape[3]
+        rows = own_ref.shape[2]
         for which, acc, factor in ((0, acc_k, SCALE), (1, acc_v, 1.0)):
             for block in range(blocks):
                 at = block * rows
-                own_ref[block, 0, which] = (acc[:, at : at + rows].T * factor).astype(own_ref.dtype)
+                own_ref[block, which] = (acc[:, at : at + rows].T * factor).astype(own_ref.dtype)
                 at += span
-                prev_ref[block, 0, which] = (acc[:, at : at + rows].T * factor).astype(prev_ref.dtype)
-
-
-def attention(bias, qg, kv0, kv1):
-    peers, heads, _, rows, _ = qg.shape
+                prev_ref[block, which] = (acc[:, at : at + rows].T * factor).astype(prev_ref.dtype)
+
+
+def attention(bias, qg, kv0, kv1, head):
+    peers, _, _, rows, _ = qg.shape
     tiles = peers * rows // TILE
     per = TILE // rows
-    whole = pl.BlockSpec((peers, 1, 2, rows, HEAD), lambda h, i: (0, h, 0, 0, 0))
-    tile = pl.BlockSpec((per, 1, 2, rows, HEAD), lambda h, i: (i, h, 0, 0, 0))
-    shape = jax.ShapeDtypeStruct(qg.shape, jnp.bfloat16)
     width = 2 * peers * rows
+    whole = pl.BlockSpec((peers, 2, rows, HEAD), lambda i: (0, 0, 0, 0))
+    shape = jax.ShapeDtypeStruct((peers, 2, rows, HEAD), jnp.bfloat16)
     return pl.pallas_call(
         attention_kernel,
-        grid=(heads, tiles),
+        grid=(tiles,),
         in_specs=[
-            pl.BlockSpec((1, TILE // CH, width), lambda h, i: (i, 0, 0)),
-            tile,
-            whole,
+            pl.BlockSpec((1, TILE // CH, width), lambda i: (i, 0, 0)),
+            pl.BlockSpec((per, 1, 2, rows, HEAD), lambda i: (i, head, 0, 0, 0)),
+            pl.BlockSpec((peers, 1, 2, rows, HEAD), lambda i: (0, head, 0, 0, 0)),
             whole,
         ],
-        out_specs=(tile, whole, whole),
-        out_shape=(shape, jax.ShapeDtypeStruct(qg.shape, jnp.float32), shape),
+        out_specs=(pl.BlockSpec((per, 2, rows, HEAD), lambda i: (i, 0, 0, 0)), whole, whole),
+        out_shape=(pltpu.HBM(shape.shape, shape.dtype), shape, shape),
         scratch_shapes=[
             pltpu.VMEM((HEAD, width), jnp.float32),
             pltpu.VMEM((HEAD, width), jnp.float32),
             pltpu.VMEM((TILE, width), jnp.float32),
         ],
         compiler_params=pltpu.CompilerParams(vmem_limit_bytes=48 * 2**20),
+        cost_estimate=pl.CostEstimate(flops=12 * 10**9, bytes_accessed=4 * 2**20, transcendentals=2 * 2**20),
     )(bias, qg, kv0, kv1)
 
 
@@ -165,19 +178,56 @@
     return wide.reshape(span * CH // TILE, TILE // CH, -1)
 
 
+def hop(value, pairs, count):
+    flat = [(i * count + s, j * count + d) for (s, i), (d, j) in pairs]
+    return lax.ppermute(value, ("inner", "outer"), flat)
+
+
+def shifted(value, steps, relay):
+    count, peers = lax.axis_size("outer"), lax.axis_size("inner")
+    edge, entry = (RUN - 1, 0) if steps == 1 else (0, RUN - 1)
+    first, second = [], []
+    for s in range(count):
+        for i in range(peers):
+            to = (s + steps) % count
+            if s % RUN == edge and i in relay:
+                near = s // RUN * RUN + entry
+                first.append(((s, i), (near, i)))
+                second.append(((near, i), (to, i)))
+            else:
+                first.append(((s, i), (to, i)))
+    got = hop(value, first, count)
+    if not second:
+        return got
+    far = hop(got, second, count)
+    inner = lax.axis_index("inner")
+    relayed = jnp.logical_and(lax.axis_index("outer") % RUN == entry, jnp.logical_and(inner >= relay[0], inner <= relay[-1]))
+    return jnp.where(relayed, far, got)
+
+
 def body(queries, keys, values, out_grad, stretch_pos, block_mask):
     peers = lax.axis_size("inner")
     groups = lax.axis_size("outer")
     group = lax.axis_index("outer")
     bias = window_bias(stretch_pos, block_mask, group, groups, 2 * peers)
     kv = exchanged(pack(keys, values, peers))
-    prev_kv = shifted(kv, "outer", 1)
-    qg = exchanged(pack(queries, out_grad, peers))
-    oq, own, prev = attention(bias, qg, kv, prev_kv)
-    back = shifted(prev, "outer", -1)
-    output, dquery = unpack(exchanged(oq))
-    dkv = (own + back.astype(jnp.float32)).astype(jnp.bfloat16)
-    d_key, d_value = unpack(exchanged(dkv))
+    head0, head1, packed = lax.optimization_barrier((kv[:, 0], kv[:, 1], pack(queries, out_grad, peers)))
+    prev_kv0 = shifted(head0, 1, range(peers))
+    prev_kv1 = shifted(head1, 1, ())
+    qg = exchanged(packed)
+    oq0, own0, prev0 = attention(bias, qg, kv, prev_kv0, 0)
+    own0, bias = lax.optimization_barrier((own0, bias))
+    oq0 = exchanged(oq0)
+    back0 = shifted(prev0, -1, ())
+    oq1, own1, prev1 = attention(bias, qg, kv, prev_kv1, 1)
+    oq0, oq1 = lax.optimization_barrier((oq0, oq1))
+    back0, prev1 = lax.optimization_barrier((back0, prev1))
+    back1 = shifted(prev1, -1, range(peers // 2, peers))
+    oq1 = exchanged(oq1)
+    output, dquery = unpack([oq0, oq1])
+    own = jnp.stack([own0, own1], axis=1)
+    back = jnp.stack([back0, back1], axis=1)
+    d_key, d_value = split(exchanged(added(own, back)))
     return (output, dquery, d_key, d_value)
 
 

time: 154 us -> 142 us (0.922)
  waiting for transfers between devices: 67.4 us -> 53.1 us
    all_to_all x4 -> x5, waiting for transfers between devices: 37 us -> 25.4 us  [exchanged(): lax.all_to_all(value, 'inner', split_axis=0, concat_axis=0, tiled=True)]
    ppermute x2 -> x6, starting transfers between devices: 3.69 us -> 13.6 us  [hop(): return lax.ppermute(value, ('inner', 'outer'), flat)]
    all_to_all x4 -> x5, starting transfers between devices: 41.6 us -> 32.7 us  [exchanged(): lax.all_to_all(value, 'inner', split_axis=0, concat_axis=0, tiled=True)]
    ppermute x2 -> x6, waiting for transfers between devices: 30.4 us -> 27.6 us  [hop(): return lax.ppermute(value, ('inner', 'outer'), flat)]
    pallas_call x3 -> x4, Pallas kernels: 27.4 us -> 28.5 us  [the longest x2 23.6 us: attention(): pl.pallas_call(attention_kernel, grid=(tiles,), in_specs=[pl.BlockSpec((1...]
  transfers between devices with their start and end apart: 6 -> 11, of which waited for: 5 -> 6; matrix products, arithmetic and copies ran while one was open for 3% -> 3% of each run, Pallas kernels for 3% -> 20%
where the time goes in v2:
time: 142 us; the launch traced here: 141 us
  waiting for transfers between devices  53.1 us (37%)
  starting transfers between devices  46.3 us (33%)
  Pallas kernels  33.2 us (23%)
  other arithmetic  4.49 us (3%)
  local copies, waits for them, and re-layouts  3.12 us (2%)
    all_to_all x5, starting transfers between devices, exchanged(): lax.all_to_all(value, 'inner', split_axis=0, concat_axis=0, tiled=True)  32.7 us
    ppermute x6, waiting for transfers between devices, hop(): return lax.ppermute(value, ('inner', 'outer'), flat)  27.6 us
    all_to_all x5, waiting for transfers between devices, exchanged(): lax.all_to_all(value, 'inner', split_axis=0, concat_axis=0, tiled=True)  25.4 us
    pallas_call x2, Pallas kernels, attention(): pl.pallas_call(attention_kernel, grid=(tiles,), in_specs=[pl.BlockSpec((1...  23.6 us
    ppermute x6, starting transfers between devices, hop(): return lax.ppermute(value, ('inner', 'outer'), flat)  13.6 us
    pallas_call x2, Pallas kernels, pack(): pl.pallas_call(pack_kernel, out_shape=jax.ShapeDtypeStruct((peers, heads,...  4.75 us
  transfers between devices with their start and end apart: 11, of which 6 were waited for; matrix products, arithmetic and copies ran while one was open for 3% of the time, Pallas kernels for 20%

profile of v2, /device:TPU:7, one launch (start us, length us, event | category | flops | bytes accessed | tf_op | source)
XLA Modules:
  0.0 140.9 jit_solution(4237531885745553156)
XLA Ops:
  0.6 2.3 %shard_map.93 = bf16[8,2,2,128,128]{4,3,2,1,0:T(8,128)(2,1)} custom-call(bf16[128,2048]{1,0:T(8,128)(2,1)} %a_ref.2, bf16[128,2048]{1,0:T(8,128)(2,1)} %b_ref.2), custom_call_target="tpu_custom_call" | custom-call | tf_op jit(solution)/shard_map/pallas_call | solution.py:46
  3.0 5.5 %all-to-all-start = ((bf16[8,2,2,128,128]{4,3,2,1,0:T(8,128)(2,1)}), bf16[8,2,2,128,128]{4,3,2,1,0:T(8,128)(2,1)S(1)}, u32[]{:S(2)}, u32[]{:S(2)}) async-start(bf16[8,2,2,128,128]{4,3,2,1,0:T(8,128)(2,1)} %shard_map.93), calls=%async_computation | async-start | bytes 2097152 | tf_op jit(solution)/shard_map/all_to_all | solution.py:19
  8.5 2.4 %shard_map.94 = bf16[8,2,2,128,128]{4,3,2,1,0:T(8,128)(2,1)} custom-call(bf16[128,2048]{1,0:T(8,128)(2,1)} %a_ref.3, bf16[128,2048]{1,0:T(8,128)(2,1)} %b_ref.3), custom_call_target="tpu_custom_call" | custom-call | tf_op jit(solution)/shard_map/pallas_call | solution.py:46
  10.9 12.5 %all-to-all-done.kv0_ref = bf16[8,2,2,128,128]{4,3,2,1,0:T(8,128)(2,1)S(1)} async-done(((bf16[8,2,2,128,128]{4,3,2,1,0:T(8,128)(2,1)}), bf16[8,2,2,128,128]{4,3,2,1,0:T(8,128)(2,1)S(1)}, u32[]{:S(2)}, u32[]{:S(2)}) %all-to-all-start) | async-done | bytes 1048608 | tf_op jit(solution)/shard_map/all_to_all | solution.py:19
  23.4 0.9 slice_bitcast_fusion
  24.3 3.8 %all-to-all-start.1 = ((bf16[8,2,2,128,128]{4,3,2,1,0:T(8,128)(2,1)}), bf16[8,2,2,128,128]{4,3,2,1,0:T(8,128)(2,1)S(1)}, u32[]{:S(2)}, u32[]{:S(2)}) async-start(bf16[8,2,2,128,128]{4,3,2,1,0:T(8,128)(2,1)} %shard_map.94), calls=%async_computation.1 | async-start | bytes 2097152 | tf_op jit(solution)/shard_map/all_to_all | solution.py:19
  28.2 0.9 collective-permute-start
  29.0 6.1 %collective-permute-done = bf16[8,2,128,128]{3,2,1,0:T(8,128)(2,1)S(1)} collective-permute-done((bf16[8,2,128,128]{3,2,1,0:T(8,128)(2,1)S(1)}, bf16[8,2,128,128]{3,2,1,0:T(8,128)(2,1)S(1)}, u32[]{:S(2)}, u32[]{:S(2)}) %collective-permute-start) | collective-permute-done | bytes 524320 | tf_op jit(solution)/shard_map/ppermute | solution.py:183
  35.1 1.5 %collective-permute-start.1 = (bf16[8,2,128,128]{3,2,1,0:T(8,128)(2,1)S(1)}, bf16[8,2,128,128]{3,2,1,0:T(8,128)(2,1)}, u32[]{:S(2)}, u32[]{:S(2)}) collective-permute-start(bf16[8,2,128,128]{3,2,1,0:T(8,128)(2,1)S(1)} %collective-permute-done), channel_id=1, source_target_pairs={{0,8},{32,40},{64,72},{96,104},{128,136},{160,168},{192,200},{224,... | collective-permute-start | bytes 1572872 | tf_op jit(solution)/shard_map/ppermute | solution.py:183
  36.6 0.1 fusion.2
  36.7 0.1 pad_add_fusion
  36.8 0.8 fusion.1
  37.5 0.1 copy.14
  37.6 0.1 broadcast_in_dim.18
  37.8 0.1 reshape.14.bias_ref
  37.9 10.6 %collective-permute-start.2 = (bf16[8,2,128,128]{3,2,1,0:T(8,128)(2,1)}, bf16[8,2,128,128]{3,2,1,0:T(8,128)(2,1)}, u32[]{:S(2)}, u32[]{:S(2)}) collective-permute-start(bf16[8,2,128,128]{3,2,1,0:T(8,128)(2,1)} %get-tuple-element.28), channel_id=1, source_target_pairs={{0,1},{32,33},{64,65},{96,97},{128,129},{160,161},{192,193},{224,2... | collective-permute-start | bytes 1572872 | tf_op jit(solution)/shard_map/ppermute | solution.py:183
  48.5 1.1 broadcast_select_fusion.kv1_ref
  49.6 11.4 %shard_map.95 = (bf16[8,2,128,128]{3,2,1,0:T(8,128)(2,1)}, bf16[8,2,128,128]{3,2,1,0:T(8,128)(2,1)S(1)}, bf16[8,2,128,128]{3,2,1,0:T(8,128)(2,1)}) custom-call(f32[4,4,2048]{2,1,0:T(4,128)S(1)} %reshape.14.bias_ref, bf16[8,2,2,128,128]{4,3,2,1,0:T(8,128)(2,1)S(1)} %all-to-all-done.1.qg_ref, bf16[8,2,2,128,128]{4,3,2,1,0:T(8,128)(2,1)S(1)} %all-to-all-done.kv0_ref, ...), custom_call_target="tpu_custom_call" | custom-call | flops 12000000000 | bytes 4194304 | tf_op jit(solution)/shard_map/pallas_call | solution.py:148
  60.9 5.4 %all-to-all-start.2 = ((bf16[8,2,128,128]{3,2,1,0:T(8,128)(2,1)}), bf16[8,2,128,128]{3,2,1,0:T(8,128)(2,1)}, u32[]{:S(2)}, u32[]{:S(2)}) async-start(bf16[8,2,128,128]{3,2,1,0:T(8,128)(2,1)} %get-tuple-element.25), calls=%async_computation.2 | async-start | bytes 1048576 | tf_op jit(solution)/shard_map/all_to_all | solution.py:19
  66.4 12.2 %shard_map.96 = (bf16[8,2,128,128]{3,2,1,0:T(8,128)(2,1)}, bf16[8,2,128,128]{3,2,1,0:T(8,128)(2,1)S(1)}, bf16[8,2,128,128]{3,2,1,0:T(8,128)(2,1)S(1)}) custom-call(f32[4,4,2048]{2,1,0:T(4,128)S(1)} %reshape.14.bias_ref, bf16[8,2,2,128,128]{4,3,2,1,0:T(8,128)(2,1)S(1)} %all-to-all-done.1.qg_ref, bf16[8,2,2,128,128]{4,3,2,1,0:T(8,128)(2,1)S(1)} %all-to-all-done.kv0_ref, ...), custom_call_target="tpu_custom_call" | custom-call | flops 12000000000 | bytes 4194304 | tf_op jit(solution)/shard_map/pallas_call | solution.py:148
  78.6 6.1 %collective-permute-done.3 = bf16[8,2,128,128]{3,2,1,0:T(8,128)(2,1)S(1)} collective-permute-done((bf16[8,2,128,128]{3,2,1,0:T(8,128)(2,1)}, bf16[8,2,128,128]{3,2,1,0:T(8,128)(2,1)S(1)}, u32[]{:S(2)}, u32[]{:S(2)}) %collective-permute-start.3) | collective-permute-done | bytes 524320 | tf_op jit(solution)/shard_map/ppermute | solution.py:183
  84.7 15.4 %collective-permute-done.4 = bf16[8,2,128,128]{3,2,1,0:T(8,128)(2,1)S(1)} collective-permute-done((bf16[8,2,128,128]{3,2,1,0:T(8,128)(2,1)S(1)}, bf16[8,2,128,128]{3,2,1,0:T(8,128)(2,1)S(1)}, u32[]{:S(2)}, u32[]{:S(2)}) %collective-permute-start.4) | collective-permute-done | bytes 524320 | tf_op jit(solution)/shard_map/ppermute | solution.py:183
  100.1 0.7 collective-permute-start.5
  100.8 12.0 %all-to-all-start.3 = ((bf16[8,2,128,128]{3,2,1,0:T(8,128)(2,1)}), bf16[8,2,128,128]{3,2,1,0:T(8,128)(2,1)S(1)}, u32[]{:S(2)}, u32[]{:S(2)}) async-start(bf16[8,2,128,128]{3,2,1,0:T(8,128)(2,1)} %get-tuple-element.31), calls=%async_computation.3 | async-start | bytes 1048576 | tf_op jit(solution)/shard_map/all_to_all | solution.py:19
  112.8 2.5 %add_convert_fusion = bf16[8,2,2,128,128]{4,3,2,1,0:T(8,128)(2,1)} fusion(bf16[8,1,2,128,128]{4,3,2,1,0:T(8,128)(2,1)S(1)} %bitcast.14, bf16[8,1,2,128,128]{4,3,2,1,0:T(8,128)(2,1)S(1)} %bitcast.13, bf16[8,1,2,128,128]{4,3,2,1,0:T(8,128)(2,1)S(1)} %select_bitcast_fusion, bf16[8,1,2,128,128]{4,3,2,1,0:T(8,128)(2,1)} %bitcast.15), kind=kLoop, calls=%fused_computation | loop fusion | flops 3145728 | bytes 3145728 | tf_op jit(solution)/shard_map/convert_element_type | solution.py:23
  115.3 5.9 %all-to-all-done.3.refs_1_ = bf16[8,2,128,128]{3,2,1,0:T(8,128)(2,1)S(1)} async-done(((bf16[8,2,128,128]{3,2,1,0:T(8,128)(2,1)}), bf16[8,2,128,128]{3,2,1,0:T(8,128)(2,1)S(1)}, u32[]{:S(2)}, u32[]{:S(2)}) %all-to-all-start.3) | async-done | bytes 524320 | tf_op jit(solution)/shard_map/all_to_all | solution.py:19
  121.2 0.8 copy-done.1
  122.0 6.0 %all-to-all-start.4 = ((bf16[8,2,2,128,128]{4,3,2,1,0:T(8,128)(2,1)}), bf16[8,2,2,128,128]{4,3,2,1,0:T(8,128)(2,1)S(1)}, u32[]{:S(2)}, u32[]{:S(2)}) async-start(bf16[8,2,2,128,128]{4,3,2,1,0:T(8,128)(2,1)} %add_convert_fusion), calls=%async_computation.4 | async-start | bytes 2097152 | tf_op jit(solution)/shard_map/all_to_all | solution.py:19
  128.0 2.5 %shard_map.97 = (bf16[128,2048]{1,0:T(8,128)(2,1)}, bf16[128,2048]{1,0:T(8,128)(2,1)}) custom-call(bf16[8,2,128,128]{3,2,1,0:T(8,128)(2,1)} %all-to-all-done.2.refs_0_, bf16[8,2,128,128]{3,2,1,0:T(8,128)(2,1)} %copy-done.1), custom_call_target="tpu_custom_call" | custom-call | tf_op jit(solution)/shard_map/pallas_call | solution.py:65
  130.4 7.0 %all-to-all-done.4.i_ref = bf16[8,2,2,128,128]{4,3,2,1,0:T(8,128)(2,1)S(1)} async-done(((bf16[8,2,2,128,128]{4,3,2,1,0:T(8,128)(2,1)}), bf16[8,2,2,128,128]{4,3,2,1,0:T(8,128)(2,1)S(1)}, u32[]{:S(2)}, u32[]{:S(2)}) %all-to-all-start.4) | async-done | bytes 1048608 | tf_op jit(solution)/shard_map/all_to_all | solution.py:19
  137.4 1.0 copy-done
  138.4 2.5 %shard_map.98 = (bf16[128,2048]{1,0:T(8,128)(2,1)}, bf16[128,2048]{1,0:T(8,128)(2,1)}) custom-call(bf16[8,2,2,128,128]{4,3,2,1,0:T(8,128)(2,1)} %copy-done), custom_call_target="tpu_custom_call" | custom-call | tf_op jit(solution)/shard_map/pallas_call | solution.py:80
  (16 shorter events, 0.1 us)
Async XLA Ops:
  3.0 20.5 %all-to-all-start = ((bf16[8,2,2,128,128]{4,3,2,1,0:T(8,128)(2,1)}), bf16[8,2,2,128,128]{4,3,2,1,0:T(8,128)(2,1)S(1)}, u32[]{:S(2)}, u32[]{:S(2)}) async-start(bf16[8,2,2,128,128]{4,3,2,1,0:T(8,128)(2,1)} %shard_map.93), calls=%async_computation | async-start | bytes 2097152 | tf_op jit(solution)/shard_map/all_to_all | solution.py:19
  24.3 12.3 %copy-start.4 = (s32[512]{0:T(512)S(1)}, s32[512]{0:T(512)}, u32[]{:S(2)}) copy-start(s32[512]{0:T(512)} %param.10) | copy-start | bytes 6148
  24.3 25.2 %all-to-all-start.1 = ((bf16[8,2,2,128,128]{4,3,2,1,0:T(8,128)(2,1)}), bf16[8,2,2,128,128]{4,3,2,1,0:T(8,128)(2,1)S(1)}, u32[]{:S(2)}, u32[]{:S(2)}) async-start(bf16[8,2,2,128,128]{4,3,2,1,0:T(8,128)(2,1)} %shard_map.94), calls=%async_computation.1 | async-start | bytes 2097152 | tf_op jit(solution)/shard_map/all_to_all | solution.py:19
  28.2 7.0 %collective-permute-start = (bf16[8,2,128,128]{3,2,1,0:T(8,128)(2,1)S(1)}, bf16[8,2,128,128]{3,2,1,0:T(8,128)(2,1)S(1)}, u32[]{:S(2)}, u32[]{:S(2)}) collective-permute-start(bf16[8,2,128,128]{3,2,1,0:T(8,128)(2,1)S(1)} %get-tuple-element.24), channel_id=1, source_target_pairs={{0,1},{32,33},{64,65},{96,97},{128,129},{160,161},{192,193},{224,2... | collective-permute-start | bytes 1572872 | tf_op jit(solution)/shard_map/ppermute | solution.py:183
  35.1 13.3 %copy-start.2 = (bf16[8,2,128,128]{3,2,1,0:T(8,128)(2,1)}, bf16[8,2,128,128]{3,2,1,0:T(8,128)(2,1)S(1)}, u32[]{:S(2)}) copy-start(bf16[8,2,128,128]{3,2,1,0:T(8,128)(2,1)S(1)} %collective-permute-done) | copy-start | bytes 1572868
  35.1 13.3 %collective-permute-start.1 = (bf16[8,2,128,128]{3,2,1,0:T(8,128)(2,1)S(1)}, bf16[8,2,128,128]{3,2,1,0:T(8,128)(2,1)}, u32[]{:S(2)}, u32[]{:S(2)}) collective-permute-start(bf16[8,2,128,128]{3,2,1,0:T(8,128)(2,1)S(1)} %collective-permute-done), channel_id=1, source_target_pairs={{0,8},{32,40},{64,72},{96,104},{128,136},{160,168},{192,200},{224,... | collective-permute-start | bytes 1572872 | tf_op jit(solution)/shard_map/ppermute | solution.py:183
  37.9 28.5 %collective-permute-start.2 = (bf16[8,2,128,128]{3,2,1,0:T(8,128)(2,1)}, bf16[8,2,128,128]{3,2,1,0:T(8,128)(2,1)}, u32[]{:S(2)}, u32[]{:S(2)}) collective-permute-start(bf16[8,2,128,128]{3,2,1,0:T(8,128)(2,1)} %get-tuple-element.28), channel_id=1, source_target_pairs={{0,1},{32,33},{64,65},{96,97},{128,129},{160,161},{192,193},{224,2... | collective-permute-start | bytes 1572872 | tf_op jit(solution)/shard_map/ppermute | solution.py:183
  60.9 39.8 %all-to-all-start.2 = ((bf16[8,2,128,128]{3,2,1,0:T(8,128)(2,1)}), bf16[8,2,128,128]{3,2,1,0:T(8,128)(2,1)}, u32[]{:S(2)}, u32[]{:S(2)}) async-start(bf16[8,2,128,128]{3,2,1,0:T(8,128)(2,1)} %get-tuple-element.25), calls=%async_computation.2 | async-start | bytes 1048576 | tf_op jit(solution)/shard_map/all_to_all | solution.py:19
  66.4 18.3 %collective-permute-start.3 = (bf16[8,2,128,128]{3,2,1,0:T(8,128)(2,1)}, bf16[8,2,128,128]{3,2,1,0:T(8,128)(2,1)S(1)}, u32[]{:S(2)}, u32[]{:S(2)}) collective-permute-start(bf16[8,2,128,128]{3,2,1,0:T(8,128)(2,1)} %get-tuple-element.36), channel_id=1, source_target_pairs={{0,31},{32,63},{64,95},{96,127},{128,159},{160,191},{192,223},{224... | collective-permute-start | bytes 1572872 | tf_op jit(solution)/shard_map/ppermute | solution.py:183
  84.7 15.4 %copy-start.3 = (bf16[8,2,128,128]{3,2,1,0:T(8,128)(2,1)}, bf16[8,2,128,128]{3,2,1,0:T(8,128)(2,1)S(1)}, u32[]{:S(2)}) copy-start(bf16[8,2,128,128]{3,2,1,0:T(8,128)(2,1)S(1)} %collective-permute-done.3) | copy-start | bytes 1572868
  84.7 15.4 %collective-permute-start.4 = (bf16[8,2,128,128]{3,2,1,0:T(8,128)(2,1)S(1)}, bf16[8,2,128,128]{3,2,1,0:T(8,128)(2,1)S(1)}, u32[]{:S(2)}, u32[]{:S(2)}) collective-permute-start(bf16[8,2,128,128]{3,2,1,0:T(8,128)(2,1)S(1)} %get-tuple-element.39), channel_id=1, source_target_pairs={{0,31},{32,63},{64,95},{96,127},{128,135},{160,167},{192,199},{224... | collective-permute-start | bytes 1572872 | tf_op jit(solution)/shard_map/ppermute | solution.py:183
  100.1 12.7 %collective-permute-start.5 = (bf16[8,2,128,128]{3,2,1,0:T(8,128)(2,1)S(1)}, bf16[8,2,128,128]{3,2,1,0:T(8,128)(2,1)S(1)}, u32[]{:S(2)}, u32[]{:S(2)}) collective-permute-start(bf16[8,2,128,128]{3,2,1,0:T(8,128)(2,1)S(1)} %collective-permute-done.4), channel_id=1, source_target_pairs={{135,159},{167,191},{199,223},{231,255},{143,135},{175,167},{207,1... | collective-permute-start | bytes 1572872 | tf_op jit(solution)/shard_map/ppermute | solution.py:183
  100.8 20.4 %all-to-all-start.3 = ((bf16[8,2,128,128]{3,2,1,0:T(8,128)(2,1)}), bf16[8,2,128,128]{3,2,1,0:T(8,128)(2,1)S(1)}, u32[]{:S(2)}, u32[]{:S(2)}) async-start(bf16[8,2,128,128]{3,2,1,0:T(8,128)(2,1)} %get-tuple-element.31), calls=%async_computation.3 | async-start | bytes 1048576 | tf_op jit(solution)/shard_map/all_to_all | solution.py:19
  121.2 0.8 copy-start.1
  122.0 15.4 %all-to-all-start.4 = ((bf16[8,2,2,128,128]{4,3,2,1,0:T(8,128)(2,1)}), bf16[8,2,2,128,128]{4,3,2,1,0:T(8,128)(2,1)S(1)}, u32[]{:S(2)}, u32[]{:S(2)}) async-start(bf16[8,2,2,128,128]{4,3,2,1,0:T(8,128)(2,1)} %add_convert_fusion), calls=%async_computation.4 | async-start | bytes 2097152 | tf_op jit(solution)/shard_map/all_to_all | solution.py:19
  137.4 1.0 copy-start

commit v3 on v1

v3 whole, which is shorter than its diff:
```python
import jax
import jax.numpy as jnp
from jax import lax
from jax.experimental import pallas as pl
from jax.experimental.pallas import tpu as pltpu
from jax.sharding import PartitionSpec as P

H = 16
HEAD = 128
CH = 64
NEG = -1e30
TILE = 256
SCALE = 1.0 / HEAD**0.5
LOG2E = 1.4426950408889634
RUN = 8


def exchanged(value):
    return lax.all_to_all(value, "inner", split_axis=0, concat_axis=0, tiled=True)


def added(a, b):
    return (a.astype(jnp.float32) + b.astype(jnp.float32)).astype(jnp.bfloat16)


def dot(a, b):
    return lax.dot_general(a, b, (((1,), (0,)), ((), ())), preferred_element_type=jnp.float32)


def dot_t(a, b):
    return lax.dot_general(a, b, (((1,), (1,)), ((), ())), preferred_element_type=jnp.float32)


def pack_kernel(a_ref, b_ref, *o_refs):
    for peer in range(o_refs[0].shape[0]):
        for head, o_ref in enumerate(o_refs):
            at = (peer * len(o_refs) + head) * HEAD
            for which, ref in enumerate((a_ref, b_ref)):
                o_ref[peer, which] = ref[:, at : at + HEAD]


def pack(a, b, peers):
    rows, width = a.shape
    shape = pltpu.HBM((peers, 2, rows, HEAD), a.dtype)
    return pl.pallas_call(pack_kernel, out_shape=(shape,) * (width // HEAD // peers))(a, b)


def unpack_kernel(i_ref, a_ref, b_ref, va, vb, come, go):
    peers, heads = i_ref.shape[:2]
    held = []
    for which, to in enumerate((va, vb)):
        for at in range(peers * heads):
            part = i_ref.at[at // heads, at % heads, which]
            held.append(pltpu.make_async_copy(part, to.at[:, pl.ds(at * HEAD, HEAD)], come.at[at, which]))
            held[-1].start()
    for copy in held:
        copy.wait()
    held = [pltpu.make_async_copy(x, y, go.at[n]) for n, (x, y) in enumerate(((va, a_ref), (vb, b_ref)))]
    for copy in held:
        copy.start()
    for copy in held:
        copy.wait()


def unpack(packed):
    peers, heads, _, rows, _ = packed.shape
    shape = pltpu.HBM((rows, peers * heads * HEAD), packed.dtype)
    room = pltpu.VMEM((rows, peers * heads * HEAD), packed.dtype)
    return pl.pallas_call(
        unpack_kernel,
        out_shape=(shape, shape),
        in_specs=[pl.BlockSpec(memory_space=pl.ANY)],
        out_specs=(pl.BlockSpec(memory_space=pltpu.HBM),) * 2,
        scratch_shapes=[room, room, pltpu.SemaphoreType.DMA((peers * heads, 2)), pltpu.SemaphoreType.DMA((2,))],
        compiler_params=pltpu.CompilerParams(vmem_limit_bytes=48 * 2**20),
    )(packed)


def attend(bias_ref, qg_ref, keys, vals, put, acc_k, acc_v, s_ref, dp_ref):
    span = keys[0].shape[0]
    rows = qg_ref.shape[2]
    per = TILE // rows
    row = lax.broadcasted_iota(jnp.int32, (TILE, TILE), 0)
    col = lax.broadcasted_iota(jnp.int32, (TILE, TILE), 1)
    later = jnp.where(jnp.logical_and(row // CH == col // CH, col > row), NEG, 0.0)
    halves = [slice(half * span, (half + 1) * span) for half in range(2)]

    def scores(tile):
        q = qg_ref[tile * per : (tile + 1) * per, 0].reshape(TILE, HEAD)
        g = qg_ref[tile * per : (tile + 1) * per, 1].reshape(TILE, HEAD)
        own = slice(tile * TILE, (tile + 1) * TILE)
        for half, cols in enumerate(halves):
            seen = [bias_ref[0, at // CH : at // CH + 1, cols] for at in range(own.start, own.stop, CH)]
            seen = jnp.concatenate([jnp.broadcast_to(line, (CH, span)) for line in seen], axis=0)
            s = dot_t(q, keys[half]) * (SCALE * LOG2E) + seen
            if half == 0:
                parts = (s[:, : own.start], s[:, own] + later, s[:, own.stop :])
                s = jnp.concatenate([part for part in parts if part.shape[1]], axis=1)
            s_ref[tile % 2, :, cols] = s
            dp_ref[tile % 2, :, cols] = dot_t(g, vals[half])
        return q, g

    def finish(tile, q, g):
        s = s_ref[tile % 2]
        top = jnp.max(s, axis=1, keepdims=True)
        e = jnp.exp2(s - top)
        total = jnp.sum(e, axis=1, keepdims=True)
        p = e * (1.0 / total)
        pb = p.astype(jnp.bfloat16)
        out = (dot(pb[:, halves[0]], vals[0]) + dot(pb[:, halves[1]], vals[1])).astype(jnp.bfloat16)
        delta = jnp.sum(g.astype(jnp.float32) * out.astype(jnp.float32), axis=1, keepdims=True)
        dq = jnp.zeros((TILE, HEAD), jnp.float32)
        qt, gt = q.T, g.T
        for half, cols in enumerate(halves):
            ds = (p[:, cols] * (dp_ref[tile % 2, :, cols] - delta)).astype(jnp.bfloat16)
            dq = dq + dot(ds, keys[half])
            for acc, term in ((acc_k, dot(qt, ds)), (acc_v, dot(gt, pb[:, cols]))):
                acc[:, cols] = term if tile == 0 else acc[:, cols] + term
        put(slice(tile * per, (tile + 1) * per), out, (dq * SCALE).astype(jnp.bfloat16))

    tiles = span // TILE
    after = scores(0)
    for tile in range(tiles):
        now = after
        if tile + 1 < tiles:
            after = scores(tile + 1)
        finish(tile, *now)


def attention_kernel(bias_ref, qg_ref, own_ref, prev_ref, *rest):
    oq_ref, d_ref, back_ref = rest[-7:-4]
    scratch = rest[-4:]
    peers, _, rows, _ = own_ref.shape

    def put(blocks, out, dq):
        for which, value in ((0, out), (1, dq)):
            oq_ref[blocks, 0, which] = value.reshape(-1, rows, HEAD)

    keys, vals = ((own_ref[:, w].reshape(-1, HEAD), prev_ref[:, w].reshape(-1, HEAD)) for w in range(2))
    attend(bias_ref, qg_ref, keys, vals, put, *scratch)
    for which, acc, factor in ((0, scratch[0], SCALE), (1, scratch[1], 1.0)):
        for block in range(peers):
            at = block * rows
            d_ref[block, 0, which] = (acc[:, at : at + rows].T * factor).astype(d_ref.dtype)
            at += peers * rows
            back_ref[block, which] = (acc[:, at : at + rows].T * factor).astype(back_ref.dtype)


def attention(bias, qg, own, prev, head, heads, *held):
    peers, _, rows, _ = own.shape
    width = 2 * peers * rows
    whole = pl.BlockSpec(own.shape, lambda i: (0, 0, 0, 0))
    slot = pl.BlockSpec((peers, 1, 2, rows, HEAD), lambda i: (0, head, 0, 0, 0))
    both = pltpu.HBM((peers, heads, 2, rows, HEAD), own.dtype)
    return pl.pallas_call(
        attention_kernel,
        grid=(1,),
        in_specs=[pl.BlockSpec((1, width // 2 // CH, width), lambda i: (0, 0, 0)), whole, whole, whole]
        + [pl.BlockSpec(memory_space=pl.ANY)] * len(held),
        out_specs=(slot, slot, whole),
        out_shape=(both, both, jax.ShapeDtypeStruct(own.shape, own.dtype)),
        input_output_aliases={4 + n: n for n in range(len(held))},
        scratch_shapes=[pltpu.VMEM((HEAD, width), jnp.float32)] * 2 + [pltpu.VMEM((2, TILE, width), jnp.float32)] * 2,
        compiler_params=pltpu.CompilerParams(vmem_limit_bytes=48 * 2**20),
        cost_estimate=pl.CostEstimate(flops=12 * 10**9, bytes_accessed=4 * 2**20, transcendentals=2 * 2**20),
    )(bias, qg, own, prev, *held)


def window_bias(stretch_pos, block_mask, group, groups, span):
    prev = (group + groups - 1) % groups
    own_pos = lax.dynamic_slice_in_dim(stretch_pos, group * span, span, 0)
    prev_pos = lax.dynamic_slice_in_dim(stretch_pos, prev * span, span, 0)
    key_pos = jnp.concatenate([own_pos, prev_pos], axis=0)
    flags = lax.dynamic_slice_in_dim(block_mask, group * span, span, 0)
    seen = jnp.logical_and(flags == 1, key_pos[None, :] <= own_pos[:, None])
    bias = jnp.where(seen, 0.0, NEG).astype(jnp.float32)
    wide = jnp.broadcast_to(bias[:, :, None], bias.shape + (CH,))
    return wide.reshape(1, span, -1)


def hop(value, pairs, count):
    flat = [(i * count + s, j * count + d) for (s, i), (d, j) in pairs]
    return lax.ppermute(value, ("inner", "outer"), flat)


def routes(steps, relay, count, peers):
    edge, entry = (RUN - 1, 0) if steps == 1 else (0, RUN - 1)
    within, direct, second = [], [], []
    for s in range(count):
        for i in range(peers):
            to = (s + steps) % count
            if s % RUN != edge:
                within.append(((s, i), (to, i)))
            elif i in relay:
                near = s // RUN * RUN + entry
                within.append(((s, i), (near, i)))
                second.append(((near, i), (to, i)))
            else:
                direct.append(((s, i), (to, i)))
    return within, direct, second


def sent(value, steps, relay):
    count, peers = lax.axis_size("outer"), lax.axis_size("inner")
    within, direct, second = routes(steps, relay, count, peers)
    across = hop(value, direct, count) if direct else None

    def finish(near):
        far = hop(near, second, count) if second else across
        if direct and second:
            inner = lax.axis_index("inner")
            far = jnp.where(jnp.logical_and(inner >= relay[0], inner <= relay[-1]), far, across)
        return jnp.where(lax.axis_index("outer") % RUN == (0 if steps == 1 else RUN - 1), far, near)

    return hop(value, within, count), finish


def shifted(value, steps):
    count = lax.axis_size("outer")
    return lax.ppermute(value, "outer", [(s, (s + steps) % count) for s in range(count)])


def after(value, *earlier):
    return lax.optimization_barrier((value, *earlier))


def add_at(d, head, back):
    own = lax.index_in_dim(d, head, 1, keepdims=False)
    return lax.dynamic_update_slice_in_dim(d, added(own, back)[:, None], head, axis=1)


def body(queries, keys, values, out_grad, stretch_pos, block_mask):
    peers = lax.axis_size("inner")
    groups = lax.axis_size("outer")
    bias = window_bias(stretch_pos, block_mask, lax.axis_index("outer"), groups, 2 * peers)
    upper = range(peers // 2, peers)
    kv0, kv1 = pack(keys, values, peers)
    qg0, qg1 = pack(queries, out_grad, peers)
    kv0 = exchanged(kv0)
    kv1, kv0 = after(kv1, kv0)
    near, finish = sent(kv0, 1, upper)
    kv1 = exchanged(kv1)
    qg0, kv1, near = after(qg0, kv1, near)
    prev_kv1 = shifted(kv1, 1)
    qg0 = exchanged(qg0)
    prev_kv0 = finish(near)
    qg1, qg0 = after(qg1, qg0)
    qg1 = exchanged(qg1)
    oq, d, back0 = attention(bias, qg0, kv0, prev_kv0, 0, 2)
    back0 = shifted(back0, -1)
    oq, d, back1 = attention(bias, qg1, kv1, prev_kv1, 1, 2, oq, d)
    back1, back0 = after(back1, back0)
    near, finish = sent(back1, -1, upper)
    oq = exchanged(oq)
    d = add_at(d, 0, back0)
    d = add_at(d, 1, finish(near))
    d, oq = after(d, oq)
    output, dquery = unpack(oq)
    d_key, d_value = unpack(exchanged(d))
    return (output, dquery, d_key, d_value)


def solution(mesh):
    rows = P(("outer", "inner"), None)
    return jax.shard_map(
        body,
        mesh=mesh,
        in_specs=(rows, rows, rows, rows, P(), P()),
        out_specs=(rows, rows, rows, rows),
        check_vma=False,
    )
```

time: 154 us -> 131 us (0.85)
  waiting for transfers between devices: 67.4 us -> 24.9 us
  blocking collectives: 0 us -> 14.2 us
  starting transfers between devices: 45.3 us -> 57.1 us
  Pallas kernels: 32.1 us -> 26.4 us
    all_to_all x4 -> x5, waiting for transfers between devices: 37 us -> 9.25 us  [exchanged(): lax.all_to_all(value, 'inner', split_axis=0, concat_axis=0, tiled=True)]
    ppermute x2 -> x8, waiting for transfers between devices: 30.4 us -> 15.6 us  [the longest x6 13.4 us: hop(): return lax.ppermute(value, ('inner', 'outer'), flat)]
    all_to_all x0 -> x1, blocking collectives: none -> 14.2 us  [exchanged(): lax.all_to_all(value, 'inner', split_axis=0, concat_axis=0, tiled=True)]
    ppermute x2 -> x8, starting transfers between devices: 3.69 us -> 17.1 us  [the longest x6 17 us: hop(): return lax.ppermute(value, ('inner', 'outer'), flat)]
    pallas_call x5 -> x6, Pallas kernels: 32.1 us -> 26.4 us  [the longest x2 18.5 us: attention(): pl.pallas_call(attention_kernel, grid=(1,), in_specs=[pl.BlockSpec((1, wi...]
    convert_element_type x1 -> x0, other arithmetic: 2.92 us -> none  [body(): dkv = (own + back.astype(jnp.float32)).astype(jnp.bfloat16)]
    dynamic_update_slice x0 -> x2, other arithmetic: none -> 2.37 us  [add_at(): lax.dynamic_update_slice_in_dim(d, added(own, back)[:, None], head, axis=1)]
    unnamed x12 -> x5, local copies, waits for them, and re-layouts: 2.95 us -> 0.72 us
  transfers between devices with their start and end apart: 6 -> 13, of which waited for: 5 -> 7; matrix products, arithmetic and copies ran while one was open for 3% -> 5% of each run, Pallas kernels for 3% -> 17%
where the time goes in v3:
time: 131 us; the launch traced here: 130 us
  starting transfers between devices  57.1 us (44%)
  Pallas kernels  26.4 us (20%)
  waiting for transfers between devices  24.9 us (19%)
  blocking collectives  14.2 us (11%)
  other arithmetic  4.35 us (3%)
  local copies, waits for them, and re-layouts  2.31 us (2%)
    all_to_all x5, starting transfers between devices, exchanged(): lax.all_to_all(value, 'inner', split_axis=0, concat_axis=0, tiled=True)  40.1 us
    pallas_call x2, Pallas kernels, attention(): pl.pallas_call(attention_kernel, grid=(1,), in_specs=[pl.BlockSpec((1, wi...  18.5 us
    ppermute x6, starting transfers between devices, hop(): return lax.ppermute(value, ('inner', 'outer'), flat)  17 us
    all_to_all x1, blocking collectives, exchanged(): lax.all_to_all(value, 'inner', split_axis=0, concat_axis=0, tiled=True)  14.2 us
    ppermute x6, waiting for transfers between devices, hop(): return lax.ppermute(value, ('inner', 'outer'), flat)  13.4 us
    all_to_all x5, waiting for transfers between devices, exchanged(): lax.all_to_all(value, 'inner', split_axis=0, concat_axis=0, tiled=True)  9.25 us
    pallas_call x2, Pallas kernels, pack(): pl.pallas_call(pack_kernel, out_shape=(shape,) * (width // HEAD // peers))  4.68 us
    pallas_call x2, Pallas kernels, unpack(): pl.pallas_call(unpack_kernel, out_shape=(shape, shape), in_specs=[pl.Bloc...  3.21 us
  transfers between devices with their start and end apart: 13, of which 7 were waited for; matrix products, arithmetic and copies ran while one was open for 5% of the time, Pallas kernels for 17%

profile of v3, /device:TPU:7, one launch (start us, length us, event | category | flops | bytes accessed | tf_op | source)
XLA Modules:
  0.0 130.1 jit_solution(16161663400090764581)
XLA Ops:
  0.6 2.3 %shard_map.94 = (bf16[8,2,128,128]{3,2,1,0:T(8,128)(2,1)}, bf16[8,2,128,128]{3,2,1,0:T(8,128)(2,1)}) custom-call(bf16[128,2048]{1,0:T(8,128)(2,1)} %a_ref.3, bf16[128,2048]{1,0:T(8,128)(2,1)} %b_ref.3), custom_call_target="tpu_custom_call" | custom-call | tf_op jit(solution)/shard_map/pallas_call | solution.py:45
  3.0 14.2 %all_to_all.30.own_ref = bf16[8,2,128,128]{3,2,1,0:T(8,128)(2,1)S(1)} all-to-all(bf16[8,2,128,128]{3,2,1,0:T(8,128)(2,1)} %get-tuple-element.32), channel_id=1, replica_groups=mesh['inner'=8,'outer'=32] {'inner'}, dimensions={0} | all-to-all | bytes 1048576 | tf_op jit(solution)/shard_map/all_to_all | solution.py:19
  17.1 3.5 %all-to-all-start.1 = ((bf16[8,2,128,128]{3,2,1,0:T(8,128)(2,1)}), bf16[8,2,128,128]{3,2,1,0:T(8,128)(2,1)S(1)}, u32[]{:S(2)}, u32[]{:S(2)}) async-start(bf16[8,2,128,128]{3,2,1,0:T(8,128)(2,1)} %get-tuple-element.33), calls=%async_computation.1 | async-start | bytes 1048576 | tf_op jit(solution)/shard_map/all_to_all | solution.py:19
  20.6 1.3 collective-permute-start
  21.9 2.3 %shard_map.93 = (bf16[8,2,128,128]{3,2,1,0:T(8,128)(2,1)}, bf16[8,2,128,128]{3,2,1,0:T(8,128)(2,1)}) custom-call(bf16[128,2048]{1,0:T(8,128)(2,1)} %a_ref.2, bf16[128,2048]{1,0:T(8,128)(2,1)} %b_ref.2), custom_call_target="tpu_custom_call" | custom-call | tf_op jit(solution)/shard_map/pallas_call | solution.py:45
  24.3 2.1 %collective-permute-done = bf16[8,2,128,128]{3,2,1,0:T(8,128)(2,1)S(1)} collective-permute-done((bf16[8,2,128,128]{3,2,1,0:T(8,128)(2,1)S(1)}, bf16[8,2,128,128]{3,2,1,0:T(8,128)(2,1)S(1)}, u32[]{:S(2)}, u32[]{:S(2)}) %collective-permute-start) | collective-permute-done | bytes 524320 | tf_op jit(solution)/shard_map/ppermute | solution.py:183
  26.3 1.4 %all-to-all-done.1.own_ref = bf16[8,2,128,128]{3,2,1,0:T(8,128)(2,1)S(1)} async-done(((bf16[8,2,128,128]{3,2,1,0:T(8,128)(2,1)}), bf16[8,2,128,128]{3,2,1,0:T(8,128)(2,1)S(1)}, u32[]{:S(2)}, u32[]{:S(2)}) %all-to-all-start.1) | async-done | bytes 524320 | tf_op jit(solution)/shard_map/all_to_all | solution.py:19
  27.7 8.8 %all-to-all-start.2 = ((bf16[8,2,128,128]{3,2,1,0:T(8,128)(2,1)}), bf16[8,2,128,128]{3,2,1,0:T(8,128)(2,1)S(1)}, u32[]{:S(2)}, u32[]{:S(2)}) async-start(bf16[8,2,128,128]{3,2,1,0:T(8,128)(2,1)} %get-tuple-element.35), calls=%async_computation.2 | async-start | bytes 1048576 | tf_op jit(solution)/shard_map/all_to_all | solution.py:19
  36.5 9.4 %collective-permute-start.3 = (bf16[8,2,128,128]{3,2,1,0:T(8,128)(2,1)S(1)}, bf16[8,2,128,128]{3,2,1,0:T(8,128)(2,1)}, u32[]{:S(2)}, u32[]{:S(2)}) collective-permute-start(bf16[8,2,128,128]{3,2,1,0:T(8,128)(2,1)S(1)} %all_to_all.30.own_ref), channel_id=1, source_target_pairs={{7,8},{39,40},{71,72},{103,104},{15,16},{47,48},{79,80},{111,112},... | collective-permute-start | bytes 1572872 | tf_op jit(solution)/shard_map/ppermute | solution.py:183
  45.9 1.5 %collective-permute-start.2 = (bf16[8,2,128,128]{3,2,1,0:T(8,128)(2,1)S(1)}, bf16[8,2,128,128]{3,2,1,0:T(8,128)(2,1)}, u32[]{:S(2)}, u32[]{:S(2)}) collective-permute-start(bf16[8,2,128,128]{3,2,1,0:T(8,128)(2,1)S(1)} %collective-permute-done), channel_id=1, source_target_pairs={{128,136},{160,168},{192,200},{224,232},{136,144},{168,176},{200,2... | collective-permute-start | bytes 1572872 | tf_op jit(solution)/shard_map/ppermute | solution.py:183
  47.3 0.7 copy-done.1
  48.2 0.8 fusion.7
  49.0 0.1 broadcast_in_dim.24
  49.2 0.1 reshape.18.bias_ref
  49.4 1.8 %collective-permute-done.3 = bf16[8,2,128,128]{3,2,1,0:T(8,128)(2,1)} collective-permute-done((bf16[8,2,128,128]{3,2,1,0:T(8,128)(2,1)S(1)}, bf16[8,2,128,128]{3,2,1,0:T(8,128)(2,1)}, u32[]{:S(2)}, u32[]{:S(2)}) %collective-permute-start.3) | collective-permute-done | bytes 524320 | tf_op jit(solution)/shard_map/ppermute | solution.py:183
  51.2 1.1 select_select_fusion.prev_ref
  52.3 6.5 %all-to-all-start.3 = ((bf16[8,2,128,128]{3,2,1,0:T(8,128)(2,1)}), bf16[8,2,128,128]{3,2,1,0:T(8,128)(2,1)S(1)}, u32[]{:S(2)}, u32[]{:S(2)}) async-start(bf16[8,2,128,128]{3,2,1,0:T(8,128)(2,1)} %get-tuple-element.36), calls=%async_computation.3 | async-start | bytes 1048576 | tf_op jit(solution)/shard_map/all_to_all | solution.py:19
  58.8 9.3 %shard_map.95 = (bf16[8,2,2,128,128]{4,3,2,1,0:T(8,128)(2,1)}, bf16[8,2,2,128,128]{4,3,2,1,0:T(8,128)(2,1)}, bf16[8,2,128,128]{3,2,1,0:T(8,128)(2,1)}) custom-call(f32[1,16,2048]{2,1,0:T(8,128)S(1)} %reshape.18.bias_ref, bf16[8,2,128,128]{3,2,1,0:T(8,128)(2,1)S(1)} %all-to-all-done.2.qg_ref, bf16[8,2,128,128]{3,2,1,0:T(8,128)(2,1)S(1)} %all_to_all.30.own_ref, ...), custom_call_target="tpu_custom_call" | custom-call | flops 12000000000 | bytes 4194304 | tf_op jit(solution)/shard_map/pallas_call | solution.py:155
  68.1 9.2 %shard_map.96 = (bf16[8,2,2,128,128]{4,3,2,1,0:T(8,128)(2,1)}, bf16[8,2,2,128,128]{4,3,2,1,0:T(8,128)(2,1)}, bf16[8,2,128,128]{3,2,1,0:T(8,128)(2,1)S(1)}) custom-call(f32[1,16,2048]{2,1,0:T(8,128)S(1)} %reshape.18.bias_ref, bf16[8,2,128,128]{3,2,1,0:T(8,128)(2,1)S(1)} %all-to-all-done.3.qg_ref, ...), custom_call_target="tpu_custom_call", output_to_operand_aliasing={{0}: (4, {}), {1}: (5, {})} | custom-call | flops 12000000000 | bytes 4194304 | tf_op jit(solution)/shard_map/pallas_call | solution.py:155
  77.3 6.1 %all-to-all-start.4 = ((bf16[8,2,2,128,128]{4,3,2,1,0:T(8,128)(2,1)}), bf16[8,2,2,128,128]{4,3,2,1,0:T(8,128)(2,1)S(1)}, u32[]{:S(2)}, u32[]{:S(2)}) async-start(bf16[8,2,2,128,128]{4,3,2,1,0:T(8,128)(2,1)} %get-tuple-element.47), calls=%async_computation.4 | async-start | bytes 2097152 | tf_op jit(solution)/shard_map/all_to_all | solution.py:19
  83.5 2.3 %collective-permute-done.4 = bf16[8,2,128,128]{3,2,1,0:T(8,128)(2,1)S(1)} collective-permute-done((bf16[8,2,128,128]{3,2,1,0:T(8,128)(2,1)}, bf16[8,2,128,128]{3,2,1,0:T(8,128)(2,1)S(1)}, u32[]{:S(2)}, u32[]{:S(2)}) %collective-permute-start.4) | collective-permute-done | bytes 524320 | tf_op jit(solution)/shard_map/ppermute | solution.py:220
  85.8 2.1 %collective-permute-start.5 = (bf16[8,2,128,128]{3,2,1,0:T(8,128)(2,1)S(1)}, bf16[8,2,128,128]{3,2,1,0:T(8,128)(2,1)}, u32[]{:S(2)}, u32[]{:S(2)}) collective-permute-start(bf16[8,2,128,128]{3,2,1,0:T(8,128)(2,1)S(1)} %get-tuple-element.46), channel_id=1, source_target_pairs={{128,135},{160,167},{192,199},{224,231},{1,0},{33,32},{65,64},{97,... | collective-permute-start | bytes 1572872 | tf_op jit(solution)/shard_map/ppermute | solution.py:183
  87.8 1.3 collective-permute-start.7
  89.1 1.5 %collective-permute-start.6 = (bf16[8,2,128,128]{3,2,1,0:T(8,128)(2,1)}, bf16[8,2,128,128]{3,2,1,0:T(8,128)(2,1)}, u32[]{:S(2)}, u32[]{:S(2)}) collective-permute-start(bf16[8,2,128,128]{3,2,1,0:T(8,128)(2,1)} %collective-permute-done.5), channel_id=1, source_target_pairs={{135,159},{167,191},{199,223},{231,255},{143,135},{175,167},{207,1... | collective-permute-start | bytes 1572872 | tf_op jit(solution)/shard_map/ppermute | solution.py:183
  90.8 0.2 fusion.3
  91.0 1.1 copy.15
  92.1 9.5 %collective-permute-done.7 = bf16[8,2,128,128]{3,2,1,0:T(8,128)(2,1)} collective-permute-done((bf16[8,2,128,128]{3,2,1,0:T(8,128)(2,1)S(1)}, bf16[8,2,128,128]{3,2,1,0:T(8,128)(2,1)}, u32[]{:S(2)}, u32[]{:S(2)}) %collective-permute-start.7) | collective-permute-done | bytes 524320 | tf_op jit(solution)/shard_map/ppermute | solution.py:183
  101.6 2.2 %fusion.5 = bf16[8,2,2,128,128]{4,3,2,1,0:T(8,128)(2,1)} fusion(bf16[8,2,2,128,128]{4,3,2,1,0:T(8,128)(2,1)} %copy.15, bf16[8,2,2,128,128]{4,3,2,0,1:T(8,128)(2,1)S(1)} %fusion.3, bf16[8,2,128,128]{3,2,1,0:T(8,128)(2,1)} %collective-permute-done.5, bf16[8,2,128,128]{3,2,1,0:T(8,128)(2,1)} %collective-permute-done.6, ...), kind=kLoop, calls=%fused_computation.7 | loop fusion | flops 1572864 | bytes 2621442 | tf_op jit(solution)/shard_map/dynamic_update_slice | solution.py:229
  103.7 15.2 %all-to-all-start.5 = ((bf16[8,2,2,128,128]{4,3,2,1,0:T(8,128)(2,1)}), bf16[8,2,2,128,128]{4,3,2,1,0:T(8,128)(2,1)S(1)}, u32[]{:S(2)}, u32[]{:S(2)}) async-start(bf16[8,2,2,128,128]{4,3,2,1,0:T(8,128)(2,1)} %fusion.5), calls=%async_computation.5 | async-start | bytes 2097152 | tf_op jit(solution)/shard_map/all_to_all | solution.py:19
  118.9 1.6 %shard_map.97 = (bf16[128,2048]{1,0:T(8,128)(2,1)}, bf16[128,2048]{1,0:T(8,128)(2,1)}) custom-call(bf16[8,2,2,128,128]{4,3,2,1,0:T(8,128)(2,1)S(1)} %all-to-all-done.4.i_ref), custom_call_target="tpu_custom_call" | custom-call | tf_op jit(solution)/shard_map/pallas_call | solution.py:69
  120.5 7.8 %all-to-all-done.5.i_ref = bf16[8,2,2,128,128]{4,3,2,1,0:T(8,128)(2,1)S(1)} async-done(((bf16[8,2,2,128,128]{4,3,2,1,0:T(8,128)(2,1)}), bf16[8,2,2,128,128]{4,3,2,1,0:T(8,128)(2,1)S(1)}, u32[]{:S(2)}, u32[]{:S(2)}) %all-to-all-start.5) | async-done | bytes 1048608 | tf_op jit(solution)/shard_map/all_to_all | solution.py:19
  128.4 1.6 %shard_map.98 = (bf16[128,2048]{1,0:T(8,128)(2,1)}, bf16[128,2048]{1,0:T(8,128)(2,1)}) custom-call(bf16[8,2,2,128,128]{4,3,2,1,0:T(8,128)(2,1)S(1)} %all-to-all-done.5.i_ref), custom_call_target="tpu_custom_call" | custom-call | tf_op jit(solution)/shard_map/pallas_call | solution.py:69
  (17 shorter events, 0.5 us)
Async XLA Ops:
  17.1 10.6 %all-to-all-start.1 = ((bf16[8,2,128,128]{3,2,1,0:T(8,128)(2,1)}), bf16[8,2,128,128]{3,2,1,0:T(8,128)(2,1)S(1)}, u32[]{:S(2)}, u32[]{:S(2)}) async-start(bf16[8,2,128,128]{3,2,1,0:T(8,128)(2,1)} %get-tuple-element.33), calls=%async_computation.1 | async-start | bytes 1048576 | tf_op jit(solution)/shard_map/all_to_all | solution.py:19
  20.6 5.7 %collective-permute-start = (bf16[8,2,128,128]{3,2,1,0:T(8,128)(2,1)S(1)}, bf16[8,2,128,128]{3,2,1,0:T(8,128)(2,1)S(1)}, u32[]{:S(2)}, u32[]{:S(2)}) collective-permute-start(bf16[8,2,128,128]{3,2,1,0:T(8,128)(2,1)S(1)} %all_to_all.30.own_ref), channel_id=1, source_target_pairs={{0,1},{32,33},{64,65},{96,97},{128,129},{160,161},{192,193},{224,2... | collective-permute-start | bytes 1572872 | tf_op jit(solution)/shard_map/ppermute | solution.py:183
  27.7 24.6 %all-to-all-start.2 = ((bf16[8,2,128,128]{3,2,1,0:T(8,128)(2,1)}), bf16[8,2,128,128]{3,2,1,0:T(8,128)(2,1)S(1)}, u32[]{:S(2)}, u32[]{:S(2)}) async-start(bf16[8,2,128,128]{3,2,1,0:T(8,128)(2,1)} %get-tuple-element.35), calls=%async_computation.2 | async-start | bytes 1048576 | tf_op jit(solution)/shard_map/all_to_all | solution.py:19
  36.5 14.7 %collective-permute-start.3 = (bf16[8,2,128,128]{3,2,1,0:T(8,128)(2,1)S(1)}, bf16[8,2,128,128]{3,2,1,0:T(8,128)(2,1)}, u32[]{:S(2)}, u32[]{:S(2)}) collective-permute-start(bf16[8,2,128,128]{3,2,1,0:T(8,128)(2,1)S(1)} %all_to_all.30.own_ref), channel_id=1, source_target_pairs={{7,8},{39,40},{71,72},{103,104},{15,16},{47,48},{79,80},{111,112},... | collective-permute-start | bytes 1572872 | tf_op jit(solution)/shard_map/ppermute | solution.py:183
  45.9 5.3 %collective-permute-start.2 = (bf16[8,2,128,128]{3,2,1,0:T(8,128)(2,1)S(1)}, bf16[8,2,128,128]{3,2,1,0:T(8,128)(2,1)}, u32[]{:S(2)}, u32[]{:S(2)}) collective-permute-start(bf16[8,2,128,128]{3,2,1,0:T(8,128)(2,1)S(1)} %collective-permute-done), channel_id=1, source_target_pairs={{128,136},{160,168},{192,200},{224,232},{136,144},{168,176},{200,2... | collective-permute-start | bytes 1572872 | tf_op jit(solution)/shard_map/ppermute | solution.py:183
  47.3 0.7 copy-start.1
  49.3 18.8 %collective-permute-start.1 = (bf16[8,2,128,128]{3,2,1,0:T(8,128)(2,1)S(1)}, bf16[8,2,128,128]{3,2,1,0:T(8,128)(2,1)S(1)}, u32[]{:S(2)}, u32[]{:S(2)}) collective-permute-start(bf16[8,2,128,128]{3,2,1,0:T(8,128)(2,1)S(1)} %all-to-all-done.1.own_ref), channel_id=1, source_target_pairs={{0,1},{1,2},{2,3},{3,4},{4,5},{5,6},{6,7},{7,8},{8,9},{9,10},{10,1... | collective-permute-start | bytes 1572872 | tf_op jit(solution)/shard_map/ppermute | solution.py:220
  52.3 15.8 %all-to-all-start.3 = ((bf16[8,2,128,128]{3,2,1,0:T(8,128)(2,1)}), bf16[8,2,128,128]{3,2,1,0:T(8,128)(2,1)S(1)}, u32[]{:S(2)}, u32[]{:S(2)}) async-start(bf16[8,2,128,128]{3,2,1,0:T(8,128)(2,1)} %get-tuple-element.36), calls=%async_computation.3 | async-start | bytes 1048576 | tf_op jit(solution)/shard_map/all_to_all | solution.py:19
  68.1 17.7 %collective-permute-start.4 = (bf16[8,2,128,128]{3,2,1,0:T(8,128)(2,1)}, bf16[8,2,128,128]{3,2,1,0:T(8,128)(2,1)S(1)}, u32[]{:S(2)}, u32[]{:S(2)}) collective-permute-start(bf16[8,2,128,128]{3,2,1,0:T(8,128)(2,1)} %get-tuple-element.44), channel_id=1, source_target_pairs={{0,31},{1,0},{2,1},{3,2},{4,3},{5,4},{6,5},{7,6},{8,7},{9,8},{10,9... | collective-permute-start | bytes 1572872 | tf_op jit(solution)/shard_map/ppermute | solution.py:220
  77.3 13.3 %copy-start = (bf16[8,2,2,128,128]{4,3,2,1,0:T(8,128)(2,1)S(1)}, bf16[8,2,2,128,128]{4,3,2,1,0:T(8,128)(2,1)}, u32[]{:S(2)}) copy-start(bf16[8,2,2,128,128]{4,3,2,1,0:T(8,128)(2,1)} %get-tuple-element.42) | copy-start | bytes 3145732
  77.3 26.4 %all-to-all-start.4 = ((bf16[8,2,2,128,128]{4,3,2,1,0:T(8,128)(2,1)}), bf16[8,2,2,128,128]{4,3,2,1,0:T(8,128)(2,1)S(1)}, u32[]{:S(2)}, u32[]{:S(2)}) async-start(bf16[8,2,2,128,128]{4,3,2,1,0:T(8,128)(2,1)} %get-tuple-element.47), calls=%async_computation.4 | async-start | bytes 2097152 | tf_op jit(solution)/shard_map/all_to_all | solution.py:19
  85.8 3.4 %collective-permute-start.5 = (bf16[8,2,128,128]{3,2,1,0:T(8,128)(2,1)S(1)}, bf16[8,2,128,128]{3,2,1,0:T(8,128)(2,1)}, u32[]{:S(2)}, u32[]{:S(2)}) collective-permute-start(bf16[8,2,128,128]{3,2,1,0:T(8,128)(2,1)S(1)} %get-tuple-element.46), channel_id=1, source_target_pairs={{128,135},{160,167},{192,199},{224,231},{1,0},{33,32},{65,64},{97,... | collective-permute-start | bytes 1572872 | tf_op jit(solution)/shard_map/ppermute | solution.py:183
  87.8 13.7 %collective-permute-start.7 = (bf16[8,2,128,128]{3,2,1,0:T(8,128)(2,1)S(1)}, bf16[8,2,128,128]{3,2,1,0:T(8,128)(2,1)}, u32[]{:S(2)}, u32[]{:S(2)}) collective-permute-start(bf16[8,2,128,128]{3,2,1,0:T(8,128)(2,1)S(1)} %get-tuple-element.46), channel_id=1, source_target_pairs={{0,31},{32,63},{64,95},{96,127},{8,7},{40,39},{72,71},{104,103},{1... | collective-permute-start | bytes 1572872 | tf_op jit(solution)/shard_map/ppermute | solution.py:183
  89.1 12.4 %collective-permute-start.6 = (bf16[8,2,128,128]{3,2,1,0:T(8,128)(2,1)}, bf16[8,2,128,128]{3,2,1,0:T(8,128)(2,1)}, u32[]{:S(2)}, u32[]{:S(2)}) collective-permute-start(bf16[8,2,128,128]{3,2,1,0:T(8,128)(2,1)} %collective-permute-done.5), channel_id=1, source_target_pairs={{135,159},{167,191},{199,223},{231,255},{143,135},{175,167},{207,1... | collective-permute-start | bytes 1572872 | tf_op jit(solution)/shard_map/ppermute | solution.py:183
  103.7 24.6 %all-to-all-start.5 = ((bf16[8,2,2,128,128]{4,3,2,1,0:T(8,128)(2,1)}), bf16[8,2,2,128,128]{4,3,2,1,0:T(8,128)(2,1)S(1)}, u32[]{:S(2)}, u32[]{:S(2)}) async-start(bf16[8,2,2,128,128]{4,3,2,1,0:T(8,128)(2,1)} %fusion.5), calls=%async_computation.5 | async-start | bytes 2097152 | tf_op jit(solution)/shard_map/all_to_all | solution.py:19

commit v4 on v3

--- a/solution.py
+++ b/solution.py
@@ -31,18 +31,17 @@
     return lax.dot_general(a, b, (((1,), (1,)), ((), ())), preferred_element_type=jnp.float32)
 
 
-def pack_kernel(a_ref, b_ref, *o_refs):
-    for peer in range(o_refs[0].shape[0]):
-        for head, o_ref in enumerate(o_refs):
-            at = (peer * len(o_refs) + head) * HEAD
-            for which, ref in enumerate((a_ref, b_ref)):
-                o_ref[peer, which] = ref[:, at : at + HEAD]
+def pack_kernel(a_ref, b_ref, o_ref):
+    peers, heads = o_ref.shape[:2]
+    for at in range(peers * heads):
+        for which, ref in enumerate((a_ref, b_ref)):
+            o_ref[at // heads, at % heads, which] = ref[:, at * HEAD : (at + 1) * HEAD]
 
 
 def pack(a, b, peers):
     rows, width = a.shape
-    shape = pltpu.HBM((peers, 2, rows, HEAD), a.dtype)
-    return pl.pallas_call(pack_kernel, out_shape=(shape,) * (width // HEAD // peers))(a, b)
+    shape = pltpu.HBM((peers, width // HEAD // peers, 2, rows, HEAD), a.dtype)
+    return pl.pallas_call(pack_kernel, out_shape=shape)(a, b)
 
 
 def unpack_kernel(i_ref, a_ref, b_ref, va, vb, come, go):
@@ -78,7 +77,7 @@
 
 def attend(bias_ref, qg_ref, keys, vals, put, acc_k, acc_v, s_ref, dp_ref):
     span = keys[0].shape[0]
-    rows = qg_ref.shape[2]
+    rows = qg_ref.shape[3]
     per = TILE // rows
     row = lax.broadcasted_iota(jnp.int32, (TILE, TILE), 0)
     col = lax.broadcasted_iota(jnp.int32, (TILE, TILE), 1)
@@ -86,8 +85,8 @@
     halves = [slice(half * span, (half + 1) * span) for half in range(2)]
 
     def scores(tile):
-        q = qg_ref[tile * per : (tile + 1) * per, 0].reshape(TILE, HEAD)
-        g = qg_ref[tile * per : (tile + 1) * per, 1].reshape(TILE, HEAD)
+        q = qg_ref[tile * per : (tile + 1) * per, 0, 0].reshape(TILE, HEAD)
+        g = qg_ref[tile * per : (tile + 1) * per, 0, 1].reshape(TILE, HEAD)
         own = slice(tile * TILE, (tile + 1) * TILE)
         for half, cols in enumerate(halves):
             seen = [bias_ref[0, at // CH : at // CH + 1, cols] for at in range(own.start, own.stop, CH)]
@@ -130,13 +129,13 @@
 def attention_kernel(bias_ref, qg_ref, own_ref, prev_ref, *rest):
     oq_ref, d_ref, back_ref = rest[-7:-4]
     scratch = rest[-4:]
-    peers, _, rows, _ = own_ref.shape
+    peers, _, rows, _ = prev_ref.shape
 
     def put(blocks, out, dq):
         for which, value in ((0, out), (1, dq)):
             oq_ref[blocks, 0, which] = value.reshape(-1, rows, HEAD)
 
-    keys, vals = ((own_ref[:, w].reshape(-1, HEAD), prev_ref[:, w].reshape(-1, HEAD)) for w in range(2))
+    keys, vals = ((own_ref[:, 0, w].reshape(-1, HEAD), prev_ref[:, w].reshape(-1, HEAD)) for w in range(2))
     attend(bias_ref, qg_ref, keys, vals, put, *scratch)
     for which, acc, factor in ((0, scratch[0], SCALE), (1, scratch[1], 1.0)):
         for block in range(peers):
@@ -146,19 +145,19 @@
             back_ref[block, which] = (acc[:, at : at + rows].T * factor).astype(back_ref.dtype)
 
 
-def attention(bias, qg, own, prev, head, heads, *held):
-    peers, _, rows, _ = own.shape
+def attention(bias, qg, own, prev, head, *held):
+    peers, _, _, rows, _ = own.shape
     width = 2 * peers * rows
-    whole = pl.BlockSpec(own.shape, lambda i: (0, 0, 0, 0))
+    whole = pl.BlockSpec(prev.shape, lambda i: (0, 0, 0, 0))
     slot = pl.BlockSpec((peers, 1, 2, rows, HEAD), lambda i: (0, head, 0, 0, 0))
-    both = pltpu.HBM((peers, heads, 2, rows, HEAD), own.dtype)
+    both = pltpu.HBM(own.shape, own.dtype)
     return pl.pallas_call(
         attention_kernel,
         grid=(1,),
-        in_specs=[pl.BlockSpec((1, width // 2 // CH, width), lambda i: (0, 0, 0)), whole, whole, whole]
+        in_specs=[pl.BlockSpec((1, width // 2 // CH, width), lambda i: (0, 0, 0)), slot, slot, whole]
         + [pl.BlockSpec(memory_space=pl.ANY)] * len(held),
         out_specs=(slot, slot, whole),
-        out_shape=(both, both, jax.ShapeDtypeStruct(own.shape, own.dtype)),
+        out_shape=(both, both, jax.ShapeDtypeStruct(prev.shape, prev.dtype)),
         input_output_aliases={4 + n: n for n in range(len(held))},
         scratch_shapes=[pltpu.VMEM((HEAD, width), jnp.float32)] * 2 + [pltpu.VMEM((2, TILE, width), jnp.float32)] * 2,
         compiler_params=pltpu.CompilerParams(vmem_limit_bytes=48 * 2**20),
@@ -234,21 +233,15 @@
     groups = lax.axis_size("outer")
     bias = window_bias(stretch_pos, block_mask, lax.axis_index("outer"), groups, 2 * peers)
     upper = range(peers // 2, peers)
-    kv0, kv1 = pack(keys, values, peers)
-    qg0, qg1 = pack(queries, out_grad, peers)
-    kv0 = exchanged(kv0)
-    kv1, kv0 = after(kv1, kv0)
+    kv = exchanged(pack(keys, values, peers))
+    kv0, kv1, qg = lax.optimization_barrier((kv[:, 0], kv[:, 1], pack(queries, out_grad, peers)))
     near, finish = sent(kv0, 1, upper)
-    kv1 = exchanged(kv1)
-    qg0, kv1, near = after(qg0, kv1, near)
     prev_kv1 = shifted(kv1, 1)
-    qg0 = exchanged(qg0)
+    qg = exchanged(qg)
     prev_kv0 = finish(near)
-    qg1, qg0 = after(qg1, qg0)
-    qg1 = exchanged(qg1)
-    oq, d, back0 = attention(bias, qg0, kv0, prev_kv0, 0, 2)
+    oq, d, back0 = attention(bias, qg, kv, prev_kv0, 0)
     back0 = shifted(back0, -1)
-    oq, d, back1 = attention(bias, qg1, kv1, prev_kv1, 1, 2, oq, d)
+    oq, d, back1 = attention(bias, qg, kv, prev_kv1, 1, oq, d)
     back1, back0 = after(back1, back0)
     near, finish = sent(back1, -1, upper)
     oq = exchanged(oq)

time: 131 us -> 126 us (0.962)
  blocking collectives: 14.2 us -> 0 us
  waiting for transfers between devices: 24.9 us -> 33 us
  starting transfers between devices: 57.1 us -> 54.1 us
  local copies, waits for them, and re-layouts: 2.31 us -> 4.77 us
    all_to_all x1 -> x0, blocking collectives: 14.2 us -> none  [exchanged(): lax.all_to_all(value, 'inner', split_axis=0, concat_axis=0, tiled=True)]
    all_to_all x5 -> x4, waiting for transfers between devices: 9.25 us -> 20.4 us  [exchanged(): lax.all_to_all(value, 'inner', split_axis=0, concat_axis=0, tiled=True)]
    ppermute x6, starting transfers between devices: 17 us -> 14.2 us  [hop(): return lax.ppermute(value, ('inner', 'outer'), flat)]
    ppermute x2, waiting for transfers between devices: 2.26 us -> 0.01 us  [shifted(): lax.ppermute(value, 'outer', [(s, (s + steps) % count) for s in range(cou...]
    all_to_all x5 -> x4, starting transfers between devices: 40.1 us -> 39.8 us  [exchanged(): lax.all_to_all(value, 'inner', split_axis=0, concat_axis=0, tiled=True)]
  transfers between devices with their start and end apart: 13 -> 12, of which waited for: 7 -> 5; matrix products, arithmetic and copies ran while one was open for 5% -> 7% of each run, Pallas kernels for 17% -> 18%
where the time goes in v4:
time: 126 us; the launch traced here: 125 us
  starting transfers between devices  54.1 us (43%)
  waiting for transfers between devices  33 us (26%)
  Pallas kernels  26.5 us (21%)
  other arithmetic  5.56 us (4%)
  local copies, waits for them, and re-layouts  4.77 us (4%)
    all_to_all x4, starting transfers between devices, exchanged(): lax.all_to_all(value, 'inner', split_axis=0, concat_axis=0, tiled=True)  39.8 us
    all_to_all x4, waiting for transfers between devices, exchanged(): lax.all_to_all(value, 'inner', split_axis=0, concat_axis=0, tiled=True)  20.4 us
    pallas_call x2, Pallas kernels, attention(): pl.pallas_call(attention_kernel, grid=(1,), in_specs=[pl.BlockSpec((1, wi...  18.6 us
    ppermute x6, starting transfers between devices, hop(): return lax.ppermute(value, ('inner', 'outer'), flat)  14.2 us
    ppermute x6, waiting for transfers between devices, hop(): return lax.ppermute(value, ('inner', 'outer'), flat)  12.6 us
    pallas_call x2, Pallas kernels, pack(): return pl.pallas_call(pack_kernel, out_shape=shape)(a, b)  4.73 us
    dynamic_update_slice x2, other arithmetic, add_at(): lax.dynamic_update_slice_in_dim(d, added(own, back)[:, None], head, axis=1)  3.42 us
    pallas_call x2, Pallas kernels, unpack(): pl.pallas_call(unpack_kernel, out_shape=(shape, shape), in_specs=[pl.Bloc...  3.21 us
  transfers between devices with their start and end apart: 12, of which 5 were waited for; matrix products, arithmetic and copies ran while one was open for 7% of the time, Pallas kernels for 18%

profile of v4, /device:TPU:7, one launch (start us, length us, event | category | flops | bytes accessed | tf_op | source)
XLA Modules:
  0.0 124.8 jit_solution(9582842714218917029)
XLA Ops:
  0.6 2.3 %shard_map.93 = bf16[8,2,2,128,128]{4,3,2,1,0:T(8,128)(2,1)} custom-call(bf16[128,2048]{1,0:T(8,128)(2,1)} %a_ref.2, bf16[128,2048]{1,0:T(8,128)(2,1)} %b_ref.2), custom_call_target="tpu_custom_call" | custom-call | tf_op jit(solution)/shard_map/pallas_call | solution.py:44
  3.0 5.5 %all-to-all-start = ((bf16[8,2,2,128,128]{4,3,2,1,0:T(8,128)(2,1)}), bf16[8,2,2,128,128]{4,3,2,1,0:T(8,128)(2,1)S(1)}, u32[]{:S(2)}, u32[]{:S(2)}) async-start(bf16[8,2,2,128,128]{4,3,2,1,0:T(8,128)(2,1)} %shard_map.93), calls=%async_computation | async-start | bytes 2097152 | tf_op jit(solution)/shard_map/all_to_all | solution.py:19
  8.5 2.4 %shard_map.94 = bf16[8,2,2,128,128]{4,3,2,1,0:T(8,128)(2,1)} custom-call(bf16[128,2048]{1,0:T(8,128)(2,1)} %a_ref.3, bf16[128,2048]{1,0:T(8,128)(2,1)} %b_ref.3), custom_call_target="tpu_custom_call" | custom-call | tf_op jit(solution)/shard_map/pallas_call | solution.py:44
  10.9 12.5 %all-to-all-done.own_ref = bf16[8,2,2,128,128]{4,3,2,1,0:T(8,128)(2,1)S(1)} async-done(((bf16[8,2,2,128,128]{4,3,2,1,0:T(8,128)(2,1)}), bf16[8,2,2,128,128]{4,3,2,1,0:T(8,128)(2,1)S(1)}, u32[]{:S(2)}, u32[]{:S(2)}) %all-to-all-start) | async-done | bytes 1048608 | tf_op jit(solution)/shard_map/all_to_all | solution.py:19
  23.4 1.1 slice_bitcast_fusion.2
  24.5 3.7 %all-to-all-start.1 = ((bf16[8,2,2,128,128]{4,3,2,1,0:T(8,128)(2,1)}), bf16[8,2,2,128,128]{4,3,2,1,0:T(8,128)(2,1)S(1)}, u32[]{:S(2)}, u32[]{:S(2)}) async-start(bf16[8,2,2,128,128]{4,3,2,1,0:T(8,128)(2,1)} %shard_map.94), calls=%async_computation.1 | async-start | bytes 2097152 | tf_op jit(solution)/shard_map/all_to_all | solution.py:19
  28.2 1.3 %collective-permute-start.1 = (bf16[8,2,128,128]{3,2,1,0:T(8,128)(2,1)}, bf16[8,2,128,128]{3,2,1,0:T(8,128)(2,1)}, u32[]{:S(2)}, u32[]{:S(2)}) collective-permute-start(bf16[8,2,128,128]{3,2,1,0:T(8,128)(2,1)} %get-tuple-element.23), channel_id=1, source_target_pairs={{0,1},{32,33},{64,65},{96,97},{128,129},{160,161},{192,193},{224,2... | collective-permute-start | bytes 1572872 | tf_op jit(solution)/shard_map/ppermute | solution.py:182
  29.5 7.4 %collective-permute-start.3 = (bf16[8,2,128,128]{3,2,1,0:T(8,128)(2,1)}, bf16[8,2,128,128]{3,2,1,0:T(8,128)(2,1)}, u32[]{:S(2)}, u32[]{:S(2)}) collective-permute-start(bf16[8,2,128,128]{3,2,1,0:T(8,128)(2,1)} %get-tuple-element.23), channel_id=1, source_target_pairs={{7,8},{39,40},{71,72},{103,104},{15,16},{47,48},{79,80},{111,112},... | collective-permute-start | bytes 1572872 | tf_op jit(solution)/shard_map/ppermute | solution.py:182
  36.9 1.5 %collective-permute-start.2 = (bf16[8,2,128,128]{3,2,1,0:T(8,128)(2,1)}, bf16[8,2,128,128]{3,2,1,0:T(8,128)(2,1)}, u32[]{:S(2)}, u32[]{:S(2)}) collective-permute-start(bf16[8,2,128,128]{3,2,1,0:T(8,128)(2,1)} %collective-permute-done.1), channel_id=1, source_target_pairs={{128,136},{160,168},{192,200},{224,232},{136,144},{168,176},{200,2... | collective-permute-start | bytes 1572872 | tf_op jit(solution)/shard_map/ppermute | solution.py:182
  38.4 0.7 copy-done.1
  39.2 0.8 fusion.7
  40.1 0.1 broadcast_in_dim.24
  40.2 0.1 reshape.18.bias_ref
  40.4 5.5 %collective-permute-done.3 = bf16[8,2,128,128]{3,2,1,0:T(8,128)(2,1)} collective-permute-done((bf16[8,2,128,128]{3,2,1,0:T(8,128)(2,1)}, bf16[8,2,128,128]{3,2,1,0:T(8,128)(2,1)}, u32[]{:S(2)}, u32[]{:S(2)}) %collective-permute-start.3) | collective-permute-done | bytes 524320 | tf_op jit(solution)/shard_map/ppermute | solution.py:182
  46.0 1.3 %select_select_fusion.prev_ref = bf16[8,2,128,128]{3,2,1,0:T(8,128)(2,1)S(1)} fusion(bf16[8,2,128,128]{3,2,1,0:T(8,128)(2,1)} %collective-permute-done.1, bf16[8,2,128,128]{3,2,1,0:T(8,128)(2,1)} %collective-permute-done.2, bf16[8,2,128,128]{3,2,1,0:T(8,128)(2,1)} %collective-permute-done.3, pred[]{:T(512)S(6)} %and.22, pred[]{:T(512)S(6)} %eq.18), kind=kLoop, calls=%fused_computation.12 | loop fusion | flops 524288 | bytes 2097154 | tf_op jit(solution)/shard_map/jit(_where)/select_n | solution.py:212
  47.2 9.3 %shard_map.95 = (bf16[8,2,2,128,128]{4,3,2,1,0:T(8,128)(2,1)}, bf16[8,2,2,128,128]{4,3,2,1,0:T(8,128)(2,1)}, bf16[8,2,128,128]{3,2,1,0:T(8,128)(2,1)}) custom-call(f32[1,16,2048]{2,1,0:T(8,128)S(1)} %reshape.18.bias_ref, bf16[8,2,2,128,128]{4,3,2,1,0:T(8,128)(2,1)S(1)} %all-to-all-done.1.qg_ref, bf16[8,2,2,128,128]{4,3,2,1,0:T(8,128)(2,1)S(1)} %all-to-all-done.own_ref, ...), custom_call_target="tpu_custom_call" | custom-call | flops 12000000000 | bytes 4194304 | tf_op jit(solution)/shard_map/pallas_call | solution.py:154
  56.6 9.2 %shard_map.96 = (bf16[8,2,2,128,128]{4,3,2,1,0:T(8,128)(2,1)}, bf16[8,2,2,128,128]{4,3,2,1,0:T(8,128)(2,1)}, bf16[8,2,128,128]{3,2,1,0:T(8,128)(2,1)S(1)}) custom-call(f32[1,16,2048]{2,1,0:T(8,128)S(1)} %reshape.18.bias_ref, bf16[8,2,2,128,128]{4,3,2,1,0:T(8,128)(2,1)S(1)} %all-to-all-done.1.qg_ref, ...), custom_call_target="tpu_custom_call", output_to_operand_aliasing={{0}: (4, {}), {1}: (5, {})} | custom-call | flops 12000000000 | bytes 4194304 | tf_op jit(solution)/shard_map/pallas_call | solution.py:154
  65.8 10.9 %all-to-all-start.2 = ((bf16[8,2,2,128,128]{4,3,2,1,0:T(8,128)(2,1)}), bf16[8,2,2,128,128]{4,3,2,1,0:T(8,128)(2,1)S(1)}, u32[]{:S(2)}, u32[]{:S(2)}) async-start(bf16[8,2,2,128,128]{4,3,2,1,0:T(8,128)(2,1)} %get-tuple-element.31), calls=%async_computation.2 | async-start | bytes 2097152 | tf_op jit(solution)/shard_map/all_to_all | solution.py:19
  76.7 1.3 %collective-permute-start.5 = (bf16[8,2,128,128]{3,2,1,0:T(8,128)(2,1)S(1)}, bf16[8,2,128,128]{3,2,1,0:T(8,128)(2,1)S(1)}, u32[]{:S(2)}, u32[]{:S(2)}) collective-permute-start(bf16[8,2,128,128]{3,2,1,0:T(8,128)(2,1)S(1)} %get-tuple-element.30), channel_id=1, source_target_pairs={{128,135},{160,167},{192,199},{224,231},{1,0},{33,32},{65,64},{97,... | collective-permute-start | bytes 1572872 | tf_op jit(solution)/shard_map/ppermute | solution.py:182
  78.0 1.3 %collective-permute-start.7 = (bf16[8,2,128,128]{3,2,1,0:T(8,128)(2,1)S(1)}, bf16[8,2,128,128]{3,2,1,0:T(8,128)(2,1)}, u32[]{:S(2)}, u32[]{:S(2)}) collective-permute-start(bf16[8,2,128,128]{3,2,1,0:T(8,128)(2,1)S(1)} %get-tuple-element.30), channel_id=1, source_target_pairs={{0,31},{32,63},{64,95},{96,127},{8,7},{40,39},{72,71},{104,103},{1... | collective-permute-start | bytes 1572872 | tf_op jit(solution)/shard_map/ppermute | solution.py:182
  79.3 0.2 collective-permute-done.5
  79.5 1.4 %collective-permute-start.6 = (bf16[8,2,128,128]{3,2,1,0:T(8,128)(2,1)S(1)}, bf16[8,2,128,128]{3,2,1,0:T(8,128)(2,1)}, u32[]{:S(2)}, u32[]{:S(2)}) collective-permute-start(bf16[8,2,128,128]{3,2,1,0:T(8,128)(2,1)S(1)} %collective-permute-done.5), channel_id=1, source_target_pairs={{135,159},{167,191},{199,223},{231,255},{143,135},{175,167},{207,1... | collective-permute-start | bytes 1572872 | tf_op jit(solution)/shard_map/ppermute | solution.py:182
  80.9 1.4 %copy.23 = bf16[8,2,2,128,128]{4,3,2,0,1:T(8,128)(2,1)S(1)} copy(bf16[8,2,2,128,128]{4,3,2,1,0:T(8,128)(2,1)} %get-tuple-element.26) | data formatting | bytes 2097152 | tf_op jit(solution)/shard_map/pallas_call | solution.py:154
  82.3 0.2 copy-done
  82.5 1.2 fusion.3
  83.8 1.0 copy.24
  84.8 6.9 %collective-permute-done.7 = bf16[8,2,128,128]{3,2,1,0:T(8,128)(2,1)} collective-permute-done((bf16[8,2,128,128]{3,2,1,0:T(8,128)(2,1)S(1)}, bf16[8,2,128,128]{3,2,1,0:T(8,128)(2,1)}, u32[]{:S(2)}, u32[]{:S(2)}) %collective-permute-start.7) | collective-permute-done | bytes 524320 | tf_op jit(solution)/shard_map/ppermute | solution.py:182
  91.7 2.2 %fusion.5 = bf16[8,2,2,128,128]{4,3,2,1,0:T(8,128)(2,1)} fusion(bf16[8,2,2,128,128]{4,3,2,1,0:T(8,128)(2,1)} %copy.24, bf16[8,2,2,128,128]{4,3,2,0,1:T(8,128)(2,1)S(1)} %fusion.3, bf16[8,2,128,128]{3,2,1,0:T(8,128)(2,1)S(1)} %collective-permute-done.5, bf16[8,2,128,128]{3,2,1,0:T(8,128)(2,1)} %collective-permute-done.6, ...), kind=kLoop, calls=%fused_computation.7 | loop fusion | flops 1572864 | bytes 2621442 | tf_op jit(solution)/shard_map/dynamic_update_slice | solution.py:228
  93.9 19.7 %all-to-all-start.3 = ((bf16[8,2,2,128,128]{4,3,2,1,0:T(8,128)(2,1)}), bf16[8,2,2,128,128]{4,3,2,1,0:T(8,128)(2,1)S(1)}, u32[]{:S(2)}, u32[]{:S(2)}) async-start(bf16[8,2,2,128,128]{4,3,2,1,0:T(8,128)(2,1)} %fusion.5), calls=%async_computation.3 | async-start | bytes 2097152 | tf_op jit(solution)/shard_map/all_to_all | solution.py:19
  113.6 1.6 %shard_map.97 = (bf16[128,2048]{1,0:T(8,128)(2,1)}, bf16[128,2048]{1,0:T(8,128)(2,1)}) custom-call(bf16[8,2,2,128,128]{4,3,2,1,0:T(8,128)(2,1)S(1)} %all-to-all-done.2.i_ref), custom_call_target="tpu_custom_call" | custom-call | tf_op jit(solution)/shard_map/pallas_call | solution.py:68
  115.2 7.8 %all-to-all-done.3.i_ref = bf16[8,2,2,128,128]{4,3,2,1,0:T(8,128)(2,1)S(1)} async-done(((bf16[8,2,2,128,128]{4,3,2,1,0:T(8,128)(2,1)}), bf16[8,2,2,128,128]{4,3,2,1,0:T(8,128)(2,1)S(1)}, u32[]{:S(2)}, u32[]{:S(2)}) %all-to-all-start.3) | async-done | bytes 1048608 | tf_op jit(solution)/shard_map/all_to_all | solution.py:19
  123.1 1.6 %shard_map.98 = (bf16[128,2048]{1,0:T(8,128)(2,1)}, bf16[128,2048]{1,0:T(8,128)(2,1)}) custom-call(bf16[8,2,2,128,128]{4,3,2,1,0:T(8,128)(2,1)S(1)} %all-to-all-done.3.i_ref), custom_call_target="tpu_custom_call" | custom-call | tf_op jit(solution)/shard_map/pallas_call | solution.py:68
  (15 shorter events, 0.4 us)
Async XLA Ops:
  3.0 20.5 %all-to-all-start = ((bf16[8,2,2,128,128]{4,3,2,1,0:T(8,128)(2,1)}), bf16[8,2,2,128,128]{4,3,2,1,0:T(8,128)(2,1)S(1)}, u32[]{:S(2)}, u32[]{:S(2)}) async-start(bf16[8,2,2,128,128]{4,3,2,1,0:T(8,128)(2,1)} %shard_map.93), calls=%async_computation | async-start | bytes 2097152 | tf_op jit(solution)/shard_map/all_to_all | solution.py:19
  24.5 22.7 %all-to-all-start.1 = ((bf16[8,2,2,128,128]{4,3,2,1,0:T(8,128)(2,1)}), bf16[8,2,2,128,128]{4,3,2,1,0:T(8,128)(2,1)S(1)}, u32[]{:S(2)}, u32[]{:S(2)}) async-start(bf16[8,2,2,128,128]{4,3,2,1,0:T(8,128)(2,1)} %shard_map.94), calls=%async_computation.1 | async-start | bytes 2097152 | tf_op jit(solution)/shard_map/all_to_all | solution.py:19
  28.2 8.7 %collective-permute-start.1 = (bf16[8,2,128,128]{3,2,1,0:T(8,128)(2,1)}, bf16[8,2,128,128]{3,2,1,0:T(8,128)(2,1)}, u32[]{:S(2)}, u32[]{:S(2)}) collective-permute-start(bf16[8,2,128,128]{3,2,1,0:T(8,128)(2,1)} %get-tuple-element.23), channel_id=1, source_target_pairs={{0,1},{32,33},{64,65},{96,97},{128,129},{160,161},{192,193},{224,2... | collective-permute-start | bytes 1572872 | tf_op jit(solution)/shard_map/ppermute | solution.py:182
  29.5 16.4 %collective-permute-start.3 = (bf16[8,2,128,128]{3,2,1,0:T(8,128)(2,1)}, bf16[8,2,128,128]{3,2,1,0:T(8,128)(2,1)}, u32[]{:S(2)}, u32[]{:S(2)}) collective-permute-start(bf16[8,2,128,128]{3,2,1,0:T(8,128)(2,1)} %get-tuple-element.23), channel_id=1, source_target_pairs={{7,8},{39,40},{71,72},{103,104},{15,16},{47,48},{79,80},{111,112},... | collective-permute-start | bytes 1572872 | tf_op jit(solution)/shard_map/ppermute | solution.py:182
  36.9 9.0 %collective-permute-start.2 = (bf16[8,2,128,128]{3,2,1,0:T(8,128)(2,1)}, bf16[8,2,128,128]{3,2,1,0:T(8,128)(2,1)}, u32[]{:S(2)}, u32[]{:S(2)}) collective-permute-start(bf16[8,2,128,128]{3,2,1,0:T(8,128)(2,1)} %collective-permute-done.1), channel_id=1, source_target_pairs={{128,136},{160,168},{192,200},{224,232},{136,144},{168,176},{200,2... | collective-permute-start | bytes 1572872 | tf_op jit(solution)/shard_map/ppermute | solution.py:182
  38.4 0.7 copy-start.1
  40.3 16.3 %collective-permute-start = (bf16[8,2,128,128]{3,2,1,0:T(8,128)(2,1)}, bf16[8,2,128,128]{3,2,1,0:T(8,128)(2,1)S(1)}, u32[]{:S(2)}, u32[]{:S(2)}) collective-permute-start(bf16[8,2,128,128]{3,2,1,0:T(8,128)(2,1)} %get-tuple-element.22), channel_id=1, source_target_pairs={{0,1},{1,2},{2,3},{3,4},{4,5},{5,6},{6,7},{7,8},{8,9},{9,10},{10,1... | collective-permute-start | bytes 1572872 | tf_op jit(solution)/shard_map/ppermute | solution.py:219
  56.6 20.1 %collective-permute-start.4 = (bf16[8,2,128,128]{3,2,1,0:T(8,128)(2,1)}, bf16[8,2,128,128]{3,2,1,0:T(8,128)(2,1)}, u32[]{:S(2)}, u32[]{:S(2)}) collective-permute-start(bf16[8,2,128,128]{3,2,1,0:T(8,128)(2,1)} %get-tuple-element.28), channel_id=1, source_target_pairs={{0,31},{1,0},{2,1},{3,2},{4,3},{5,4},{6,5},{7,6},{8,7},{9,8},{10,9... | collective-permute-start | bytes 1572872 | tf_op jit(solution)/shard_map/ppermute | solution.py:219
  65.8 28.1 %all-to-all-start.2 = ((bf16[8,2,2,128,128]{4,3,2,1,0:T(8,128)(2,1)}), bf16[8,2,2,128,128]{4,3,2,1,0:T(8,128)(2,1)S(1)}, u32[]{:S(2)}, u32[]{:S(2)}) async-start(bf16[8,2,2,128,128]{4,3,2,1,0:T(8,128)(2,1)} %get-tuple-element.31), calls=%async_computation.2 | async-start | bytes 2097152 | tf_op jit(solution)/shard_map/all_to_all | solution.py:19
  76.7 2.8 %collective-permute-start.5 = (bf16[8,2,128,128]{3,2,1,0:T(8,128)(2,1)S(1)}, bf16[8,2,128,128]{3,2,1,0:T(8,128)(2,1)S(1)}, u32[]{:S(2)}, u32[]{:S(2)}) collective-permute-start(bf16[8,2,128,128]{3,2,1,0:T(8,128)(2,1)S(1)} %get-tuple-element.30), channel_id=1, source_target_pairs={{128,135},{160,167},{192,199},{224,231},{1,0},{33,32},{65,64},{97,... | collective-permute-start | bytes 1572872 | tf_op jit(solution)/shard_map/ppermute | solution.py:182
  78.0 13.7 %collective-permute-start.7 = (bf16[8,2,128,128]{3,2,1,0:T(8,128)(2,1)S(1)}, bf16[8,2,128,128]{3,2,1,0:T(8,128)(2,1)}, u32[]{:S(2)}, u32[]{:S(2)}) collective-permute-start(bf16[8,2,128,128]{3,2,1,0:T(8,128)(2,1)S(1)} %get-tuple-element.30), channel_id=1, source_target_pairs={{0,31},{32,63},{64,95},{96,127},{8,7},{40,39},{72,71},{104,103},{1... | collective-permute-start | bytes 1572872 | tf_op jit(solution)/shard_map/ppermute | solution.py:182
  79.5 12.2 %collective-permute-start.6 = (bf16[8,2,128,128]{3,2,1,0:T(8,128)(2,1)S(1)}, bf16[8,2,128,128]{3,2,1,0:T(8,128)(2,1)}, u32[]{:S(2)}, u32[]{:S(2)}) collective-permute-start(bf16[8,2,128,128]{3,2,1,0:T(8,128)(2,1)S(1)} %collective-permute-done.5), channel_id=1, source_target_pairs={{135,159},{167,191},{199,223},{231,255},{143,135},{175,167},{207,1... | collective-permute-start | bytes 1572872 | tf_op jit(solution)/shard_map/ppermute | solution.py:182
  80.9 1.5 %copy-start = (bf16[8,2,2,128,128]{4,3,2,1,0:T(8,128)(2,1)S(1)}, bf16[8,2,2,128,128]{4,3,2,1,0:T(8,128)(2,1)}, u32[]{:S(2)}) copy-start(bf16[8,2,2,128,128]{4,3,2,1,0:T(8,128)(2,1)} %get-tuple-element.26) | copy-start | bytes 3145732
  93.9 29.1 %all-to-all-start.3 = ((bf16[8,2,2,128,128]{4,3,2,1,0:T(8,128)(2,1)}), bf16[8,2,2,128,128]{4,3,2,1,0:T(8,128)(2,1)S(1)}, u32[]{:S(2)}, u32[]{:S(2)}) async-start(bf16[8,2,2,128,128]{4,3,2,1,0:T(8,128)(2,1)} %fusion.5), calls=%async_computation.3 | async-start | bytes 2097152 | tf_op jit(solution)/shard_map/all_to_all | solution.py:19

commit v5 on v4

--- a/solution.py
+++ b/solution.py
@@ -40,8 +40,15 @@
 
 def pack(a, b, peers):
     rows, width = a.shape
-    shape = pltpu.HBM((peers, width // HEAD // peers, 2, rows, HEAD), a.dtype)
-    return pl.pallas_call(pack_kernel, out_shape=shape)(a, b)
+    heads = width // HEAD // peers
+    part = pl.BlockSpec((rows, width // 2), lambda i: (0, i))
+    return pl.pallas_call(
+        pack_kernel,
+        grid=(2,),
+        in_specs=[part, part],
+        out_specs=pl.BlockSpec((peers // 2, heads, 2, rows, HEAD), lambda i: (i, 0, 0, 0, 0)),
+        out_shape=pltpu.HBM((peers, heads, 2, rows, HEAD), a.dtype),
+    )(a, b)
 
 
 def unpack_kernel(i_ref, a_ref, b_ref, va, vb, come, go):
@@ -236,6 +243,7 @@
     kv = exchanged(pack(keys, values, peers))
     kv0, kv1, qg = lax.optimization_barrier((kv[:, 0], kv[:, 1], pack(queries, out_grad, peers)))
     near, finish = sent(kv0, 1, upper)
+    kv1, near = after(kv1, near)
     prev_kv1 = shifted(kv1, 1)
     qg = exchanged(qg)
     prev_kv0 = finish(near)

time: 126 us -> 125 us (level)
  no operation moved by 1% of the time
where the time goes in v5:
time: 125 us
  starting transfers between devices  54.1 us (43%)
  waiting for transfers between devices  33.3 us (27%)
  Pallas kernels  26 us (21%)
  other arithmetic  5.56 us (4%)
  local copies, waits for them, and re-layouts  4.77 us (4%)
    all_to_all x4, starting transfers between devices, exchanged(): lax.all_to_all(value, 'inner', split_axis=0, concat_axis=0, tiled=True)  39.8 us
    all_to_all x4, waiting for transfers between devices, exchanged(): lax.all_to_all(value, 'inner', split_axis=0, concat_axis=0, tiled=True)  20.6 us
    pallas_call x2, Pallas kernels, attention(): pl.pallas_call(attention_kernel, grid=(1,), in_specs=[pl.BlockSpec((1, wi...  18.6 us
    ppermute x6, starting transfers between devices, hop(): return lax.ppermute(value, ('inner', 'outer'), flat)  14.2 us
    ppermute x6, waiting for transfers between devices, hop(): return lax.ppermute(value, ('inner', 'outer'), flat)  12.6 us
    pallas_call x2, Pallas kernels, pack(): pl.pallas_call(pack_kernel, grid=(2,), in_specs=[part, part], out_specs=p...  4.23 us
    dynamic_update_slice x2, other arithmetic, add_at(): lax.dynamic_update_slice_in_dim(d, added(own, back)[:, None], head, axis=1)  3.42 us
    pallas_call x2, Pallas kernels, unpack(): pl.pallas_call(unpack_kernel, out_shape=(shape, shape), in_specs=[pl.Bloc...  3.21 us
  transfers between devices with their start and end apart: 12, of which 5 were waited for; matrix products, arithmetic and copies ran while one was open for 7% of the time, Pallas kernels for 18%

profile of v5, /device:TPU:7, one launch (start us, length us, event | category | flops | bytes accessed | tf_op | source)
XLA Modules:
  0.0 124.6 jit_solution(1221493767473924653)
XLA Ops:
  0.6 2.1 %shard_map.93 = bf16[8,2,2,128,128]{4,3,2,1,0:T(8,128)(2,1)} custom-call(bf16[128,2048]{1,0:T(8,128)(2,1)} %a_ref.2, bf16[128,2048]{1,0:T(8,128)(2,1)} %b_ref.2), custom_call_target="tpu_custom_call" | custom-call | tf_op jit(solution)/shard_map/pallas_call | solution.py:45
  2.7 5.5 %all-to-all-start = ((bf16[8,2,2,128,128]{4,3,2,1,0:T(8,128)(2,1)}), bf16[8,2,2,128,128]{4,3,2,1,0:T(8,128)(2,1)S(1)}, u32[]{:S(2)}, u32[]{:S(2)}) async-start(bf16[8,2,2,128,128]{4,3,2,1,0:T(8,128)(2,1)} %shard_map.93), calls=%async_computation | async-start | bytes 2097152 | tf_op jit(solution)/shard_map/all_to_all | solution.py:19
  8.3 2.1 %shard_map.94 = bf16[8,2,2,128,128]{4,3,2,1,0:T(8,128)(2,1)} custom-call(bf16[128,2048]{1,0:T(8,128)(2,1)} %a_ref.3, bf16[128,2048]{1,0:T(8,128)(2,1)} %b_ref.3), custom_call_target="tpu_custom_call" | custom-call | tf_op jit(solution)/shard_map/pallas_call | solution.py:45
  10.4 12.8 %all-to-all-done.own_ref = bf16[8,2,2,128,128]{4,3,2,1,0:T(8,128)(2,1)S(1)} async-done(((bf16[8,2,2,128,128]{4,3,2,1,0:T(8,128)(2,1)}), bf16[8,2,2,128,128]{4,3,2,1,0:T(8,128)(2,1)S(1)}, u32[]{:S(2)}, u32[]{:S(2)}) %all-to-all-start) | async-done | bytes 1048608 | tf_op jit(solution)/shard_map/all_to_all | solution.py:19
  23.2 1.1 slice_bitcast_fusion.2
  24.3 3.7 %all-to-all-start.1 = ((bf16[8,2,2,128,128]{4,3,2,1,0:T(8,128)(2,1)}), bf16[8,2,2,128,128]{4,3,2,1,0:T(8,128)(2,1)S(1)}, u32[]{:S(2)}, u32[]{:S(2)}) async-start(bf16[8,2,2,128,128]{4,3,2,1,0:T(8,128)(2,1)} %shard_map.94), calls=%async_computation.1 | async-start | bytes 2097152 | tf_op jit(solution)/shard_map/all_to_all | solution.py:19
  28.0 1.3 %collective-permute-start = (bf16[8,2,128,128]{3,2,1,0:T(8,128)(2,1)}, bf16[8,2,128,128]{3,2,1,0:T(8,128)(2,1)}, u32[]{:S(2)}, u32[]{:S(2)}) collective-permute-start(bf16[8,2,128,128]{3,2,1,0:T(8,128)(2,1)} %get-tuple-element.25), channel_id=1, source_target_pairs={{0,1},{32,33},{64,65},{96,97},{128,129},{160,161},{192,193},{224,2... | collective-permute-start | bytes 1572872 | tf_op jit(solution)/shard_map/ppermute | solution.py:189
  29.3 7.4 %collective-permute-start.3 = (bf16[8,2,128,128]{3,2,1,0:T(8,128)(2,1)}, bf16[8,2,128,128]{3,2,1,0:T(8,128)(2,1)}, u32[]{:S(2)}, u32[]{:S(2)}) collective-permute-start(bf16[8,2,128,128]{3,2,1,0:T(8,128)(2,1)} %get-tuple-element.25), channel_id=1, source_target_pairs={{7,8},{39,40},{71,72},{103,104},{15,16},{47,48},{79,80},{111,112},... | collective-permute-start | bytes 1572872 | tf_op jit(solution)/shard_map/ppermute | solution.py:189
  36.7 1.5 %collective-permute-start.2 = (bf16[8,2,128,128]{3,2,1,0:T(8,128)(2,1)}, bf16[8,2,128,128]{3,2,1,0:T(8,128)(2,1)}, u32[]{:S(2)}, u32[]{:S(2)}) collective-permute-start(bf16[8,2,128,128]{3,2,1,0:T(8,128)(2,1)} %collective-permute-done), channel_id=1, source_target_pairs={{128,136},{160,168},{192,200},{224,232},{136,144},{168,176},{200,2... | collective-permute-start | bytes 1572872 | tf_op jit(solution)/shard_map/ppermute | solution.py:189
  38.1 0.7 copy-done.1
  39.0 0.8 fusion.7
  39.8 0.1 broadcast_in_dim.24
  40.0 0.1 reshape.18.bias_ref
  40.2 5.5 %collective-permute-done.3 = bf16[8,2,128,128]{3,2,1,0:T(8,128)(2,1)} collective-permute-done((bf16[8,2,128,128]{3,2,1,0:T(8,128)(2,1)}, bf16[8,2,128,128]{3,2,1,0:T(8,128)(2,1)}, u32[]{:S(2)}, u32[]{:S(2)}) %collective-permute-start.3) | collective-permute-done | bytes 524320 | tf_op jit(solution)/shard_map/ppermute | solution.py:189
  45.7 1.3 %select_select_fusion.prev_ref = bf16[8,2,128,128]{3,2,1,0:T(8,128)(2,1)S(1)} fusion(bf16[8,2,128,128]{3,2,1,0:T(8,128)(2,1)} %collective-permute-done, bf16[8,2,128,128]{3,2,1,0:T(8,128)(2,1)} %collective-permute-done.2, bf16[8,2,128,128]{3,2,1,0:T(8,128)(2,1)} %collective-permute-done.3, pred[]{:T(512)S(6)} %and.22, pred[]{:T(512)S(6)} %eq.18), kind=kLoop, calls=%fused_computation.12 | loop fusion | flops 524288 | bytes 2097154 | tf_op jit(solution)/shard_map/jit(_where)/select_n | solution.py:219
  47.0 9.4 %shard_map.95 = (bf16[8,2,2,128,128]{4,3,2,1,0:T(8,128)(2,1)}, bf16[8,2,2,128,128]{4,3,2,1,0:T(8,128)(2,1)}, bf16[8,2,128,128]{3,2,1,0:T(8,128)(2,1)}) custom-call(f32[1,16,2048]{2,1,0:T(8,128)S(1)} %reshape.18.bias_ref, bf16[8,2,2,128,128]{4,3,2,1,0:T(8,128)(2,1)S(1)} %all-to-all-done.1.qg_ref, bf16[8,2,2,128,128]{4,3,2,1,0:T(8,128)(2,1)S(1)} %all-to-all-done.own_ref, ...), custom_call_target="tpu_custom_call" | custom-call | flops 12000000000 | bytes 4194304 | tf_op jit(solution)/shard_map/pallas_call | solution.py:161
  56.4 9.2 %shard_map.96 = (bf16[8,2,2,128,128]{4,3,2,1,0:T(8,128)(2,1)}, bf16[8,2,2,128,128]{4,3,2,1,0:T(8,128)(2,1)}, bf16[8,2,128,128]{3,2,1,0:T(8,128)(2,1)S(1)}) custom-call(f32[1,16,2048]{2,1,0:T(8,128)S(1)} %reshape.18.bias_ref, bf16[8,2,2,128,128]{4,3,2,1,0:T(8,128)(2,1)S(1)} %all-to-all-done.1.qg_ref, ...), custom_call_target="tpu_custom_call", output_to_operand_aliasing={{0}: (4, {}), {1}: (5, {})} | custom-call | flops 12000000000 | bytes 4194304 | tf_op jit(solution)/shard_map/pallas_call | solution.py:161
  65.6 10.8 %all-to-all-start.2 = ((bf16[8,2,2,128,128]{4,3,2,1,0:T(8,128)(2,1)}), bf16[8,2,2,128,128]{4,3,2,1,0:T(8,128)(2,1)S(1)}, u32[]{:S(2)}, u32[]{:S(2)}) async-start(bf16[8,2,2,128,128]{4,3,2,1,0:T(8,128)(2,1)} %get-tuple-element.35), calls=%async_computation.2 | async-start | bytes 2097152 | tf_op jit(solution)/shard_map/all_to_all | solution.py:19
  76.4 1.3 %collective-permute-start.5 = (bf16[8,2,128,128]{3,2,1,0:T(8,128)(2,1)S(1)}, bf16[8,2,128,128]{3,2,1,0:T(8,128)(2,1)S(1)}, u32[]{:S(2)}, u32[]{:S(2)}) collective-permute-start(bf16[8,2,128,128]{3,2,1,0:T(8,128)(2,1)S(1)} %get-tuple-element.34), channel_id=1, source_target_pairs={{128,135},{160,167},{192,199},{224,231},{1,0},{33,32},{65,64},{97,... | collective-permute-start | bytes 1572872 | tf_op jit(solution)/shard_map/ppermute | solution.py:189
  77.8 1.3 %collective-permute-start.7 = (bf16[8,2,128,128]{3,2,1,0:T(8,128)(2,1)S(1)}, bf16[8,2,128,128]{3,2,1,0:T(8,128)(2,1)}, u32[]{:S(2)}, u32[]{:S(2)}) collective-permute-start(bf16[8,2,128,128]{3,2,1,0:T(8,128)(2,1)S(1)} %get-tuple-element.34), channel_id=1, source_target_pairs={{0,31},{32,63},{64,95},{96,127},{8,7},{40,39},{72,71},{104,103},{1... | collective-permute-start | bytes 1572872 | tf_op jit(solution)/shard_map/ppermute | solution.py:189
  79.1 0.2 collective-permute-done.5
  79.3 1.4 %collective-permute-start.6 = (bf16[8,2,128,128]{3,2,1,0:T(8,128)(2,1)S(1)}, bf16[8,2,128,128]{3,2,1,0:T(8,128)(2,1)}, u32[]{:S(2)}, u32[]{:S(2)}) collective-permute-start(bf16[8,2,128,128]{3,2,1,0:T(8,128)(2,1)S(1)} %collective-permute-done.5), channel_id=1, source_target_pairs={{135,159},{167,191},{199,223},{231,255},{143,135},{175,167},{207,1... | collective-permute-start | bytes 1572872 | tf_op jit(solution)/shard_map/ppermute | solution.py:189
  80.7 1.4 %copy.23 = bf16[8,2,2,128,128]{4,3,2,0,1:T(8,128)(2,1)S(1)} copy(bf16[8,2,2,128,128]{4,3,2,1,0:T(8,128)(2,1)} %get-tuple-element.30) | data formatting | bytes 2097152 | tf_op jit(solution)/shard_map/pallas_call | solution.py:161
  82.1 0.2 copy-done
  82.3 1.2 fusion.3
  83.5 1.0 copy.24
  84.6 6.9 %collective-permute-done.7 = bf16[8,2,128,128]{3,2,1,0:T(8,128)(2,1)} collective-permute-done((bf16[8,2,128,128]{3,2,1,0:T(8,128)(2,1)S(1)}, bf16[8,2,128,128]{3,2,1,0:T(8,128)(2,1)}, u32[]{:S(2)}, u32[]{:S(2)}) %collective-permute-start.7) | collective-permute-done | bytes 524320 | tf_op jit(solution)/shard_map/ppermute | solution.py:189
  91.5 2.2 %fusion.5 = bf16[8,2,2,128,128]{4,3,2,1,0:T(8,128)(2,1)} fusion(bf16[8,2,2,128,128]{4,3,2,1,0:T(8,128)(2,1)} %copy.24, bf16[8,2,2,128,128]{4,3,2,0,1:T(8,128)(2,1)S(1)} %fusion.3, bf16[8,2,128,128]{3,2,1,0:T(8,128)(2,1)S(1)} %collective-permute-done.5, bf16[8,2,128,128]{3,2,1,0:T(8,128)(2,1)} %collective-permute-done.6, ...), kind=kLoop, calls=%fused_computation.7 | loop fusion | flops 1572864 | bytes 2621442 | tf_op jit(solution)/shard_map/dynamic_update_slice | solution.py:235
  93.7 19.7 %all-to-all-start.3 = ((bf16[8,2,2,128,128]{4,3,2,1,0:T(8,128)(2,1)}), bf16[8,2,2,128,128]{4,3,2,1,0:T(8,128)(2,1)S(1)}, u32[]{:S(2)}, u32[]{:S(2)}) async-start(bf16[8,2,2,128,128]{4,3,2,1,0:T(8,128)(2,1)} %fusion.5), calls=%async_computation.3 | async-start | bytes 2097152 | tf_op jit(solution)/shard_map/all_to_all | solution.py:19
  113.4 1.6 %shard_map.97 = (bf16[128,2048]{1,0:T(8,128)(2,1)}, bf16[128,2048]{1,0:T(8,128)(2,1)}) custom-call(bf16[8,2,2,128,128]{4,3,2,1,0:T(8,128)(2,1)S(1)} %all-to-all-done.2.i_ref), custom_call_target="tpu_custom_call" | custom-call | tf_op jit(solution)/shard_map/pallas_call | solution.py:75
  115.0 7.8 %all-to-all-done.3.i_ref = bf16[8,2,2,128,128]{4,3,2,1,0:T(8,128)(2,1)S(1)} async-done(((bf16[8,2,2,128,128]{4,3,2,1,0:T(8,128)(2,1)}), bf16[8,2,2,128,128]{4,3,2,1,0:T(8,128)(2,1)S(1)}, u32[]{:S(2)}, u32[]{:S(2)}) %all-to-all-start.3) | async-done | bytes 1048608 | tf_op jit(solution)/shard_map/all_to_all | solution.py:19
  122.8 1.6 %shard_map.98 = (bf16[128,2048]{1,0:T(8,128)(2,1)}, bf16[128,2048]{1,0:T(8,128)(2,1)}) custom-call(bf16[8,2,2,128,128]{4,3,2,1,0:T(8,128)(2,1)S(1)} %all-to-all-done.3.i_ref), custom_call_target="tpu_custom_call" | custom-call | tf_op jit(solution)/shard_map/pallas_call | solution.py:75
  (15 shorter events, 0.4 us)
Async XLA Ops:
  2.7 20.5 %all-to-all-start = ((bf16[8,2,2,128,128]{4,3,2,1,0:T(8,128)(2,1)}), bf16[8,2,2,128,128]{4,3,2,1,0:T(8,128)(2,1)S(1)}, u32[]{:S(2)}, u32[]{:S(2)}) async-start(bf16[8,2,2,128,128]{4,3,2,1,0:T(8,128)(2,1)} %shard_map.93), calls=%async_computation | async-start | bytes 2097152 | tf_op jit(solution)/shard_map/all_to_all | solution.py:19
  24.3 22.7 %all-to-all-start.1 = ((bf16[8,2,2,128,128]{4,3,2,1,0:T(8,128)(2,1)}), bf16[8,2,2,128,128]{4,3,2,1,0:T(8,128)(2,1)S(1)}, u32[]{:S(2)}, u32[]{:S(2)}) async-start(bf16[8,2,2,128,128]{4,3,2,1,0:T(8,128)(2,1)} %shard_map.94), calls=%async_computation.1 | async-start | bytes 2097152 | tf_op jit(solution)/shard_map/all_to_all | solution.py:19
  28.0 8.7 %collective-permute-start = (bf16[8,2,128,128]{3,2,1,0:T(8,128)(2,1)}, bf16[8,2,128,128]{3,2,1,0:T(8,128)(2,1)}, u32[]{:S(2)}, u32[]{:S(2)}) collective-permute-start(bf16[8,2,128,128]{3,2,1,0:T(8,128)(2,1)} %get-tuple-element.25), channel_id=1, source_target_pairs={{0,1},{32,33},{64,65},{96,97},{128,129},{160,161},{192,193},{224,2... | collective-permute-start | bytes 1572872 | tf_op jit(solution)/shard_map/ppermute | solution.py:189
  29.3 16.4 %collective-permute-start.3 = (bf16[8,2,128,128]{3,2,1,0:T(8,128)(2,1)}, bf16[8,2,128,128]{3,2,1,0:T(8,128)(2,1)}, u32[]{:S(2)}, u32[]{:S(2)}) collective-permute-start(bf16[8,2,128,128]{3,2,1,0:T(8,128)(2,1)} %get-tuple-element.25), channel_id=1, source_target_pairs={{7,8},{39,40},{71,72},{103,104},{15,16},{47,48},{79,80},{111,112},... | collective-permute-start | bytes 1572872 | tf_op jit(solution)/shard_map/ppermute | solution.py:189
  36.7 9.0 %collective-permute-start.2 = (bf16[8,2,128,128]{3,2,1,0:T(8,128)(2,1)}, bf16[8,2,128,128]{3,2,1,0:T(8,128)(2,1)}, u32[]{:S(2)}, u32[]{:S(2)}) collective-permute-start(bf16[8,2,128,128]{3,2,1,0:T(8,128)(2,1)} %collective-permute-done), channel_id=1, source_target_pairs={{128,136},{160,168},{192,200},{224,232},{136,144},{168,176},{200,2... | collective-permute-start | bytes 1572872 | tf_op jit(solution)/shard_map/ppermute | solution.py:189
  38.1 0.7 copy-start.1
  40.1 16.3 %collective-permute-start.1 = (bf16[8,2,128,128]{3,2,1,0:T(8,128)(2,1)}, bf16[8,2,128,128]{3,2,1,0:T(8,128)(2,1)S(1)}, u32[]{:S(2)}, u32[]{:S(2)}) collective-permute-start(bf16[8,2,128,128]{3,2,1,0:T(8,128)(2,1)} %get-tuple-element.26), channel_id=1, source_target_pairs={{0,1},{1,2},{2,3},{3,4},{4,5},{5,6},{6,7},{7,8},{8,9},{9,10},{10,1... | collective-permute-start | bytes 1572872 | tf_op jit(solution)/shard_map/ppermute | solution.py:226
  56.4 20.1 %collective-permute-start.4 = (bf16[8,2,128,128]{3,2,1,0:T(8,128)(2,1)}, bf16[8,2,128,128]{3,2,1,0:T(8,128)(2,1)}, u32[]{:S(2)}, u32[]{:S(2)}) collective-permute-start(bf16[8,2,128,128]{3,2,1,0:T(8,128)(2,1)} %get-tuple-element.32), channel_id=1, source_target_pairs={{0,31},{1,0},{2,1},{3,2},{4,3},{5,4},{6,5},{7,6},{8,7},{9,8},{10,9... | collective-permute-start | bytes 1572872 | tf_op jit(solution)/shard_map/ppermute | solution.py:226
  65.6 28.1 %all-to-all-start.2 = ((bf16[8,2,2,128,128]{4,3,2,1,0:T(8,128)(2,1)}), bf16[8,2,2,128,128]{4,3,2,1,0:T(8,128)(2,1)S(1)}, u32[]{:S(2)}, u32[]{:S(2)}) async-start(bf16[8,2,2,128,128]{4,3,2,1,0:T(8,128)(2,1)} %get-tuple-element.35), calls=%async_computation.2 | async-start | bytes 2097152 | tf_op jit(solution)/shard_map/all_to_all | solution.py:19
  76.4 2.8 %collective-permute-start.5 = (bf16[8,2,128,128]{3,2,1,0:T(8,128)(2,1)S(1)}, bf16[8,2,128,128]{3,2,1,0:T(8,128)(2,1)S(1)}, u32[]{:S(2)}, u32[]{:S(2)}) collective-permute-start(bf16[8,2,128,128]{3,2,1,0:T(8,128)(2,1)S(1)} %get-tuple-element.34), channel_id=1, source_target_pairs={{128,135},{160,167},{192,199},{224,231},{1,0},{33,32},{65,64},{97,... | collective-permute-start | bytes 1572872 | tf_op jit(solution)/shard_map/ppermute | solution.py:189
  77.8 13.7 %collective-permute-start.7 = (bf16[8,2,128,128]{3,2,1,0:T(8,128)(2,1)S(1)}, bf16[8,2,128,128]{3,2,1,0:T(8,128)(2,1)}, u32[]{:S(2)}, u32[]{:S(2)}) collective-permute-start(bf16[8,2,128,128]{3,2,1,0:T(8,128)(2,1)S(1)} %get-tuple-element.34), channel_id=1, source_target_pairs={{0,31},{32,63},{64,95},{96,127},{8,7},{40,39},{72,71},{104,103},{1... | collective-permute-start | bytes 1572872 | tf_op jit(solution)/shard_map/ppermute | solution.py:189
  79.3 12.2 %collective-permute-start.6 = (bf16[8,2,128,128]{3,2,1,0:T(8,128)(2,1)S(1)}, bf16[8,2,128,128]{3,2,1,0:T(8,128)(2,1)}, u32[]{:S(2)}, u32[]{:S(2)}) collective-permute-start(bf16[8,2,128,128]{3,2,1,0:T(8,128)(2,1)S(1)} %collective-permute-done.5), channel_id=1, source_target_pairs={{135,159},{167,191},{199,223},{231,255},{143,135},{175,167},{207,1... | collective-permute-start | bytes 1572872 | tf_op jit(solution)/shard_map/ppermute | solution.py:189
  80.7 1.5 %copy-start = (bf16[8,2,2,128,128]{4,3,2,1,0:T(8,128)(2,1)S(1)}, bf16[8,2,2,128,128]{4,3,2,1,0:T(8,128)(2,1)}, u32[]{:S(2)}) copy-start(bf16[8,2,2,128,128]{4,3,2,1,0:T(8,128)(2,1)} %get-tuple-element.30) | copy-start | bytes 3145732
  93.7 29.1 %all-to-all-start.3 = ((bf16[8,2,2,128,128]{4,3,2,1,0:T(8,128)(2,1)}), bf16[8,2,2,128,128]{4,3,2,1,0:T(8,128)(2,1)S(1)}, u32[]{:S(2)}, u32[]{:S(2)}) async-start(bf16[8,2,2,128,128]{4,3,2,1,0:T(8,128)(2,1)} %fusion.5), calls=%async_computation.3 | async-start | bytes 2097152 | tf_op jit(solution)/shard_map/all_to_all | solution.py:19

commit v6 on v5

--- a/solution.py
+++ b/solution.py
@@ -82,7 +82,7 @@
     )(packed)
 
 
-def attend(bias_ref, qg_ref, keys, vals, put, acc_k, acc_v, s_ref, dp_ref):
+def attend(bias_ref, qg_ref, keys, vals, put, acc_k, acc_v, s_ref, dp_ref, p_ref):
     span = keys[0].shape[0]
     rows = qg_ref.shape[3]
     per = TILE // rows
@@ -103,39 +103,44 @@
                 parts = (s[:, : own.start], s[:, own] + later, s[:, own.stop :])
                 s = jnp.concatenate([part for part in parts if part.shape[1]], axis=1)
             s_ref[tile % 2, :, cols] = s
-            dp_ref[tile % 2, :, cols] = dot_t(g, vals[half])
+            dp_ref[tile % 3, :, cols] = dot_t(g, vals[half])
         return q, g
 
-    def finish(tile, q, g):
+    def soften(tile):
         s = s_ref[tile % 2]
         top = jnp.max(s, axis=1, keepdims=True)
         e = jnp.exp2(s - top)
         total = jnp.sum(e, axis=1, keepdims=True)
-        p = e * (1.0 / total)
+        p_ref[tile % 2] = e * (1.0 / total)
+
+    def finish(tile, q, g):
+        p = p_ref[tile % 2]
         pb = p.astype(jnp.bfloat16)
         out = (dot(pb[:, halves[0]], vals[0]) + dot(pb[:, halves[1]], vals[1])).astype(jnp.bfloat16)
         delta = jnp.sum(g.astype(jnp.float32) * out.astype(jnp.float32), axis=1, keepdims=True)
         dq = jnp.zeros((TILE, HEAD), jnp.float32)
         qt, gt = q.T, g.T
         for half, cols in enumerate(halves):
-            ds = (p[:, cols] * (dp_ref[tile % 2, :, cols] - delta)).astype(jnp.bfloat16)
+            ds = (p[:, cols] * (dp_ref[tile % 3, :, cols] - delta)).astype(jnp.bfloat16)
             dq = dq + dot(ds, keys[half])
             for acc, term in ((acc_k, dot(qt, ds)), (acc_v, dot(gt, pb[:, cols]))):
                 acc[:, cols] = term if tile == 0 else acc[:, cols] + term
         put(slice(tile * per, (tile + 1) * per), out, (dq * SCALE).astype(jnp.bfloat16))
 
     tiles = span // TILE
-    after = scores(0)
-    for tile in range(tiles):
-        now = after
-        if tile + 1 < tiles:
-            after = scores(tile + 1)
-        finish(tile, *now)
+    rows_of = {}
+    for step in range(tiles + 2):
+        if step < tiles:
+            rows_of[step] = scores(step)
+        if 0 <= step - 1 < tiles:
+            soften(step - 1)
+        if 0 <= step - 2 < tiles:
+            finish(step - 2, *rows_of[step - 2])
 
 
 def attention_kernel(bias_ref, qg_ref, own_ref, prev_ref, *rest):
-    oq_ref, d_ref, back_ref = rest[-7:-4]
-    scratch = rest[-4:]
+    oq_ref, d_ref, back_ref = rest[-8:-5]
+    scratch = rest[-5:]
     peers, _, rows, _ = prev_ref.shape
 
     def put(blocks, out, dq):
@@ -166,7 +171,7 @@
         out_specs=(slot, slot, whole),
         out_shape=(both, both, jax.ShapeDtypeStruct(prev.shape, prev.dtype)),
         input_output_aliases={4 + n: n for n in range(len(held))},
-        scratch_shapes=[pltpu.VMEM((HEAD, width), jnp.float32)] * 2 + [pltpu.VMEM((2, TILE, width), jnp.float32)] * 2,
+        scratch_shapes=[pltpu.VMEM((HEAD, width), jnp.float32)] * 2 + [pltpu.VMEM((n, TILE, width), jnp.float32) for n in (2, 3, 2)],
         compiler_params=pltpu.CompilerParams(vmem_limit_bytes=48 * 2**20),
         cost_estimate=pl.CostEstimate(flops=12 * 10**9, bytes_accessed=4 * 2**20, transcendentals=2 * 2**20),
     )(bias, qg, own, prev, *held)

time: 125 us -> 125 us (level)
  no operation moved by 1% of the time
where the time goes in v6:
time: 125 us; the launch traced here: 124 us
  starting transfers between devices  54.1 us (43%)
  waiting for transfers between devices  33.3 us (27%)
  Pallas kernels  25.8 us (21%)
  other arithmetic  5.56 us (4%)
  local copies, waits for them, and re-layouts  4.77 us (4%)
    all_to_all x4, starting transfers between devices, exchanged(): lax.all_to_all(value, 'inner', split_axis=0, concat_axis=0, tiled=True)  39.8 us
    all_to_all x4, waiting for transfers between devices, exchanged(): lax.all_to_all(value, 'inner', split_axis=0, concat_axis=0, tiled=True)  20.6 us
    pallas_call x2, Pallas kernels, attention(): pl.pallas_call(attention_kernel, grid=(1,), in_specs=[pl.BlockSpec((1, wi...  18.4 us
    ppermute x6, starting transfers between devices, hop(): return lax.ppermute(value, ('inner', 'outer'), flat)  14.2 us
    ppermute x6, waiting for transfers between devices, hop(): return lax.ppermute(value, ('inner', 'outer'), flat)  12.6 us
    pallas_call x2, Pallas kernels, pack(): pl.pallas_call(pack_kernel, grid=(2,), in_specs=[part, part], out_specs=p...  4.23 us
    dynamic_update_slice x2, other arithmetic, add_at(): lax.dynamic_update_slice_in_dim(d, added(own, back)[:, None], head, axis=1)  3.42 us
    pallas_call x2, Pallas kernels, unpack(): pl.pallas_call(unpack_kernel, out_shape=(shape, shape), in_specs=[pl.Bloc...  3.21 us
  transfers between devices with their start and end apart: 12, of which 5 were waited for; matrix products, arithmetic and copies ran while one was open for 7% of the time, Pallas kernels for 18%

profile of v6, /device:TPU:7, one launch (start us, length us, event | category | flops | bytes accessed | tf_op | source)
XLA Modules:
  0.0 124.4 jit_solution(14214041945492568691)
XLA Ops:
  0.6 2.1 %shard_map.93 = bf16[8,2,2,128,128]{4,3,2,1,0:T(8,128)(2,1)} custom-call(bf16[128,2048]{1,0:T(8,128)(2,1)} %a_ref.2, bf16[128,2048]{1,0:T(8,128)(2,1)} %b_ref.2), custom_call_target="tpu_custom_call" | custom-call | tf_op jit(solution)/shard_map/pallas_call | solution.py:45
  2.7 5.5 %all-to-all-start = ((bf16[8,2,2,128,128]{4,3,2,1,0:T(8,128)(2,1)}), bf16[8,2,2,128,128]{4,3,2,1,0:T(8,128)(2,1)S(1)}, u32[]{:S(2)}, u32[]{:S(2)}) async-start(bf16[8,2,2,128,128]{4,3,2,1,0:T(8,128)(2,1)} %shard_map.93), calls=%async_computation | async-start | bytes 2097152 | tf_op jit(solution)/shard_map/all_to_all | solution.py:19
  8.3 2.1 %shard_map.94 = bf16[8,2,2,128,128]{4,3,2,1,0:T(8,128)(2,1)} custom-call(bf16[128,2048]{1,0:T(8,128)(2,1)} %a_ref.3, bf16[128,2048]{1,0:T(8,128)(2,1)} %b_ref.3), custom_call_target="tpu_custom_call" | custom-call | tf_op jit(solution)/shard_map/pallas_call | solution.py:45
  10.4 12.8 %all-to-all-done.own_ref = bf16[8,2,2,128,128]{4,3,2,1,0:T(8,128)(2,1)S(1)} async-done(((bf16[8,2,2,128,128]{4,3,2,1,0:T(8,128)(2,1)}), bf16[8,2,2,128,128]{4,3,2,1,0:T(8,128)(2,1)S(1)}, u32[]{:S(2)}, u32[]{:S(2)}) %all-to-all-start) | async-done | bytes 1048608 | tf_op jit(solution)/shard_map/all_to_all | solution.py:19
  23.2 1.1 slice_bitcast_fusion.2
  24.3 3.7 %all-to-all-start.1 = ((bf16[8,2,2,128,128]{4,3,2,1,0:T(8,128)(2,1)}), bf16[8,2,2,128,128]{4,3,2,1,0:T(8,128)(2,1)S(1)}, u32[]{:S(2)}, u32[]{:S(2)}) async-start(bf16[8,2,2,128,128]{4,3,2,1,0:T(8,128)(2,1)} %shard_map.94), calls=%async_computation.1 | async-start | bytes 2097152 | tf_op jit(solution)/shard_map/all_to_all | solution.py:19
  28.0 1.3 %collective-permute-start = (bf16[8,2,128,128]{3,2,1,0:T(8,128)(2,1)}, bf16[8,2,128,128]{3,2,1,0:T(8,128)(2,1)}, u32[]{:S(2)}, u32[]{:S(2)}) collective-permute-start(bf16[8,2,128,128]{3,2,1,0:T(8,128)(2,1)} %get-tuple-element.25), channel_id=1, source_target_pairs={{0,1},{32,33},{64,65},{96,97},{128,129},{160,161},{192,193},{224,2... | collective-permute-start | bytes 1572872 | tf_op jit(solution)/shard_map/ppermute | solution.py:194
  29.3 7.4 %collective-permute-start.3 = (bf16[8,2,128,128]{3,2,1,0:T(8,128)(2,1)}, bf16[8,2,128,128]{3,2,1,0:T(8,128)(2,1)}, u32[]{:S(2)}, u32[]{:S(2)}) collective-permute-start(bf16[8,2,128,128]{3,2,1,0:T(8,128)(2,1)} %get-tuple-element.25), channel_id=1, source_target_pairs={{7,8},{39,40},{71,72},{103,104},{15,16},{47,48},{79,80},{111,112},... | collective-permute-start | bytes 1572872 | tf_op jit(solution)/shard_map/ppermute | solution.py:194
  36.7 1.5 %collective-permute-start.2 = (bf16[8,2,128,128]{3,2,1,0:T(8,128)(2,1)}, bf16[8,2,128,128]{3,2,1,0:T(8,128)(2,1)}, u32[]{:S(2)}, u32[]{:S(2)}) collective-permute-start(bf16[8,2,128,128]{3,2,1,0:T(8,128)(2,1)} %collective-permute-done), channel_id=1, source_target_pairs={{128,136},{160,168},{192,200},{224,232},{136,144},{168,176},{200,2... | collective-permute-start | bytes 1572872 | tf_op jit(solution)/shard_map/ppermute | solution.py:194
  38.1 0.7 copy-done.1
  39.0 0.8 fusion.7
  39.8 0.1 broadcast_in_dim.24
  40.0 0.1 reshape.18.bias_ref
  40.2 5.5 %collective-permute-done.3 = bf16[8,2,128,128]{3,2,1,0:T(8,128)(2,1)} collective-permute-done((bf16[8,2,128,128]{3,2,1,0:T(8,128)(2,1)}, bf16[8,2,128,128]{3,2,1,0:T(8,128)(2,1)}, u32[]{:S(2)}, u32[]{:S(2)}) %collective-permute-start.3) | collective-permute-done | bytes 524320 | tf_op jit(solution)/shard_map/ppermute | solution.py:194
  45.7 1.3 %select_select_fusion.prev_ref = bf16[8,2,128,128]{3,2,1,0:T(8,128)(2,1)S(1)} fusion(bf16[8,2,128,128]{3,2,1,0:T(8,128)(2,1)} %collective-permute-done, bf16[8,2,128,128]{3,2,1,0:T(8,128)(2,1)} %collective-permute-done.2, bf16[8,2,128,128]{3,2,1,0:T(8,128)(2,1)} %collective-permute-done.3, pred[]{:T(512)S(6)} %and.22, pred[]{:T(512)S(6)} %eq.18), kind=kLoop, calls=%fused_computation.12 | loop fusion | flops 524288 | bytes 2097154 | tf_op jit(solution)/shard_map/jit(_where)/select_n | solution.py:224
  47.0 9.2 %shard_map.95 = (bf16[8,2,2,128,128]{4,3,2,1,0:T(8,128)(2,1)}, bf16[8,2,2,128,128]{4,3,2,1,0:T(8,128)(2,1)}, bf16[8,2,128,128]{3,2,1,0:T(8,128)(2,1)}) custom-call(f32[1,16,2048]{2,1,0:T(8,128)S(1)} %reshape.18.bias_ref, bf16[8,2,2,128,128]{4,3,2,1,0:T(8,128)(2,1)S(1)} %all-to-all-done.1.qg_ref, bf16[8,2,2,128,128]{4,3,2,1,0:T(8,128)(2,1)S(1)} %all-to-all-done.own_ref, ...), custom_call_target="tpu_custom_call" | custom-call | flops 12000000000 | bytes 4194304 | tf_op jit(solution)/shard_map/pallas_call | solution.py:166
  56.2 9.1 %shard_map.96 = (bf16[8,2,2,128,128]{4,3,2,1,0:T(8,128)(2,1)}, bf16[8,2,2,128,128]{4,3,2,1,0:T(8,128)(2,1)}, bf16[8,2,128,128]{3,2,1,0:T(8,128)(2,1)S(1)}) custom-call(f32[1,16,2048]{2,1,0:T(8,128)S(1)} %reshape.18.bias_ref, bf16[8,2,2,128,128]{4,3,2,1,0:T(8,128)(2,1)S(1)} %all-to-all-done.1.qg_ref, ...), custom_call_target="tpu_custom_call", output_to_operand_aliasing={{0}: (4, {}), {1}: (5, {})} | custom-call | flops 12000000000 | bytes 4194304 | tf_op jit(solution)/shard_map/pallas_call | solution.py:166
  65.4 10.8 %all-to-all-start.2 = ((bf16[8,2,2,128,128]{4,3,2,1,0:T(8,128)(2,1)}), bf16[8,2,2,128,128]{4,3,2,1,0:T(8,128)(2,1)S(1)}, u32[]{:S(2)}, u32[]{:S(2)}) async-start(bf16[8,2,2,128,128]{4,3,2,1,0:T(8,128)(2,1)} %get-tuple-element.35), calls=%async_computation.2 | async-start | bytes 2097152 | tf_op jit(solution)/shard_map/all_to_all | solution.py:19
  76.2 1.3 %collective-permute-start.5 = (bf16[8,2,128,128]{3,2,1,0:T(8,128)(2,1)S(1)}, bf16[8,2,128,128]{3,2,1,0:T(8,128)(2,1)S(1)}, u32[]{:S(2)}, u32[]{:S(2)}) collective-permute-start(bf16[8,2,128,128]{3,2,1,0:T(8,128)(2,1)S(1)} %get-tuple-element.34), channel_id=1, source_target_pairs={{128,135},{160,167},{192,199},{224,231},{1,0},{33,32},{65,64},{97,... | collective-permute-start | bytes 1572872 | tf_op jit(solution)/shard_map/ppermute | solution.py:194
  77.6 1.3 %collective-permute-start.7 = (bf16[8,2,128,128]{3,2,1,0:T(8,128)(2,1)S(1)}, bf16[8,2,128,128]{3,2,1,0:T(8,128)(2,1)}, u32[]{:S(2)}, u32[]{:S(2)}) collective-permute-start(bf16[8,2,128,128]{3,2,1,0:T(8,128)(2,1)S(1)} %get-tuple-element.34), channel_id=1, source_target_pairs={{0,31},{32,63},{64,95},{96,127},{8,7},{40,39},{72,71},{104,103},{1... | collective-permute-start | bytes 1572872 | tf_op jit(solution)/shard_map/ppermute | solution.py:194
  78.9 0.2 collective-permute-done.5
  79.0 1.4 %collective-permute-start.6 = (bf16[8,2,128,128]{3,2,1,0:T(8,128)(2,1)S(1)}, bf16[8,2,128,128]{3,2,1,0:T(8,128)(2,1)}, u32[]{:S(2)}, u32[]{:S(2)}) collective-permute-start(bf16[8,2,128,128]{3,2,1,0:T(8,128)(2,1)S(1)} %collective-permute-done.5), channel_id=1, source_target_pairs={{135,159},{167,191},{199,223},{231,255},{143,135},{175,167},{207,1... | collective-permute-start | bytes 1572872 | tf_op jit(solution)/shard_map/ppermute | solution.py:194
  80.5 1.4 %copy.23 = bf16[8,2,2,128,128]{4,3,2,0,1:T(8,128)(2,1)S(1)} copy(bf16[8,2,2,128,128]{4,3,2,1,0:T(8,128)(2,1)} %get-tuple-element.30) | data formatting | bytes 2097152 | tf_op jit(solution)/shard_map/pallas_call | solution.py:166
  81.9 0.2 copy-done
  82.1 1.2 fusion.3
  83.3 1.0 copy.24
  84.3 6.9 %collective-permute-done.7 = bf16[8,2,128,128]{3,2,1,0:T(8,128)(2,1)} collective-permute-done((bf16[8,2,128,128]{3,2,1,0:T(8,128)(2,1)S(1)}, bf16[8,2,128,128]{3,2,1,0:T(8,128)(2,1)}, u32[]{:S(2)}, u32[]{:S(2)}) %collective-permute-start.7) | collective-permute-done | bytes 524320 | tf_op jit(solution)/shard_map/ppermute | solution.py:194
  91.3 2.2 %fusion.5 = bf16[8,2,2,128,128]{4,3,2,1,0:T(8,128)(2,1)} fusion(bf16[8,2,2,128,128]{4,3,2,1,0:T(8,128)(2,1)} %copy.24, bf16[8,2,2,128,128]{4,3,2,0,1:T(8,128)(2,1)S(1)} %fusion.3, bf16[8,2,128,128]{3,2,1,0:T(8,128)(2,1)S(1)} %collective-permute-done.5, bf16[8,2,128,128]{3,2,1,0:T(8,128)(2,1)} %collective-permute-done.6, ...), kind=kLoop, calls=%fused_computation.7 | loop fusion | flops 1572864 | bytes 2621442 | tf_op jit(solution)/shard_map/dynamic_update_slice | solution.py:240
  93.5 19.7 %all-to-all-start.3 = ((bf16[8,2,2,128,128]{4,3,2,1,0:T(8,128)(2,1)}), bf16[8,2,2,128,128]{4,3,2,1,0:T(8,128)(2,1)S(1)}, u32[]{:S(2)}, u32[]{:S(2)}) async-start(bf16[8,2,2,128,128]{4,3,2,1,0:T(8,128)(2,1)} %fusion.5), calls=%async_computation.3 | async-start | bytes 2097152 | tf_op jit(solution)/shard_map/all_to_all | solution.py:19
  113.1 1.6 %shard_map.97 = (bf16[128,2048]{1,0:T(8,128)(2,1)}, bf16[128,2048]{1,0:T(8,128)(2,1)}) custom-call(bf16[8,2,2,128,128]{4,3,2,1,0:T(8,128)(2,1)S(1)} %all-to-all-done.2.i_ref), custom_call_target="tpu_custom_call" | custom-call | tf_op jit(solution)/shard_map/pallas_call | solution.py:75
  114.8 7.8 %all-to-all-done.3.i_ref = bf16[8,2,2,128,128]{4,3,2,1,0:T(8,128)(2,1)S(1)} async-done(((bf16[8,2,2,128,128]{4,3,2,1,0:T(8,128)(2,1)}), bf16[8,2,2,128,128]{4,3,2,1,0:T(8,128)(2,1)S(1)}, u32[]{:S(2)}, u32[]{:S(2)}) %all-to-all-start.3) | async-done | bytes 1048608 | tf_op jit(solution)/shard_map/all_to_all | solution.py:19
  122.6 1.6 %shard_map.98 = (bf16[128,2048]{1,0:T(8,128)(2,1)}, bf16[128,2048]{1,0:T(8,128)(2,1)}) custom-call(bf16[8,2,2,128,128]{4,3,2,1,0:T(8,128)(2,1)S(1)} %all-to-all-done.3.i_ref), custom_call_target="tpu_custom_call" | custom-call | tf_op jit(solution)/shard_map/pallas_call | solution.py:75
  (15 shorter events, 0.4 us)
Async XLA Ops:
  2.7 20.5 %all-to-all-start = ((bf16[8,2,2,128,128]{4,3,2,1,0:T(8,128)(2,1)}), bf16[8,2,2,128,128]{4,3,2,1,0:T(8,128)(2,1)S(1)}, u32[]{:S(2)}, u32[]{:S(2)}) async-start(bf16[8,2,2,128,128]{4,3,2,1,0:T(8,128)(2,1)} %shard_map.93), calls=%async_computation | async-start | bytes 2097152 | tf_op jit(solution)/shard_map/all_to_all | solution.py:19
  24.3 22.7 %all-to-all-start.1 = ((bf16[8,2,2,128,128]{4,3,2,1,0:T(8,128)(2,1)}), bf16[8,2,2,128,128]{4,3,2,1,0:T(8,128)(2,1)S(1)}, u32[]{:S(2)}, u32[]{:S(2)}) async-start(bf16[8,2,2,128,128]{4,3,2,1,0:T(8,128)(2,1)} %shard_map.94), calls=%async_computation.1 | async-start | bytes 2097152 | tf_op jit(solution)/shard_map/all_to_all | solution.py:19
  28.0 8.7 %collective-permute-start = (bf16[8,2,128,128]{3,2,1,0:T(8,128)(2,1)}, bf16[8,2,128,128]{3,2,1,0:T(8,128)(2,1)}, u32[]{:S(2)}, u32[]{:S(2)}) collective-permute-start(bf16[8,2,128,128]{3,2,1,0:T(8,128)(2,1)} %get-tuple-element.25), channel_id=1, source_target_pairs={{0,1},{32,33},{64,65},{96,97},{128,129},{160,161},{192,193},{224,2... | collective-permute-start | bytes 1572872 | tf_op jit(solution)/shard_map/ppermute | solution.py:194
  29.3 16.4 %collective-permute-start.3 = (bf16[8,2,128,128]{3,2,1,0:T(8,128)(2,1)}, bf16[8,2,128,128]{3,2,1,0:T(8,128)(2,1)}, u32[]{:S(2)}, u32[]{:S(2)}) collective-permute-start(bf16[8,2,128,128]{3,2,1,0:T(8,128)(2,1)} %get-tuple-element.25), channel_id=1, source_target_pairs={{7,8},{39,40},{71,72},{103,104},{15,16},{47,48},{79,80},{111,112},... | collective-permute-start | bytes 1572872 | tf_op jit(solution)/shard_map/ppermute | solution.py:194
  36.7 9.0 %collective-permute-start.2 = (bf16[8,2,128,128]{3,2,1,0:T(8,128)(2,1)}, bf16[8,2,128,128]{3,2,1,0:T(8,128)(2,1)}, u32[]{:S(2)}, u32[]{:S(2)}) collective-permute-start(bf16[8,2,128,128]{3,2,1,0:T(8,128)(2,1)} %collective-permute-done), channel_id=1, source_target_pairs={{128,136},{160,168},{192,200},{224,232},{136,144},{168,176},{200,2... | collective-permute-start | bytes 1572872 | tf_op jit(solution)/shard_map/ppermute | solution.py:194
  38.1 0.7 copy-start.1
  40.1 16.1 %collective-permute-start.1 = (bf16[8,2,128,128]{3,2,1,0:T(8,128)(2,1)}, bf16[8,2,128,128]{3,2,1,0:T(8,128)(2,1)S(1)}, u32[]{:S(2)}, u32[]{:S(2)}) collective-permute-start(bf16[8,2,128,128]{3,2,1,0:T(8,128)(2,1)} %get-tuple-element.26), channel_id=1, source_target_pairs={{0,1},{1,2},{2,3},{3,4},{4,5},{5,6},{6,7},{7,8},{8,9},{9,10},{10,1... | collective-permute-start | bytes 1572872 | tf_op jit(solution)/shard_map/ppermute | solution.py:231
  56.2 20.0 %collective-permute-start.4 = (bf16[8,2,128,128]{3,2,1,0:T(8,128)(2,1)}, bf16[8,2,128,128]{3,2,1,0:T(8,128)(2,1)}, u32[]{:S(2)}, u32[]{:S(2)}) collective-permute-start(bf16[8,2,128,128]{3,2,1,0:T(8,128)(2,1)} %get-tuple-element.32), channel_id=1, source_target_pairs={{0,31},{1,0},{2,1},{3,2},{4,3},{5,4},{6,5},{7,6},{8,7},{9,8},{10,9... | collective-permute-start | bytes 1572872 | tf_op jit(solution)/shard_map/ppermute | solution.py:231
  65.4 28.1 %all-to-all-start.2 = ((bf16[8,2,2,128,128]{4,3,2,1,0:T(8,128)(2,1)}), bf16[8,2,2,128,128]{4,3,2,1,0:T(8,128)(2,1)S(1)}, u32[]{:S(2)}, u32[]{:S(2)}) async-start(bf16[8,2,2,128,128]{4,3,2,1,0:T(8,128)(2,1)} %get-tuple-element.35), calls=%async_computation.2 | async-start | bytes 2097152 | tf_op jit(solution)/shard_map/all_to_all | solution.py:19
  76.2 2.8 %collective-permute-start.5 = (bf16[8,2,128,128]{3,2,1,0:T(8,128)(2,1)S(1)}, bf16[8,2,128,128]{3,2,1,0:T(8,128)(2,1)S(1)}, u32[]{:S(2)}, u32[]{:S(2)}) collective-permute-start(bf16[8,2,128,128]{3,2,1,0:T(8,128)(2,1)S(1)} %get-tuple-element.34), channel_id=1, source_target_pairs={{128,135},{160,167},{192,199},{224,231},{1,0},{33,32},{65,64},{97,... | collective-permute-start | bytes 1572872 | tf_op jit(solution)/shard_map/ppermute | solution.py:194
  77.6 13.7 %collective-permute-start.7 = (bf16[8,2,128,128]{3,2,1,0:T(8,128)(2,1)S(1)}, bf16[8,2,128,128]{3,2,1,0:T(8,128)(2,1)}, u32[]{:S(2)}, u32[]{:S(2)}) collective-permute-start(bf16[8,2,128,128]{3,2,1,0:T(8,128)(2,1)S(1)} %get-tuple-element.34), channel_id=1, source_target_pairs={{0,31},{32,63},{64,95},{96,127},{8,7},{40,39},{72,71},{104,103},{1... | collective-permute-start | bytes 1572872 | tf_op jit(solution)/shard_map/ppermute | solution.py:194
  79.0 12.2 %collective-permute-start.6 = (bf16[8,2,128,128]{3,2,1,0:T(8,128)(2,1)S(1)}, bf16[8,2,128,128]{3,2,1,0:T(8,128)(2,1)}, u32[]{:S(2)}, u32[]{:S(2)}) collective-permute-start(bf16[8,2,128,128]{3,2,1,0:T(8,128)(2,1)S(1)} %collective-permute-done.5), channel_id=1, source_target_pairs={{135,159},{167,191},{199,223},{231,255},{143,135},{175,167},{207,1... | collective-permute-start | bytes 1572872 | tf_op jit(solution)/shard_map/ppermute | solution.py:194
  80.5 1.5 %copy-start = (bf16[8,2,2,128,128]{4,3,2,1,0:T(8,128)(2,1)S(1)}, bf16[8,2,2,128,128]{4,3,2,1,0:T(8,128)(2,1)}, u32[]{:S(2)}) copy-start(bf16[8,2,2,128,128]{4,3,2,1,0:T(8,128)(2,1)} %get-tuple-element.30) | copy-start | bytes 3145732
  93.5 29.1 %all-to-all-start.3 = ((bf16[8,2,2,128,128]{4,3,2,1,0:T(8,128)(2,1)}), bf16[8,2,2,128,128]{4,3,2,1,0:T(8,128)(2,1)S(1)}, u32[]{:S(2)}, u32[]{:S(2)}) async-start(bf16[8,2,2,128,128]{4,3,2,1,0:T(8,128)(2,1)} %fusion.5), calls=%async_computation.3 | async-start | bytes 2097152 | tf_op jit(solution)/shard_map/all_to_all | solution.py:19
